TPU v7x, 512 devices: a whole 4x8x8 slice. The times are simulated.
512 devices in a mesh: member: 8 (over y_lo, core), patch: 64 (over x, y_hi, z).
Axes of the slice: x: 4, y: 8 (y_hi: 2, y_lo: 4; y = y_hi * 4 + y_lo), z: 8, core: 2. Of those that a mesh axis runs over, the one named last changes fastest.
Arguments:
- perturbations: float32 [64, 55, 16384], P('member', None, 'patch'), may hold values from -6 to 6
- gradient: float32 [55, 64, 256], P(None, 'patch', 'member'), may hold values from -6 to 6
- kappa: float32 [16384], P('patch'), may hold values from 0.02 to 0.08
- vloc: float32 [55, 55], replicated, may hold values from -0.875 to 0.875
- neighbors: int32 [6, 16384], P(None, 'patch'), may hold values from 0 to 320, as said below
- send_lists: int32 [4, 1024], P(None, 'patch'), may hold values from 0 to 255, as said below
- counts: int32 [64], P('patch'), may hold values from 248 to 256, as said below
Outputs:
- control_gradient: float32 [64, 55, 16384], P('member', None, 'patch')
Inputs may be any that keep to these rules, and one draw needn't show every extreme that they name: `neighbors`: neighbor relations are symmetric; live cells only name live cells; entries at or above 256 name the received cells of the four neighboring patches; cells of slots at or above the patch's count have only empty entries. `send_lists`: each entry is the slot of a live cell of the sending patch. `counts`: some patch is full.
All inputs are finite; a program needn't handle non-finite values.
Results may differ from a plain program's by a relative error of at most 0.000073.
Values sent between devices are 32-bit elements; how exact they have to be, the bound alone decides.
No kernel may reach another device: no remote copies, remote signals or barrier semaphores. Data moves between devices by JAX's collectives and lax.ppermute only.
A program may use at most 64 MiB of HBM per device.

v0:
```python
import jax
import jax.numpy as jnp
from jax import lax
from jax.sharding import PartitionSpec as P

PW = 8
STEPS = 4


def from_behind(block, axis, distance):
    devices = range(lax.axis_size(axis))
    route = [((i - distance) % len(devices), i) for i in devices]
    return lax.ppermute(block, axis, route)


def fetch_rims(flux, send_lists):
    offsets = (1, -1, PW, -PW)
    received = []
    for direction in range(4):
        outgoing = jnp.take(flux, send_lists[direction], axis=2)
        received.append(from_behind(outgoing, "patch", offsets[direction]))
    return jnp.concatenate(received, axis=2)


def local(perturbations, gradient, kappa, vloc, neighbors, send_lists, counts):
    gathered = lax.all_gather(gradient, "member", axis=2, tiled=True)
    cell_total = gathered.shape[2]
    field_gradient = gathered.reshape(gathered.shape[0], cell_total)
    rim_len = send_lists.shape[1]
    null_index = cell_total + 4 * rim_len
    degree = jnp.sum((neighbors < null_index).astype(jnp.float32), axis=0)
    state = perturbations * field_gradient[None, :, :]
    zero_column = jnp.zeros((state.shape[0], state.shape[1], 1), jnp.float32)
    ghost_index = jnp.where(neighbors >= cell_total, neighbors - cell_total, 4 * rim_len)
    ghost_slots = jnp.arange(4 * rim_len, dtype=jnp.int32)
    ghost_map = jnp.zeros((4 * rim_len, cell_total), jnp.float32)
    for column in range(6):
        ghost_map = ghost_map + (ghost_index[column][None, :] == ghost_slots[:, None]).astype(
            jnp.float32
        )
    for step in range(STEPS):
        flux = kappa[None, None, :] * state
        extended = jnp.concatenate([flux, fetch_rims(flux, send_lists), zero_column], axis=2)
        total = jnp.take(extended, neighbors[0], axis=2)
        for column in range(1, 6):
            total = total + jnp.take(extended, neighbors[column], axis=2)
        state = state - degree[None, None, :] * flux + total
    mixed = jnp.einsum("lk,mlc->mkc", vloc, state, precision=lax.Precision.HIGHEST)
    alive_mask = (jnp.arange(cell_total, dtype=jnp.int32) < counts[0]).astype(jnp.float32)
    return mixed * alive_mask[None, None, :]


def solution(mesh):
    return jax.shard_map(
        local,
        mesh=mesh,
        in_specs=(
            P("member", None, "patch"),
            P(None, "patch", "member"),
            P("patch"),
            P(),
            P(None, "patch"),
            P(None, "patch"),
            P("patch"),
        ),
        out_specs=P("member", None, "patch"),
        check_vma=False,
    )
```

profile of v0, /device:TPU:6, one launch (start us, length us, event | category | flops | bytes accessed | tf_op | source)
XLA Modules:
  0.0 230.2 jit_solution(13661819826470258678)
XLA Ops:
  0.0 1.5 copy.12
  1.6 14.3 %all_gather.3 = f32[55,1,256]{0,2,1:T(8,128)S(1)} all-gather(f32[55,1,32]{0,2,1:T(8,128)S(1)} %copy-done.5), channel_id=1, replica_groups=mesh['member'=8,'patch'=64] {'member'}, dimensions={2}, use_global_device_ids=true | all-gather | bytes 63360 | tf_op jit(solution)/shard_map/all_gather | solution.py:26
  17.0 0.7 select_bitcast_fusion.15
  17.8 4.3 %collective-permute-start = (f32[8,55,16]{1,0,2:T(8,128)}, f32[8,55,16]{1,0,2:T(8,128)}, u32[]{:S(2)}, u32[]{:S(2)}) collective-permute-start(f32[8,55,16]{1,0,2:T(8,128)} %select_bitcast_fusion.15), channel_id=1, source_target_pairs={{63,0},{0,1},{1,2},{2,3},{3,4},{4,5},{5,6},{6,7},{7,8},{8,9},{9,10... | collective-permute-start | bytes 84488 | tf_op jit(solution)/shard_map/ppermute | solution.py:13
  22.6 0.7 select_bitcast_fusion.14
  23.4 13.8 %collective-permute-start.1 = (f32[8,55,16]{1,0,2:T(8,128)}, f32[8,55,16]{1,0,2:T(8,128)}, u32[]{:S(2)}, u32[]{:S(2)}) collective-permute-start(f32[8,55,16]{1,0,2:T(8,128)} %select_bitcast_fusion.14), channel_id=1, source_target_pairs={{1,0},{2,1},{3,2},{4,3},{5,4},{6,5},{7,6},{8,7},{9,8},{10,9},{11,1... | collective-permute-start | bytes 84488 | tf_op jit(solution)/shard_map/ppermute | solution.py:13
  37.8 0.7 select_bitcast_fusion.13
  38.5 2.0 collective-permute-start.2
  41.2 8.6 %collective-permute-start.3 = (f32[8,55,16]{1,0,2:T(8,128)S(1)}, f32[8,55,16]{1,0,2:T(8,128)S(1)}, u32[]{:S(2)}, u32[]{:S(2)}) collective-permute-start(f32[8,55,16]{1,0,2:T(8,128)S(1)} %select_bitcast_fusion.12), channel_id=1, source_target_pairs={{8,0},{9,1},{10,2},{11,3},{12,4},{13,5},{14,6},{15,7},{16,8},{17,9... | collective-permute-start | bytes 84488 | tf_op jit(solution)/shard_map/ppermute | solution.py:13
  51.3 0.8 constant_dynamic-update-slice_fusion.4
  52.2 0.8 constant_dynamic-update-slice_fusion.3
  53.0 0.8 constant_dynamic-update-slice_fusion.2
  53.9 2.0 gather_fusion.9
  55.9 2.0 gather_fusion.8
  57.9 2.0 gather_fusion.7
  59.9 2.0 gather_fusion.6
  61.9 2.0 gather_fusion.5
  64.0 2.0 gather_fusion.4
  66.0 6.8 %broadcast_multiply_fusion.2 = (f32[8,55,256]{1,0,2:T(8,128)S(1)}, f32[8,55,256]{1,0,2:T(8,128)S(1)}) fusion(f32[256]{0:T(256)S(1)} %copy-done.3, f32[256,8,55]{2,1,0:T(8,128)} %gather_fusion.9, pred[256]{0:T(512)(128)(4,1)S(1)} %get-tuple-element.41, f32[256,8,55]{2,1,0:T(8,128)} %gather_fusion.8, pred[256]{0:T(512)(128)(4,1)S(1)} %get-tuple-element.42, ...), kind=kLoop, calls=%fused_computation.70 | loop fusion | flops 1914880 | bytes 4114944 | tf_op jit(solution)/shard_map/mul | solution.py:42
  72.9 0.7 gather_fusion.10
  73.6 0.7 gather_fusion.11
  74.3 0.7 gather_fusion.12
  75.0 0.7 gather_fusion.13
  76.1 1.9 collective-permute-start.4
  78.1 10.8 %collective-permute-start.5 = (f32[8,55,16]{1,0,2:T(8,128)S(1)}, f32[8,55,16]{1,0,2:T(8,128)S(1)}, u32[]{:S(2)}, u32[]{:S(2)}) collective-permute-start(f32[8,55,16]{1,0,2:T(8,128)S(1)} %select_bitcast_fusion.10), channel_id=1, source_target_pairs={{1,0},{2,1},{3,2},{4,3},{5,4},{6,5},{7,6},{8,7},{9,8},{10,9},{11,1... | collective-permute-start | bytes 84488 | tf_op jit(solution)/shard_map/ppermute | solution.py:13
  89.1 8.2 %collective-permute-start.6 = (f32[8,55,16]{1,0,2:T(8,128)S(1)}, f32[8,55,16]{1,0,2:T(8,128)S(1)}, u32[]{:S(2)}, u32[]{:S(2)}) collective-permute-start(f32[8,55,16]{1,0,2:T(8,128)S(1)} %select_bitcast_fusion.9), channel_id=1, source_target_pairs={{56,0},{57,1},{58,2},{59,3},{60,4},{61,5},{62,6},{63,7},{0,8},{1,9... | collective-permute-start | bytes 84488 | tf_op jit(solution)/shard_map/ppermute | solution.py:13
  97.3 2.5 %collective-permute-start.7 = (f32[8,55,16]{1,0,2:T(8,128)S(1)}, f32[8,55,16]{1,0,2:T(8,128)S(1)}, u32[]{:S(2)}, u32[]{:S(2)}) collective-permute-start(f32[8,55,16]{1,0,2:T(8,128)S(1)} %select_bitcast_fusion.8), channel_id=1, source_target_pairs={{8,0},{9,1},{10,2},{11,3},{12,4},{13,5},{14,6},{15,7},{16,8},{17,9... | collective-permute-start | bytes 84488 | tf_op jit(solution)/shard_map/ppermute | solution.py:13
  100.1 7.3 %collective-permute-done.7 = f32[8,55,16]{1,0,2:T(8,128)S(1)} collective-permute-done((f32[8,55,16]{1,0,2:T(8,128)S(1)}, f32[8,55,16]{1,0,2:T(8,128)S(1)}, u32[]{:S(2)}, u32[]{:S(2)}) %collective-permute-start.7) | collective-permute-done | bytes 28192 | tf_op jit(solution)/shard_map/ppermute | solution.py:13
  107.4 2.0 gather_fusion.19
  109.5 2.0 gather_fusion.18
  111.5 2.0 gather_fusion.17
  113.5 2.0 gather_fusion.16
  115.5 2.0 gather_fusion.15
  117.5 2.0 gather_fusion.14
  119.6 6.8 %broadcast_multiply_fusion.1 = (f32[8,55,256]{1,0,2:T(8,128)S(1)}, f32[8,55,256]{1,0,2:T(8,128)S(1)}) fusion(f32[256]{0:T(256)S(1)} %copy-done.3, f32[256,8,55]{2,1,0:T(8,128)} %gather_fusion.19, pred[256]{0:T(512)(128)(4,1)S(1)} %copy-done.7, f32[256,8,55]{2,1,0:T(8,128)} %gather_fusion.18, pred[256]{0:T(512)(128)(4,1)S(1)} %copy-done.10, ...), kind=kLoop, calls=%fused_computation.69 | loop fusion | flops 1802240 | bytes 4058624 | tf_op jit(solution)/shard_map/mul | solution.py:42
  126.4 0.7 gather_fusion.20
  127.1 0.7 gather_fusion.21
  127.8 0.7 gather_fusion.22
  129.7 1.9 collective-permute-start.8
  131.7 10.8 %collective-permute-start.9 = (f32[8,55,16]{1,0,2:T(8,128)S(1)}, f32[8,55,16]{1,0,2:T(8,128)S(1)}, u32[]{:S(2)}, u32[]{:S(2)}) collective-permute-start(f32[8,55,16]{1,0,2:T(8,128)S(1)} %select_bitcast_fusion.6), channel_id=1, source_target_pairs={{1,0},{2,1},{3,2},{4,3},{5,4},{6,5},{7,6},{8,7},{9,8},{10,9},{11,1... | collective-permute-start | bytes 84488 | tf_op jit(solution)/shard_map/ppermute | solution.py:13
  142.6 7.0 %collective-permute-start.10 = (f32[8,55,16]{1,0,2:T(8,128)S(1)}, f32[8,55,16]{1,0,2:T(8,128)S(1)}, u32[]{:S(2)}, u32[]{:S(2)}) collective-permute-start(f32[8,55,16]{1,0,2:T(8,128)S(1)} %select_bitcast_fusion.5), channel_id=1, source_target_pairs={{56,0},{57,1},{58,2},{59,3},{60,4},{61,5},{62,6},{63,7},{0,8},{1,9... | collective-permute-start | bytes 84488 | tf_op jit(solution)/shard_map/ppermute | solution.py:13
  149.7 3.8 %collective-permute-start.11 = (f32[8,55,16]{1,0,2:T(8,128)S(1)}, f32[8,55,16]{1,0,2:T(8,128)S(1)}, u32[]{:S(2)}, u32[]{:S(2)}) collective-permute-start(f32[8,55,16]{1,0,2:T(8,128)S(1)} %select_bitcast_fusion.4), channel_id=1, source_target_pairs={{8,0},{9,1},{10,2},{11,3},{12,4},{13,5},{14,6},{15,7},{16,8},{17,9... | collective-permute-start | bytes 84488 | tf_op jit(solution)/shard_map/ppermute | solution.py:13
  154.1 6.4 %collective-permute-done.11 = f32[8,55,16]{1,0,2:T(8,128)S(1)} collective-permute-done((f32[8,55,16]{1,0,2:T(8,128)S(1)}, f32[8,55,16]{1,0,2:T(8,128)S(1)}, u32[]{:S(2)}, u32[]{:S(2)}) %collective-permute-start.11) | collective-permute-done | bytes 28192 | tf_op jit(solution)/shard_map/ppermute | solution.py:13
  160.5 2.0 gather_fusion.29
  162.6 2.0 gather_fusion.28
  164.6 2.0 gather_fusion.27
  166.6 2.0 gather_fusion.26
  168.6 2.0 gather_fusion.25
  170.6 2.0 gather_fusion.24
  172.7 6.8 %broadcast_multiply_fusion = (f32[8,55,256]{1,0,2:T(8,128)S(1)}, f32[8,55,256]{1,0,2:T(8,128)S(1)}) fusion(f32[256]{0:T(256)S(1)} %copy-done.3, f32[256,8,55]{2,1,0:T(8,128)} %gather_fusion.29, pred[256]{0:T(512)(128)(4,1)S(1)} %copy-done.7, f32[256,8,55]{2,1,0:T(8,128)} %gather_fusion.28, pred[256]{0:T(512)(128)(4,1)S(1)} %copy-done.11, ...), kind=kLoop, calls=%fused_computation.68 | loop fusion | flops 1802240 | bytes 4058624 | tf_op jit(solution)/shard_map/mul | solution.py:42
  182.7 1.9 collective-permute-start.12
  184.8 10.8 %collective-permute-start.13 = (f32[8,55,16]{1,0,2:T(8,128)S(1)}, f32[8,55,16]{1,0,2:T(8,128)S(1)}, u32[]{:S(2)}, u32[]{:S(2)}) collective-permute-start(f32[8,55,16]{1,0,2:T(8,128)S(1)} %select_bitcast_fusion.2), channel_id=1, source_target_pairs={{1,0},{2,1},{3,2},{4,3},{5,4},{6,5},{7,6},{8,7},{9,8},{10,9},{11,1... | collective-permute-start | bytes 84488 | tf_op jit(solution)/shard_map/ppermute | solution.py:13
  195.7 4.2 %collective-permute-start.14 = (f32[8,55,16]{1,0,2:T(8,128)S(1)}, f32[8,55,16]{1,0,2:T(8,128)S(1)}, u32[]{:S(2)}, u32[]{:S(2)}) collective-permute-start(f32[8,55,16]{1,0,2:T(8,128)S(1)} %select_bitcast_fusion.1), channel_id=1, source_target_pairs={{56,0},{57,1},{58,2},{59,3},{60,4},{61,5},{62,6},{63,7},{0,8},{1,9... | collective-permute-start | bytes 84488 | tf_op jit(solution)/shard_map/ppermute | solution.py:13
  200.0 6.5 %collective-permute-start.15 = (f32[8,55,16]{1,0,2:T(8,128)S(1)}, f32[8,55,16]{1,0,2:T(8,128)S(1)}, u32[]{:S(2)}, u32[]{:S(2)}) collective-permute-start(f32[8,55,16]{1,0,2:T(8,128)S(1)} %select_bitcast_fusion), channel_id=1, source_target_pairs={{8,0},{9,1},{10,2},{11,3},{12,4},{13,5},{14,6},{15,7},{16,8},{17,9... | collective-permute-start | bytes 84488 | tf_op jit(solution)/shard_map/ppermute | solution.py:13
  206.9 3.1 %collective-permute-done.15 = f32[8,55,16]{1,0,2:T(8,128)S(1)} collective-permute-done((f32[8,55,16]{1,0,2:T(8,128)S(1)}, f32[8,55,16]{1,0,2:T(8,128)S(1)}, u32[]{:S(2)}, u32[]{:S(2)}) %collective-permute-start.15) | collective-permute-done | bytes 28192 | tf_op jit(solution)/shard_map/ppermute | solution.py:13
  210.1 1.0 gather_fusion.39
  211.1 2.0 gather_fusion.38
  213.1 2.0 gather_fusion.37
  215.2 2.0 gather_fusion.36
  217.2 2.0 gather_fusion.35
  219.2 2.0 gather_fusion.34
  221.3 6.7 %fusion.1 = f32[8,55,256]{1,0,2:T(8,128)S(1)} fusion(f32[256,8,55]{2,1,0:T(8,128)S(1)} %gather_fusion.39, f32[256,8,55]{2,1,0:T(8,128)} %gather_fusion.38, f32[256,8,55]{2,1,0:T(8,128)} %gather_fusion.37, f32[256,8,55]{2,1,0:T(8,128)} %gather_fusion.36, f32[256,8,55]{2,1,0:T(8,128)} %gather_fusion.35, f32[256,8,55]{2,1,0:T(8,128)} %gather_fusion.34, ...), kind=kLoop, calls=%fused_computation.43 | loop fusion | flops 1689600 | bytes 3608064 | tf_op jit(solution)/shard_map/add | solution.py:47
  228.0 1.4 fusion
  229.3 0.9 copy.15
  (146 shorter events, 10.5 us)
Async XLA Ops:
  0.0 227.9 %copy-start = (f32[55,55]{1,0:T(8,128)S(1)}, f32[55,55]{1,0:T(8,128)}, u32[]{:S(2)}) copy-start(f32[55,55]{1,0:T(8,128)} %param.14) | copy-start | bytes 36304
  0.0 1.5 copy-start.5
  0.0 15.8 %copy-start.33 = (s32[4,16]{1,0:T(4,128)S(1)}, s32[4,16]{1,0:T(4,128)}, u32[]{:S(2)}) copy-start(s32[4,16]{1,0:T(4,128)} %param.16) | copy-start | bytes 772
  0.0 15.8 %copy-start.3 = (f32[256]{0:T(256)S(1)}, f32[256]{0:T(256)}, u32[]{:S(2)}) copy-start(f32[256]{0:T(256)} %param.13) | copy-start | bytes 3076
  15.8 0.7 copy-start.1
  15.8 0.6 copy-start.29
  16.5 33.4 %copy-start.4 = (s32[6,256]{1,0:T(8,128)S(1)}, s32[6,256]{1,0:T(8,128)}, u32[]{:S(2)}) copy-start(s32[6,256]{1,0:T(8,128)} %param.15) | copy-start | bytes 18436
  17.8 33.6 %collective-permute-start = (f32[8,55,16]{1,0,2:T(8,128)}, f32[8,55,16]{1,0,2:T(8,128)}, u32[]{:S(2)}, u32[]{:S(2)}) collective-permute-start(f32[8,55,16]{1,0,2:T(8,128)} %select_bitcast_fusion.15), channel_id=1, source_target_pairs={{63,0},{0,1},{1,2},{2,3},{3,4},{4,5},{5,6},{6,7},{7,8},{8,9},{9,10... | collective-permute-start | bytes 84488 | tf_op jit(solution)/shard_map/ppermute | solution.py:13
  22.1 19.2 %copy-start.30 = (s32[1024]{0:T(1024)}, s32[1024]{0:T(1024)S(1)}, u32[]{:S(2)}) copy-start(s32[1024]{0:T(1024)S(1)} %pad_clamp_fusion.8) | copy-start | bytes 12292
  23.4 28.8 %collective-permute-start.1 = (f32[8,55,16]{1,0,2:T(8,128)}, f32[8,55,16]{1,0,2:T(8,128)}, u32[]{:S(2)}, u32[]{:S(2)}) collective-permute-start(f32[8,55,16]{1,0,2:T(8,128)} %select_bitcast_fusion.14), channel_id=1, source_target_pairs={{1,0},{2,1},{3,2},{4,3},{5,4},{6,5},{7,6},{8,7},{9,8},{10,9},{11,1... | collective-permute-start | bytes 84488 | tf_op jit(solution)/shard_map/ppermute | solution.py:13
  37.2 4.0 %copy-start.31 = (s32[1024]{0:T(1024)}, s32[1024]{0:T(1024)S(1)}, u32[]{:S(2)}) copy-start(s32[1024]{0:T(1024)S(1)} %pad_clamp_fusion.7) | copy-start | bytes 12292
  38.5 14.5 %collective-permute-start.2 = (f32[8,55,16]{1,0,2:T(8,128)}, f32[8,55,16]{1,0,2:T(8,128)}, u32[]{:S(2)}, u32[]{:S(2)}) collective-permute-start(f32[8,55,16]{1,0,2:T(8,128)} %select_bitcast_fusion.13), channel_id=1, source_target_pairs={{56,0},{57,1},{58,2},{59,3},{60,4},{61,5},{62,6},{63,7},{0,8},{1,9... | collective-permute-start | bytes 84488 | tf_op jit(solution)/shard_map/ppermute | solution.py:13
  40.5 0.7 copy-start.32
  41.2 12.6 %collective-permute-start.3 = (f32[8,55,16]{1,0,2:T(8,128)S(1)}, f32[8,55,16]{1,0,2:T(8,128)S(1)}, u32[]{:S(2)}, u32[]{:S(2)}) collective-permute-start(f32[8,55,16]{1,0,2:T(8,128)S(1)} %select_bitcast_fusion.12), channel_id=1, source_target_pairs={{8,0},{9,1},{10,2},{11,3},{12,4},{13,5},{14,6},{15,7},{16,8},{17,9... | collective-permute-start | bytes 84488 | tf_op jit(solution)/shard_map/ppermute | solution.py:13
  49.9 16.1 %copy-start.6 = (pred[256]{0:T(512)(128)(4,1)}, pred[256]{0:T(512)(128)(4,1)S(1)}, u32[]{:S(2)}) copy-start(pred[256]{0:T(512)(128)(4,1)S(1)} %get-tuple-element.41) | copy-start | bytes 772
  49.9 16.1 %copy-start.9 = (pred[256]{0:T(512)(128)(4,1)}, pred[256]{0:T(512)(128)(4,1)S(1)}, u32[]{:S(2)}) copy-start(pred[256]{0:T(512)(128)(4,1)S(1)} %get-tuple-element.42) | copy-start | bytes 772
  50.0 16.0 %copy-start.13 = (pred[256]{0:T(512)(128)(4,1)}, pred[256]{0:T(512)(128)(4,1)S(1)}, u32[]{:S(2)}) copy-start(pred[256]{0:T(512)(128)(4,1)S(1)} %get-tuple-element.43) | copy-start | bytes 772
  50.0 16.0 %copy-start.17 = (pred[256]{0:T(512)(128)(4,1)}, pred[256]{0:T(512)(128)(4,1)S(1)}, u32[]{:S(2)}) copy-start(pred[256]{0:T(512)(128)(4,1)S(1)} %get-tuple-element.44) | copy-start | bytes 772
  50.0 16.0 %copy-start.21 = (pred[256]{0:T(512)(128)(4,1)}, pred[256]{0:T(512)(128)(4,1)S(1)}, u32[]{:S(2)}) copy-start(pred[256]{0:T(512)(128)(4,1)S(1)} %get-tuple-element.45) | copy-start | bytes 772
  50.0 16.0 %copy-start.25 = (pred[256]{0:T(512)(128)(4,1)}, pred[256]{0:T(512)(128)(4,1)S(1)}, u32[]{:S(2)}) copy-start(pred[256]{0:T(512)(128)(4,1)S(1)} %get-tuple-element.46) | copy-start | bytes 772
  59.9 6.1 %copy-start.2 = (f32[55,1,256]{0,2,1:T(8,128)S(1)}, f32[55,1,256]{0,2,1:T(8,128)}, u32[]{:S(2)}) copy-start(f32[55,1,256]{0,2,1:T(8,128)} %copy-done.1) | copy-start | bytes 168964
  76.1 23.7 %collective-permute-start.4 = (f32[8,55,16]{1,0,2:T(8,128)S(1)}, f32[8,55,16]{1,0,2:T(8,128)S(1)}, u32[]{:S(2)}, u32[]{:S(2)}) collective-permute-start(f32[8,55,16]{1,0,2:T(8,128)S(1)} %select_bitcast_fusion.11), channel_id=1, source_target_pairs={{63,0},{0,1},{1,2},{2,3},{3,4},{4,5},{5,6},{6,7},{7,8},{8,9},{9,10... | collective-permute-start | bytes 84488 | tf_op jit(solution)/shard_map/ppermute | solution.py:13
  78.1 21.7 %collective-permute-start.5 = (f32[8,55,16]{1,0,2:T(8,128)S(1)}, f32[8,55,16]{1,0,2:T(8,128)S(1)}, u32[]{:S(2)}, u32[]{:S(2)}) collective-permute-start(f32[8,55,16]{1,0,2:T(8,128)S(1)} %select_bitcast_fusion.10), channel_id=1, source_target_pairs={{1,0},{2,1},{3,2},{4,3},{5,4},{6,5},{7,6},{8,7},{9,8},{10,9},{11,1... | collective-permute-start | bytes 84488 | tf_op jit(solution)/shard_map/ppermute | solution.py:13
  89.1 11.1 %collective-permute-start.6 = (f32[8,55,16]{1,0,2:T(8,128)S(1)}, f32[8,55,16]{1,0,2:T(8,128)S(1)}, u32[]{:S(2)}, u32[]{:S(2)}) collective-permute-start(f32[8,55,16]{1,0,2:T(8,128)S(1)} %select_bitcast_fusion.9), channel_id=1, source_target_pairs={{56,0},{57,1},{58,2},{59,3},{60,4},{61,5},{62,6},{63,7},{0,8},{1,9... | collective-permute-start | bytes 84488 | tf_op jit(solution)/shard_map/ppermute | solution.py:13
  97.3 10.1 %collective-permute-start.7 = (f32[8,55,16]{1,0,2:T(8,128)S(1)}, f32[8,55,16]{1,0,2:T(8,128)S(1)}, u32[]{:S(2)}, u32[]{:S(2)}) collective-permute-start(f32[8,55,16]{1,0,2:T(8,128)S(1)} %select_bitcast_fusion.8), channel_id=1, source_target_pairs={{8,0},{9,1},{10,2},{11,3},{12,4},{13,5},{14,6},{15,7},{16,8},{17,9... | collective-permute-start | bytes 84488 | tf_op jit(solution)/shard_map/ppermute | solution.py:13
  113.5 6.1 %copy-start.7 = (pred[256]{0:T(512)(128)(4,1)S(1)}, pred[256]{0:T(512)(128)(4,1)}, u32[]{:S(2)}) copy-start(pred[256]{0:T(512)(128)(4,1)} %copy-done.6) | copy-start | bytes 772
  113.5 6.1 %copy-start.10 = (pred[256]{0:T(512)(128)(4,1)S(1)}, pred[256]{0:T(512)(128)(4,1)}, u32[]{:S(2)}) copy-start(pred[256]{0:T(512)(128)(4,1)} %copy-done.9) | copy-start | bytes 772
  113.5 6.1 %copy-start.14 = (pred[256]{0:T(512)(128)(4,1)S(1)}, pred[256]{0:T(512)(128)(4,1)}, u32[]{:S(2)}) copy-start(pred[256]{0:T(512)(128)(4,1)} %copy-done.13) | copy-start | bytes 772
  113.5 6.1 %copy-start.18 = (pred[256]{0:T(512)(128)(4,1)S(1)}, pred[256]{0:T(512)(128)(4,1)}, u32[]{:S(2)}) copy-start(pred[256]{0:T(512)(128)(4,1)} %copy-done.17) | copy-start | bytes 772
  113.5 6.1 %copy-start.22 = (pred[256]{0:T(512)(128)(4,1)S(1)}, pred[256]{0:T(512)(128)(4,1)}, u32[]{:S(2)}) copy-start(pred[256]{0:T(512)(128)(4,1)} %copy-done.21) | copy-start | bytes 772
  113.5 6.1 %copy-start.26 = (pred[256]{0:T(512)(128)(4,1)S(1)}, pred[256]{0:T(512)(128)(4,1)}, u32[]{:S(2)}) copy-start(pred[256]{0:T(512)(128)(4,1)} %copy-done.25) | copy-start | bytes 772
  129.7 23.9 %collective-permute-start.8 = (f32[8,55,16]{1,0,2:T(8,128)S(1)}, f32[8,55,16]{1,0,2:T(8,128)S(1)}, u32[]{:S(2)}, u32[]{:S(2)}) collective-permute-start(f32[8,55,16]{1,0,2:T(8,128)S(1)} %select_bitcast_fusion.7), channel_id=1, source_target_pairs={{63,0},{0,1},{1,2},{2,3},{3,4},{4,5},{5,6},{6,7},{7,8},{8,9},{9,10... | collective-permute-start | bytes 84488 | tf_op jit(solution)/shard_map/ppermute | solution.py:13
  131.7 21.9 %collective-permute-start.9 = (f32[8,55,16]{1,0,2:T(8,128)S(1)}, f32[8,55,16]{1,0,2:T(8,128)S(1)}, u32[]{:S(2)}, u32[]{:S(2)}) collective-permute-start(f32[8,55,16]{1,0,2:T(8,128)S(1)} %select_bitcast_fusion.6), channel_id=1, source_target_pairs={{1,0},{2,1},{3,2},{4,3},{5,4},{6,5},{7,6},{8,7},{9,8},{10,9},{11,1... | collective-permute-start | bytes 84488 | tf_op jit(solution)/shard_map/ppermute | solution.py:13
  142.6 11.5 %collective-permute-start.10 = (f32[8,55,16]{1,0,2:T(8,128)S(1)}, f32[8,55,16]{1,0,2:T(8,128)S(1)}, u32[]{:S(2)}, u32[]{:S(2)}) collective-permute-start(f32[8,55,16]{1,0,2:T(8,128)S(1)} %select_bitcast_fusion.5), channel_id=1, source_target_pairs={{56,0},{57,1},{58,2},{59,3},{60,4},{61,5},{62,6},{63,7},{0,8},{1,9... | collective-permute-start | bytes 84488 | tf_op jit(solution)/shard_map/ppermute | solution.py:13
  149.7 10.8 %collective-permute-start.11 = (f32[8,55,16]{1,0,2:T(8,128)S(1)}, f32[8,55,16]{1,0,2:T(8,128)S(1)}, u32[]{:S(2)}, u32[]{:S(2)}) collective-permute-start(f32[8,55,16]{1,0,2:T(8,128)S(1)} %select_bitcast_fusion.4), channel_id=1, source_target_pairs={{8,0},{9,1},{10,2},{11,3},{12,4},{13,5},{14,6},{15,7},{16,8},{17,9... | collective-permute-start | bytes 84488 | tf_op jit(solution)/shard_map/ppermute | solution.py:13
  166.6 6.1 %copy-start.11 = (pred[256]{0:T(512)(128)(4,1)S(1)}, pred[256]{0:T(512)(128)(4,1)}, u32[]{:S(2)}) copy-start(pred[256]{0:T(512)(128)(4,1)} %copy-done.9) | copy-start | bytes 772
  166.6 6.1 %copy-start.15 = (pred[256]{0:T(512)(128)(4,1)S(1)}, pred[256]{0:T(512)(128)(4,1)}, u32[]{:S(2)}) copy-start(pred[256]{0:T(512)(128)(4,1)} %copy-done.13) | copy-start | bytes 772
  166.6 6.1 %copy-start.19 = (pred[256]{0:T(512)(128)(4,1)S(1)}, pred[256]{0:T(512)(128)(4,1)}, u32[]{:S(2)}) copy-start(pred[256]{0:T(512)(128)(4,1)} %copy-done.17) | copy-start | bytes 772
  166.6 6.1 %copy-start.23 = (pred[256]{0:T(512)(128)(4,1)S(1)}, pred[256]{0:T(512)(128)(4,1)}, u32[]{:S(2)}) copy-start(pred[256]{0:T(512)(128)(4,1)} %copy-done.21) | copy-start | bytes 772
  166.6 6.1 %copy-start.27 = (pred[256]{0:T(512)(128)(4,1)S(1)}, pred[256]{0:T(512)(128)(4,1)}, u32[]{:S(2)}) copy-start(pred[256]{0:T(512)(128)(4,1)} %copy-done.25) | copy-start | bytes 772
  182.7 23.7 %collective-permute-start.12 = (f32[8,55,16]{1,0,2:T(8,128)S(1)}, f32[8,55,16]{1,0,2:T(8,128)S(1)}, u32[]{:S(2)}, u32[]{:S(2)}) collective-permute-start(f32[8,55,16]{1,0,2:T(8,128)S(1)} %select_bitcast_fusion.3), channel_id=1, source_target_pairs={{63,0},{0,1},{1,2},{2,3},{3,4},{4,5},{5,6},{6,7},{7,8},{8,9},{9,10... | collective-permute-start | bytes 84488 | tf_op jit(solution)/shard_map/ppermute | solution.py:13
  184.8 21.7 %collective-permute-start.13 = (f32[8,55,16]{1,0,2:T(8,128)S(1)}, f32[8,55,16]{1,0,2:T(8,128)S(1)}, u32[]{:S(2)}, u32[]{:S(2)}) collective-permute-start(f32[8,55,16]{1,0,2:T(8,128)S(1)} %select_bitcast_fusion.2), channel_id=1, source_target_pairs={{1,0},{2,1},{3,2},{4,3},{5,4},{6,5},{7,6},{8,7},{9,8},{10,9},{11,1... | collective-permute-start | bytes 84488 | tf_op jit(solution)/shard_map/ppermute | solution.py:13
  195.7 11.2 %collective-permute-start.14 = (f32[8,55,16]{1,0,2:T(8,128)S(1)}, f32[8,55,16]{1,0,2:T(8,128)S(1)}, u32[]{:S(2)}, u32[]{:S(2)}) collective-permute-start(f32[8,55,16]{1,0,2:T(8,128)S(1)} %select_bitcast_fusion.1), channel_id=1, source_target_pairs={{56,0},{57,1},{58,2},{59,3},{60,4},{61,5},{62,6},{63,7},{0,8},{1,9... | collective-permute-start | bytes 84488 | tf_op jit(solution)/shard_map/ppermute | solution.py:13
  200.0 10.1 %collective-permute-start.15 = (f32[8,55,16]{1,0,2:T(8,128)S(1)}, f32[8,55,16]{1,0,2:T(8,128)S(1)}, u32[]{:S(2)}, u32[]{:S(2)}) collective-permute-start(f32[8,55,16]{1,0,2:T(8,128)S(1)} %select_bitcast_fusion), channel_id=1, source_target_pairs={{8,0},{9,1},{10,2},{11,3},{12,4},{13,5},{14,6},{15,7},{16,8},{17,9... | collective-permute-start | bytes 84488 | tf_op jit(solution)/shard_map/ppermute | solution.py:13
  215.1 6.1 %copy-start.8 = (pred[256]{0:T(512)(128)(4,1)S(1)}, pred[256]{0:T(512)(128)(4,1)}, u32[]{:S(2)}) copy-start(pred[256]{0:T(512)(128)(4,1)} %copy-done.6) | copy-start | bytes 772
  215.1 6.1 %copy-start.12 = (pred[256]{0:T(512)(128)(4,1)S(1)}, pred[256]{0:T(512)(128)(4,1)}, u32[]{:S(2)}) copy-start(pred[256]{0:T(512)(128)(4,1)} %copy-done.9) | copy-start | bytes 772
  215.1 6.1 %copy-start.16 = (pred[256]{0:T(512)(128)(4,1)S(1)}, pred[256]{0:T(512)(128)(4,1)}, u32[]{:S(2)}) copy-start(pred[256]{0:T(512)(128)(4,1)} %copy-done.13) | copy-start | bytes 772
  215.1 6.1 %copy-start.20 = (pred[256]{0:T(512)(128)(4,1)S(1)}, pred[256]{0:T(512)(128)(4,1)}, u32[]{:S(2)}) copy-start(pred[256]{0:T(512)(128)(4,1)} %copy-done.17) | copy-start | bytes 772
  215.1 6.1 %copy-start.24 = (pred[256]{0:T(512)(128)(4,1)S(1)}, pred[256]{0:T(512)(128)(4,1)}, u32[]{:S(2)}) copy-start(pred[256]{0:T(512)(128)(4,1)} %copy-done.21) | copy-start | bytes 772
  215.2 6.1 %copy-start.28 = (pred[256]{0:T(512)(128)(4,1)S(1)}, pred[256]{0:T(512)(128)(4,1)}, u32[]{:S(2)}) copy-start(pred[256]{0:T(512)(128)(4,1)} %copy-done.25) | copy-start | bytes 772
  221.3 6.7 %copy-start.34 = (f32[256]{0:T(256)S(1)}, f32[256]{0:T(256)}, u32[]{:S(2)}) copy-start(f32[256]{0:T(256)} %compare_convert_fusion) | copy-start | bytes 3076
where the time goes:
time: 232 us; the launch traced here: 230 us
  starting transfers between devices  99.1 us (43%)
  local copies, waits for them, and re-layouts  63.4 us (27%)
  other arithmetic  32.4 us (14%)
  waiting for transfers between devices  18 us (8%)
  blocking collectives  14.3 us (6%)
    ppermute x16, starting transfers between devices, from_behind(): return lax.ppermute(block, axis, route)  99.1 us
    gather x20, local copies, waits for them, and re-layouts, local(): total = total + jnp.take(extended, neighbors[column], axis=2)  39.3 us
    mul x4, other arithmetic, local(): flux = kappa[None, None, :] * state  20.9 us
    ppermute x16, waiting for transfers between devices, from_behind(): return lax.ppermute(block, axis, route)  18 us
    all_gather x1, blocking collectives, local(): gathered = lax.all_gather(gradient, 'member', axis=2, tiled=True)  14.3 us
    gather x16, local copies, waits for them, and re-layouts, fetch_rims(): outgoing = jnp.take(flux, send_lists[direction], axis=2)  10.5 us
    gather x4, local copies, waits for them, and re-layouts, local(): total = jnp.take(extended, neighbors[0], axis=2)  8.11 us
    add x1, other arithmetic, local(): state = state - degree[None, None, :] * flux + total  6.67 us
  transfers between devices with their start and end apart: 16, of which 6 were waited for; matrix products, arithmetic and copies ran while one was open for 3% of the time, Pallas kernels for 0%

commit v1 on v0

v1 whole, which is shorter than its diff:
```python
import itertools

import jax
import jax.numpy as jnp
from jax import lax
from jax.experimental import pallas as pl
from jax.experimental.pallas import tpu as pltpu
from jax.sharding import Mesh
from jax.sharding import PartitionSpec as P

STEPS = 4
AXES = ("member", "x", "yh", "z")
LEV = 55
ROWS = 56
MEM = 8
FIELDS = MEM * ROWS
CELLS = 256
RIM = 16
GHOSTS = 4 * RIM
NULL = CELLS + GHOSTS
SLOT = 24
F32 = jnp.float32
BF16 = jnp.bfloat16


def flat(x, yh, l, z, core):
    return (l * 2 + core) * 64 + (x % 4) * 16 + yh * 8 + z % 8


def pairs(move):
    every = itertools.product(range(4), range(2), range(4), range(8), range(2))
    return sorted((flat(*c), flat(*move(*c))) for c in every)


def next_column(x, yh, l, z, core):
    if z < 7:
        return x, yh, l, z + 1, core
    return x + core, yh, l, 0, 1 - core


SWAP = pairs(lambda x, yh, l, z, core: (x, core, l, z, yh))
EAST = pairs(next_column)
WEST = sorted((b, a) for a, b in EAST)
SOUTH = pairs(lambda x, yh, l, z, core: (x + core, yh, l, z, 1 - core))
NORTH = sorted((b, a) for a, b in SOUTH)
ROUTES = (EAST, WEST, SOUTH, NORTH)
ORDER = (0, 2, 1, 3)


def thirds(value):
    high = value.astype(BF16)
    rest = value - high.astype(F32)
    middle = rest.astype(BF16)
    low = (rest - middle.astype(F32)).astype(BF16)
    return high, middle, low


def exact_dot(left, right, dims):
    split_left = left.dtype == F32
    total = None
    for part in reversed(thirds(left if split_left else right)):
        a, b = (part, right) if split_left else (left, part)
        term = lax.dot_general(a, b, (dims, ((), ())), preferred_element_type=F32)
        total = term if total is None else total + term
    return total


def pack_kernel(member, grad, table, out):
    piece = jnp.concatenate([grad[...], jnp.zeros((4 * RIM - LEV, 32), F32)], axis=0)
    out[0, 0:RIM, :] = jnp.concatenate(
        [piece[g * RIM : (g + 1) * RIM] for g in range(4)], axis=1
    )
    row = table[pl.ds(member[0], 1), :]
    out[0, RIM:, :] = jnp.concatenate(
        [row[:, :128], row[:, 128:], jnp.zeros((SLOT - RIM - 2, 128), F32)], axis=0
    )
    for s in range(1, 16):
        out[s] = out[0]


def rims_out(rims, outs):
    for d in range(4):
        outs[d][...] = rims[d * RIM : (d + 1) * RIM]


def first_kernel(core, slots, pert, r0, r1, r2, r3, x_out, adj_out, sel_out, rows_out):
    base = core[0] * MEM
    lane = lax.broadcasted_iota(jnp.int32, (RIM, 128), 1)
    halves = [[], []]
    for g in range(4):
        for half in range(2):
            total = jnp.zeros((RIM, 128), F32)
            for i in range(4):
                piece = slots[base + half * 4 + i, 0:RIM, :]
                shift = (32 * (i - g)) % 128
                moved = pltpu.roll(piece, shift, 1) if shift else piece
                total = jnp.where(lane // 32 == i, moved, total)
            halves[half].append(total)
    grad = jnp.concatenate(
        [jnp.concatenate(halves[0], axis=0), jnp.concatenate(halves[1], axis=0)], axis=1
    )

    def table_row(j):
        two = slots[base + j, RIM : RIM + 8, :]
        return jnp.concatenate([two[0:1], two[1:2]], axis=1)

    kappa = table_row(6)
    misc = table_row(7)
    ids = lax.broadcasted_iota(jnp.int32, (NULL, CELLS), 0)
    adj = jnp.zeros((NULL, CELLS), F32)
    degree = jnp.zeros((1, CELLS), F32)
    for j in range(6):
        named = table_row(j).astype(jnp.int32)
        adj = adj + (ids == named).astype(F32)
        degree = degree + (named < NULL).astype(F32)
    adj_out[...] = adj.astype(BF16)
    sends = jnp.broadcast_to(misc[:, :128], (128, 128)).T
    sends = jnp.concatenate([sends[0:GHOSTS], sends[0:GHOSTS]], axis=1).astype(jnp.int32)
    sel = (sends == lax.broadcasted_iota(jnp.int32, (GHOSTS, CELLS), 1)).astype(F32)
    sel = sel.astype(BF16)
    sel_out[...] = sel
    count = jnp.max(
        jnp.where(lax.broadcasted_iota(jnp.int32, (1, 128), 1) == GHOSTS, misc[:, :128], 0.0),
        axis=1,
        keepdims=True,
    ).astype(jnp.int32)
    alive = (lax.broadcasted_iota(jnp.int32, (1, CELLS), 1) < count).astype(F32)
    rows_out[...] = jnp.concatenate(
        [kappa, 1.0 - degree * kappa, alive, jnp.zeros((5, CELLS), F32)], axis=0
    )
    for m in range(MEM):
        x_out[m * ROWS : m * ROWS + LEV, :] = pert[m] * grad[0:LEV]
        x_out[m * ROWS + LEV : (m + 1) * ROWS, :] = jnp.zeros((1, CELLS), F32)
    rims = exact_dot(sel, kappa * x_out[...], ((1,), (1,)))
    rims_out(rims, (r0, r1, r2, r3))


def stay(x, adj, sel, rows, y_out, b_out):
    kappa = rows[0:1, :]
    y = x * rows[1:2, :] + exact_dot(kappa * x, adj[0:CELLS, :], ((1,), (0,)))
    y_out[...] = y
    if b_out is not None:
        b_out[...] = exact_dot(sel[...], kappa * y, ((1,), (1,)))


def first_stay_kernel(x, adj, sel, rows, y_out, b_out, gsel_out, ksel_out):
    stay(x[...], adj, sel, rows, y_out, b_out)
    gsel_out[...] = lax.dot_general(
        sel[...], adj[CELLS:, :], (((1,), (1,)), ((), ())), preferred_element_type=F32
    ).astype(BF16)
    ksel_out[...] = exact_dot(
        sel[...], jnp.broadcast_to(rows[0:1, :], (128, CELLS)), ((1,), (1,))
    )


def rim_kernel(b, gsel, ksel, i0, i1, i2, i3, r0, r1, r2, r3):
    came = jnp.concatenate([i0[...], i1[...], i2[...], i3[...]], axis=0)
    rims = b[...] + ksel[:, 0:1] * exact_dot(gsel[...], came, ((1,), (0,)))
    rims_out(rims, (r0, r1, r2, r3))


def arrive(y, adj, i0, i1, i2, i3):
    came = jnp.concatenate([i0[...], i1[...], i2[...], i3[...]], axis=0)
    return y[...] + exact_dot(came.T, adj[CELLS:, :], ((1,), (0,)))


def stay_kernel(y, adj, sel, rows, i0, i1, i2, i3, y_out, b_out=None):
    stay(arrive(y, adj, i0, i1, i2, i3), adj, sel, rows, y_out, b_out)


def last_kernel(y, adj, rows, vloc, i0, i1, i2, i3, out):
    x = arrive(y, adj, i0, i1, i2, i3)
    mix = vloc[...].T
    for m in range(MEM):
        part = x[m * ROWS : m * ROWS + LEV] * rows[2:3, :]
        out[m] = jnp.dot(
            mix, part, precision=lax.Precision.HIGHEST, preferred_element_type=F32
        )


VM = pl.BlockSpec(memory_space=pltpu.VMEM)
SM = pl.BlockSpec(memory_space=pltpu.SMEM)


def call(kernel, shapes, args, scalars=0, flops=10**8):
    specs = [SM] * scalars + [VM] * (len(args) - scalars)
    return pl.pallas_call(
        kernel,
        out_shape=[jax.ShapeDtypeStruct(s, t) for s, t in shapes],
        in_specs=specs,
        out_specs=[VM] * len(shapes),
        cost_estimate=pl.CostEstimate(flops=flops, bytes_accessed=10**6, transcendentals=0),
        compiler_params=pltpu.CompilerParams(vmem_limit_bytes=32 * 1024 * 1024),
    )(*args)


def exchange(rims):
    came = {d: lax.ppermute(rims[d], AXES, ROUTES[d]) for d in ORDER}
    return [came[d] for d in range(4)]


def local(perturbations, gradient, kappa, vloc, neighbors, send_lists, counts):
    pert = lax.ppermute(perturbations, AXES, SWAP)
    member = lax.axis_index("member")
    misc = jnp.concatenate(
        [
            send_lists.reshape(GHOSTS),
            counts.reshape(1),
            jnp.zeros((CELLS - GHOSTS - 1,), jnp.int32),
        ]
    )
    table = jnp.concatenate(
        [neighbors.astype(F32), kappa.reshape(1, CELLS), misc.reshape(1, CELLS).astype(F32)]
    )
    (slots,) = call(
        pack_kernel,
        [((16, SLOT, 128), F32)],
        (member.reshape(1), gradient.reshape(LEV, 32), table),
        scalars=1,
    )
    slots = lax.all_to_all(slots, ("yh", "member"), 0, 0)
    rim_shapes = [((RIM, FIELDS), F32)] * 4
    state = ((FIELDS, CELLS), F32)
    border = ((GHOSTS, FIELDS), F32)
    *rims, x, adj, sel, rows = call(
        first_kernel,
        rim_shapes
        + [state, ((NULL, CELLS), BF16), ((GHOSTS, CELLS), BF16), ((8, CELLS), F32)],
        ((member % 2).reshape(1), slots, pert),
        scalars=1,
    )
    came = exchange(rims)
    y, b, gsel, ksel = call(
        first_stay_kernel,
        [state, border, ((GHOSTS, GHOSTS), BF16), ((GHOSTS, 128), F32)],
        (x, adj, sel, rows),
    )
    for step in range(1, STEPS):
        rims = call(rim_kernel, rim_shapes, (b, gsel, ksel, *came))
        shapes = [state, border] if step < STEPS - 1 else [state]
        y, *b = call(stay_kernel, shapes, (y, adj, sel, rows, *came))
        b = b[0] if b else None
        came = exchange(rims)
    (out,) = call(
        last_kernel, [((MEM, LEV, CELLS), F32)], (y, adj, rows, vloc, *came)
    )
    return lax.ppermute(out, AXES, SWAP)


def solution(mesh):
    near = Mesh(mesh.devices.reshape(8, 4, 2, 8), AXES)
    patch = ("x", "yh", "z")
    return jax.shard_map(
        local,
        mesh=near,
        in_specs=(
            P("member", None, patch),
            P(None, patch, "member"),
            P(patch),
            P(),
            P(None, patch),
            P(None, patch),
            P(patch),
        ),
        out_specs=P("member", None, patch),
        check_vma=False,
    )
```

time: 232 us -> 107 us (0.46)
  the two profiles are of different devices: /device:TPU:6 before, /device:TPU:7 now
where the time goes in v1:
time: 107 us
  starting transfers between devices  55.3 us (52%)
  waiting for transfers between devices  40.1 us (37%)
  Pallas kernels  7.37 us (7%)
  local copies, waits for them, and re-layouts  3.05 us (3%)
    ppermute x16, starting transfers between devices, exchange(): came = {d: lax.ppermute(rims[d], AXES, ROUTES[d]) for d in ORDER}  42 us
    ppermute x1, waiting for transfers between devices, local(): return lax.ppermute(out, AXES, SWAP)  15.4 us
    ppermute x16, waiting for transfers between devices, exchange(): came = {d: lax.ppermute(rims[d], AXES, ROUTES[d]) for d in ORDER}  14 us
    all_to_all x1, waiting for transfers between devices, local(): slots = lax.all_to_all(slots, ('yh', 'member'), 0, 0)  10.7 us
    ppermute x1, starting transfers between devices, local(): pert = lax.ppermute(perturbations, AXES, SWAP)  8.01 us
    pallas_call x10, Pallas kernels, call(): pl.pallas_call(kernel, out_shape=[jax.ShapeDtypeStruct(s, t) for s, t in...  7.37 us
    all_to_all x1, starting transfers between devices, local(): slots = lax.all_to_all(slots, ('yh', 'member'), 0, 0)  3.42 us
  transfers between devices with their start and end apart: 19, of which 8 were waited for; matrix products, arithmetic and copies ran while one was open for 0% of the time, Pallas kernels for 5%

profile of v1, /device:TPU:7, one launch (start us, length us, event | category | flops | bytes accessed | tf_op | source)
XLA Modules:
  0.0 106.8 jit_solution(266368134542468435)
XLA Ops:
  0.0 0.0 copy-start.3
  0.0 0.0 copy-start.2
  0.0 1.2 %copy.9 = f32[8,55,256]{2,1,0:T(8,128)S(1)} copy(f32[8,55,256]{2,0,1:T(8,128)} %param.7) | data formatting | bytes 901120 | tf_op args[0]
  1.2 0.0 copy-start.1
  1.2 8.0 %collective-permute-start = (f32[8,55,256]{2,1,0:T(8,128)S(1)}, f32[8,55,256]{2,1,0:T(8,128)S(1)}, u32[]{:S(2)}, u32[]{:S(2)}) collective-permute-start(f32[8,55,256]{2,1,0:T(8,128)S(1)} %copy.9), channel_id=1, source_target_pairs={{0,0},{1,1},{2,2},{3,3},{4,4},{5,5},{6,6},{7,7},{8,64},{9,65},{10,... | collective-permute-start | bytes 1351688 | tf_op jit(solution)/shard_map/ppermute | solution.py:203
  9.9 0.0 copy-done.3
  9.9 0.1 concatenate.17
  10.0 0.1 pad.5.clone
  10.1 0.0 copy-done.2
  10.1 0.0 copy-done.1
  10.1 0.1 copy.8
  10.2 0.1 add_convert_fusion
  10.2 0.0 copy-start.4
  10.2 0.7 copy-done.4
  10.9 0.8 shard_map.73
  11.7 3.4 %all-to-all-start = ((f32[16,24,128]{2,1,0:T(8,128)}), f32[16,24,128]{2,1,0:T(8,128)S(1)}, u32[]{:S(2)}, u32[]{:S(2)}) async-start(f32[16,24,128]{2,1,0:T(8,128)} %shard_map.73), calls=%async_computation | async-start | bytes 393216 | tf_op jit(solution)/shard_map/all_to_all | solution.py:221
  15.1 10.7 %all-to-all-done.slots = f32[16,24,128]{2,1,0:T(8,128)S(1)} async-done(((f32[16,24,128]{2,1,0:T(8,128)}), f32[16,24,128]{2,1,0:T(8,128)S(1)}, u32[]{:S(2)}, u32[]{:S(2)}) %all-to-all-start) | async-done | bytes 196640 | tf_op jit(solution)/shard_map/all_to_all | solution.py:221
  25.8 0.0 collective-permute-done.pert
  25.8 0.8 shard_map.74
  26.7 4.0 %collective-permute-start.1 = (f32[16,448]{1,0:T(8,128)S(1)}, f32[16,448]{1,0:T(8,128)S(1)}, u32[]{:S(2)}, u32[]{:S(2)}) collective-permute-start(f32[16,448]{1,0:T(8,128)S(1)} %get-tuple-element.38), channel_id=1, source_target_pairs={{0,1},{1,2},{2,3},{3,4},{4,5},{5,6},{6,7},{7,64},{8,9},{9,10},{10,... | collective-permute-start | bytes 86024 | tf_op jit(solution)/shard_map/ppermute | solution.py:198
  30.7 8.9 %collective-permute-start.2 = (f32[16,448]{1,0:T(8,128)S(1)}, f32[16,448]{1,0:T(8,128)S(1)}, u32[]{:S(2)}, u32[]{:S(2)}) collective-permute-start(f32[16,448]{1,0:T(8,128)S(1)} %get-tuple-element.39), channel_id=1, source_target_pairs={{0,119},{1,0},{2,1},{3,2},{4,3},{5,4},{6,5},{7,6},{8,127},{9,8},{1... | collective-permute-start | bytes 86024 | tf_op jit(solution)/shard_map/ppermute | solution.py:198
  39.5 2.4 %collective-permute-start.3 = (f32[16,448]{1,0:T(8,128)S(1)}, f32[16,448]{1,0:T(8,128)S(1)}, u32[]{:S(2)}, u32[]{:S(2)}) collective-permute-start(f32[16,448]{1,0:T(8,128)S(1)} %get-tuple-element.40), channel_id=1, source_target_pairs={{0,64},{1,65},{2,66},{3,67},{4,68},{5,69},{6,70},{7,71},{8,72},{9,... | collective-permute-start | bytes 86024 | tf_op jit(solution)/shard_map/ppermute | solution.py:198
  41.9 0.0 collective-permute-start.4
  41.9 0.9 shard_map.75
  42.8 0.0 collective-permute-done.1.i0
  42.8 0.0 collective-permute-done.2.i1
  42.8 0.1 collective-permute-done.3.i2
  43.0 3.5 %collective-permute-done.4.i3 = f32[16,448]{1,0:T(8,128)S(1)} collective-permute-done((f32[16,448]{1,0:T(8,128)S(1)}, f32[16,448]{1,0:T(8,128)S(1)}, u32[]{:S(2)}, u32[]{:S(2)}) %collective-permute-start.4) | collective-permute-done | bytes 28704 | tf_op jit(solution)/shard_map/ppermute | solution.py:198
  46.5 0.2 shard_map.77
  46.7 1.9 %collective-permute-start.5 = (f32[16,448]{1,0:T(8,128)S(1)}, f32[16,448]{1,0:T(8,128)S(1)}, u32[]{:S(2)}, u32[]{:S(2)}) collective-permute-start(f32[16,448]{1,0:T(8,128)S(1)} %get-tuple-element.46), channel_id=1, source_target_pairs={{0,1},{1,2},{2,3},{3,4},{4,5},{5,6},{6,7},{7,64},{8,9},{9,10},{10,... | collective-permute-start | bytes 86024 | tf_op jit(solution)/shard_map/ppermute | solution.py:198
  48.6 4.9 %collective-permute-start.6 = (f32[16,448]{1,0:T(8,128)S(1)}, f32[16,448]{1,0:T(8,128)S(1)}, u32[]{:S(2)}, u32[]{:S(2)}) collective-permute-start(f32[16,448]{1,0:T(8,128)S(1)} %get-tuple-element.47), channel_id=1, source_target_pairs={{0,119},{1,0},{2,1},{3,2},{4,3},{5,4},{6,5},{7,6},{8,127},{9,8},{1... | collective-permute-start | bytes 86024 | tf_op jit(solution)/shard_map/ppermute | solution.py:198
  53.5 2.1 %collective-permute-start.7 = (f32[16,448]{1,0:T(8,128)S(1)}, f32[16,448]{1,0:T(8,128)S(1)}, u32[]{:S(2)}, u32[]{:S(2)}) collective-permute-start(f32[16,448]{1,0:T(8,128)S(1)} %get-tuple-element.48), channel_id=1, source_target_pairs={{0,64},{1,65},{2,66},{3,67},{4,68},{5,69},{6,70},{7,71},{8,72},{9,... | collective-permute-start | bytes 86024 | tf_op jit(solution)/shard_map/ppermute | solution.py:198
  55.6 0.0 collective-permute-start.8
  55.6 1.2 %shard_map.76 = (f32[448,256]{1,0:T(8,128)S(1)}, f32[64,448]{1,0:T(8,128)S(1)}) custom-call(f32[448,256]{1,0:T(8,128)S(1)} %get-tuple-element.37.y, bf16[320,256]{1,0:T(8,128)(2,1)S(1)} %get-tuple-element.34.adj, bf16[64,256]{1,0:T(8,128)(2,1)S(1)} %get-tuple-element.35.sel, f32[8,256]{1,0:T(8,128)S(1)} %get-tuple-element.36.rows, ...), custom_call_target="tpu_custom_call" | custom-call | flops 100000000 | bytes 1000000 | tf_op jit(solution)/shard_map/pallas_call | solution.py:187
  56.8 0.0 collective-permute-done.5.i0
  56.8 0.0 collective-permute-done.6.i1
  56.8 0.0 collective-permute-done.7.i2
  56.8 3.4 %collective-permute-done.8.i3 = f32[16,448]{1,0:T(8,128)S(1)} collective-permute-done((f32[16,448]{1,0:T(8,128)S(1)}, f32[16,448]{1,0:T(8,128)S(1)}, u32[]{:S(2)}, u32[]{:S(2)}) %collective-permute-start.8) | collective-permute-done | bytes 28704 | tf_op jit(solution)/shard_map/ppermute | solution.py:198
  60.2 0.2 shard_map.79
  60.4 1.9 %collective-permute-start.9 = (f32[16,448]{1,0:T(8,128)S(1)}, f32[16,448]{1,0:T(8,128)S(1)}, u32[]{:S(2)}, u32[]{:S(2)}) collective-permute-start(f32[16,448]{1,0:T(8,128)S(1)} %get-tuple-element.52), channel_id=1, source_target_pairs={{0,1},{1,2},{2,3},{3,4},{4,5},{5,6},{6,7},{7,64},{8,9},{9,10},{10,... | collective-permute-start | bytes 86024 | tf_op jit(solution)/shard_map/ppermute | solution.py:198
  62.3 4.9 %collective-permute-start.10 = (f32[16,448]{1,0:T(8,128)S(1)}, f32[16,448]{1,0:T(8,128)S(1)}, u32[]{:S(2)}, u32[]{:S(2)}) collective-permute-start(f32[16,448]{1,0:T(8,128)S(1)} %get-tuple-element.53), channel_id=1, source_target_pairs={{0,119},{1,0},{2,1},{3,2},{4,3},{5,4},{6,5},{7,6},{8,127},{9,8},{1... | collective-permute-start | bytes 86024 | tf_op jit(solution)/shard_map/ppermute | solution.py:198
  67.1 2.1 %collective-permute-start.11 = (f32[16,448]{1,0:T(8,128)S(1)}, f32[16,448]{1,0:T(8,128)S(1)}, u32[]{:S(2)}, u32[]{:S(2)}) collective-permute-start(f32[16,448]{1,0:T(8,128)S(1)} %get-tuple-element.54), channel_id=1, source_target_pairs={{0,64},{1,65},{2,66},{3,67},{4,68},{5,69},{6,70},{7,71},{8,72},{9,... | collective-permute-start | bytes 86024 | tf_op jit(solution)/shard_map/ppermute | solution.py:198
  69.3 0.0 collective-permute-start.12
  69.3 1.2 %shard_map.78 = (f32[448,256]{1,0:T(8,128)S(1)}, f32[64,448]{1,0:T(8,128)S(1)}) custom-call(f32[448,256]{1,0:T(8,128)S(1)} %get-tuple-element.42.y, bf16[320,256]{1,0:T(8,128)(2,1)S(1)} %get-tuple-element.34.adj, bf16[64,256]{1,0:T(8,128)(2,1)S(1)} %get-tuple-element.35.sel, f32[8,256]{1,0:T(8,128)S(1)} %get-tuple-element.36.rows, ...), custom_call_target="tpu_custom_call" | custom-call | flops 100000000 | bytes 1000000 | tf_op jit(solution)/shard_map/pallas_call | solution.py:187
  70.4 0.0 collective-permute-done.9.i0
  70.4 0.0 collective-permute-done.10.i1
  70.4 0.0 collective-permute-done.11.i2
  70.5 3.4 %collective-permute-done.12.i3 = f32[16,448]{1,0:T(8,128)S(1)} collective-permute-done((f32[16,448]{1,0:T(8,128)S(1)}, f32[16,448]{1,0:T(8,128)S(1)}, u32[]{:S(2)}, u32[]{:S(2)}) %collective-permute-start.12) | collective-permute-done | bytes 28704 | tf_op jit(solution)/shard_map/ppermute | solution.py:198
  73.8 0.2 shard_map.81
  74.0 1.9 %collective-permute-start.13 = (f32[16,448]{1,0:T(8,128)S(1)}, f32[16,448]{1,0:T(8,128)S(1)}, u32[]{:S(2)}, u32[]{:S(2)}) collective-permute-start(f32[16,448]{1,0:T(8,128)S(1)} %get-tuple-element.57), channel_id=1, source_target_pairs={{0,1},{1,2},{2,3},{3,4},{4,5},{5,6},{6,7},{7,64},{8,9},{9,10},{10,... | collective-permute-start | bytes 86024 | tf_op jit(solution)/shard_map/ppermute | solution.py:198
  76.0 4.9 %collective-permute-start.14 = (f32[16,448]{1,0:T(8,128)S(1)}, f32[16,448]{1,0:T(8,128)S(1)}, u32[]{:S(2)}, u32[]{:S(2)}) collective-permute-start(f32[16,448]{1,0:T(8,128)S(1)} %get-tuple-element.58), channel_id=1, source_target_pairs={{0,119},{1,0},{2,1},{3,2},{4,3},{5,4},{6,5},{7,6},{8,127},{9,8},{1... | collective-permute-start | bytes 86024 | tf_op jit(solution)/shard_map/ppermute | solution.py:198
  80.8 2.1 %collective-permute-start.15 = (f32[16,448]{1,0:T(8,128)S(1)}, f32[16,448]{1,0:T(8,128)S(1)}, u32[]{:S(2)}, u32[]{:S(2)}) collective-permute-start(f32[16,448]{1,0:T(8,128)S(1)} %get-tuple-element.59), channel_id=1, source_target_pairs={{0,64},{1,65},{2,66},{3,67},{4,68},{5,69},{6,70},{7,71},{8,72},{9,... | collective-permute-start | bytes 86024 | tf_op jit(solution)/shard_map/ppermute | solution.py:198
  82.9 0.0 collective-permute-start.16
  82.9 0.0 copy-start
  82.9 0.9 shard_map.80.y
  83.8 0.0 collective-permute-done.13.i0
  83.9 0.0 collective-permute-done.14.i1
  83.9 0.1 collective-permute-done.15.i2
  84.0 3.5 %collective-permute-done.16.i3 = f32[16,448]{1,0:T(8,128)S(1)} collective-permute-done((f32[16,448]{1,0:T(8,128)S(1)}, f32[16,448]{1,0:T(8,128)S(1)}, u32[]{:S(2)}, u32[]{:S(2)}) %collective-permute-start.16) | collective-permute-done | bytes 28704 | tf_op jit(solution)/shard_map/ppermute | solution.py:198
  87.5 0.0 copy-done
  87.5 1.1 %shard_map.82 = f32[8,55,256]{2,1,0:T(8,128)S(1)} custom-call(f32[448,256]{1,0:T(8,128)S(1)} %shard_map.80.y, bf16[320,256]{1,0:T(8,128)(2,1)S(1)} %get-tuple-element.34.adj, f32[8,256]{1,0:T(8,128)S(1)} %get-tuple-element.36.rows, f32[55,55]{1,0:T(8,128)S(1)} %copy-done, f32[16,448]{1,0:T(8,128)S(1)} %collective-permute-done.13.i0, ...), custom_call_target="tpu_custom_call" | custom-call | flops 100000000 | bytes 1000000 | tf_op jit(solution)/shard_map/pallas_call | solution.py:187
  88.6 1.9 %collective-permute-start.17 = (f32[8,55,256]{2,1,0:T(8,128)S(1)}, f32[8,55,256]{2,1,0:T(8,128)S(1)}, u32[]{:S(2)}, u32[]{:S(2)}) collective-permute-start(f32[8,55,256]{2,1,0:T(8,128)S(1)} %shard_map.82), channel_id=1, source_target_pairs={{0,0},{1,1},{2,2},{3,3},{4,4},{5,5},{6,6},{7,7},{8,64},{9,65},{10,... | collective-permute-start | bytes 1351688 | tf_op jit(solution)/shard_map/ppermute | solution.py:247
  90.5 15.4 %collective-permute-done.17 = f32[8,55,256]{2,1,0:T(8,128)S(1)} collective-permute-done((f32[8,55,256]{2,1,0:T(8,128)S(1)}, f32[8,55,256]{2,1,0:T(8,128)S(1)}, u32[]{:S(2)}, u32[]{:S(2)}) %collective-permute-start.17) | collective-permute-done | bytes 450592 | tf_op jit(solution)/shard_map/ppermute | solution.py:247
  105.9 0.9 copy.10
  (3 shorter events, 0.0 us)
Async XLA Ops:
  0.0 9.9 %copy-start.3 = (s32[4,16]{1,0:T(4,128)S(1)}, s32[4,16]{1,0:T(4,128)}, u32[]{:S(2)}) copy-start(s32[4,16]{1,0:T(4,128)} %param.12) | copy-start | bytes 772
  0.0 10.1 %copy-start.2 = (s32[6,256]{1,0:T(8,128)S(1)}, s32[6,256]{1,0:T(8,128)}, u32[]{:S(2)}) copy-start(s32[6,256]{1,0:T(8,128)} %param.11) | copy-start | bytes 18436
  1.2 8.9 %copy-start.1 = (f32[55,1,32]{0,2,1:T(8,128)S(1)}, f32[55,1,32]{0,2,1:T(8,128)}, u32[]{:S(2)}) copy-start(f32[55,1,32]{0,2,1:T(8,128)} %param.8) | copy-start | bytes 21124
  1.2 24.6 %collective-permute-start = (f32[8,55,256]{2,1,0:T(8,128)S(1)}, f32[8,55,256]{2,1,0:T(8,128)S(1)}, u32[]{:S(2)}, u32[]{:S(2)}) collective-permute-start(f32[8,55,256]{2,1,0:T(8,128)S(1)} %copy.9), channel_id=1, source_target_pairs={{0,0},{1,1},{2,2},{3,3},{4,4},{5,5},{6,6},{7,7},{8,64},{9,65},{10,... | collective-permute-start | bytes 1351688 | tf_op jit(solution)/shard_map/ppermute | solution.py:203
  10.2 0.7 copy-start.4
  11.7 14.1 %all-to-all-start = ((f32[16,24,128]{2,1,0:T(8,128)}), f32[16,24,128]{2,1,0:T(8,128)S(1)}, u32[]{:S(2)}, u32[]{:S(2)}) async-start(f32[16,24,128]{2,1,0:T(8,128)} %shard_map.73), calls=%async_computation | async-start | bytes 393216 | tf_op jit(solution)/shard_map/all_to_all | solution.py:221
  26.7 16.2 %collective-permute-start.1 = (f32[16,448]{1,0:T(8,128)S(1)}, f32[16,448]{1,0:T(8,128)S(1)}, u32[]{:S(2)}, u32[]{:S(2)}) collective-permute-start(f32[16,448]{1,0:T(8,128)S(1)} %get-tuple-element.38), channel_id=1, source_target_pairs={{0,1},{1,2},{2,3},{3,4},{4,5},{5,6},{6,7},{7,64},{8,9},{9,10},{10,... | collective-permute-start | bytes 86024 | tf_op jit(solution)/shard_map/ppermute | solution.py:198
  30.7 12.2 %collective-permute-start.2 = (f32[16,448]{1,0:T(8,128)S(1)}, f32[16,448]{1,0:T(8,128)S(1)}, u32[]{:S(2)}, u32[]{:S(2)}) collective-permute-start(f32[16,448]{1,0:T(8,128)S(1)} %get-tuple-element.39), channel_id=1, source_target_pairs={{0,119},{1,0},{2,1},{3,2},{4,3},{5,4},{6,5},{7,6},{8,127},{9,8},{1... | collective-permute-start | bytes 86024 | tf_op jit(solution)/shard_map/ppermute | solution.py:198
  39.5 3.4 %collective-permute-start.3 = (f32[16,448]{1,0:T(8,128)S(1)}, f32[16,448]{1,0:T(8,128)S(1)}, u32[]{:S(2)}, u32[]{:S(2)}) collective-permute-start(f32[16,448]{1,0:T(8,128)S(1)} %get-tuple-element.40), channel_id=1, source_target_pairs={{0,64},{1,65},{2,66},{3,67},{4,68},{5,69},{6,70},{7,71},{8,72},{9,... | collective-permute-start | bytes 86024 | tf_op jit(solution)/shard_map/ppermute | solution.py:198
  41.9 4.6 %collective-permute-start.4 = (f32[16,448]{1,0:T(8,128)S(1)}, f32[16,448]{1,0:T(8,128)S(1)}, u32[]{:S(2)}, u32[]{:S(2)}) collective-permute-start(f32[16,448]{1,0:T(8,128)S(1)} %get-tuple-element.41), channel_id=1, source_target_pairs={{0,112},{1,113},{2,114},{3,115},{4,116},{5,117},{6,118},{7,119},{8... | collective-permute-start | bytes 86024 | tf_op jit(solution)/shard_map/ppermute | solution.py:198
  46.7 10.1 %collective-permute-start.5 = (f32[16,448]{1,0:T(8,128)S(1)}, f32[16,448]{1,0:T(8,128)S(1)}, u32[]{:S(2)}, u32[]{:S(2)}) collective-permute-start(f32[16,448]{1,0:T(8,128)S(1)} %get-tuple-element.46), channel_id=1, source_target_pairs={{0,1},{1,2},{2,3},{3,4},{4,5},{5,6},{6,7},{7,64},{8,9},{9,10},{10,... | collective-permute-start | bytes 86024 | tf_op jit(solution)/shard_map/ppermute | solution.py:198
  48.6 8.2 %collective-permute-start.6 = (f32[16,448]{1,0:T(8,128)S(1)}, f32[16,448]{1,0:T(8,128)S(1)}, u32[]{:S(2)}, u32[]{:S(2)}) collective-permute-start(f32[16,448]{1,0:T(8,128)S(1)} %get-tuple-element.47), channel_id=1, source_target_pairs={{0,119},{1,0},{2,1},{3,2},{4,3},{5,4},{6,5},{7,6},{8,127},{9,8},{1... | collective-permute-start | bytes 86024 | tf_op jit(solution)/shard_map/ppermute | solution.py:198
  53.5 3.3 %collective-permute-start.7 = (f32[16,448]{1,0:T(8,128)S(1)}, f32[16,448]{1,0:T(8,128)S(1)}, u32[]{:S(2)}, u32[]{:S(2)}) collective-permute-start(f32[16,448]{1,0:T(8,128)S(1)} %get-tuple-element.48), channel_id=1, source_target_pairs={{0,64},{1,65},{2,66},{3,67},{4,68},{5,69},{6,70},{7,71},{8,72},{9,... | collective-permute-start | bytes 86024 | tf_op jit(solution)/shard_map/ppermute | solution.py:198
  55.6 4.6 %collective-permute-start.8 = (f32[16,448]{1,0:T(8,128)S(1)}, f32[16,448]{1,0:T(8,128)S(1)}, u32[]{:S(2)}, u32[]{:S(2)}) collective-permute-start(f32[16,448]{1,0:T(8,128)S(1)} %get-tuple-element.49), channel_id=1, source_target_pairs={{0,112},{1,113},{2,114},{3,115},{4,116},{5,117},{6,118},{7,119},{8... | collective-permute-start | bytes 86024 | tf_op jit(solution)/shard_map/ppermute | solution.py:198
  60.4 10.1 %collective-permute-start.9 = (f32[16,448]{1,0:T(8,128)S(1)}, f32[16,448]{1,0:T(8,128)S(1)}, u32[]{:S(2)}, u32[]{:S(2)}) collective-permute-start(f32[16,448]{1,0:T(8,128)S(1)} %get-tuple-element.52), channel_id=1, source_target_pairs={{0,1},{1,2},{2,3},{3,4},{4,5},{5,6},{6,7},{7,64},{8,9},{9,10},{10,... | collective-permute-start | bytes 86024 | tf_op jit(solution)/shard_map/ppermute | solution.py:198
  62.3 8.2 %collective-permute-start.10 = (f32[16,448]{1,0:T(8,128)S(1)}, f32[16,448]{1,0:T(8,128)S(1)}, u32[]{:S(2)}, u32[]{:S(2)}) collective-permute-start(f32[16,448]{1,0:T(8,128)S(1)} %get-tuple-element.53), channel_id=1, source_target_pairs={{0,119},{1,0},{2,1},{3,2},{4,3},{5,4},{6,5},{7,6},{8,127},{9,8},{1... | collective-permute-start | bytes 86024 | tf_op jit(solution)/shard_map/ppermute | solution.py:198
  67.1 3.3 %collective-permute-start.11 = (f32[16,448]{1,0:T(8,128)S(1)}, f32[16,448]{1,0:T(8,128)S(1)}, u32[]{:S(2)}, u32[]{:S(2)}) collective-permute-start(f32[16,448]{1,0:T(8,128)S(1)} %get-tuple-element.54), channel_id=1, source_target_pairs={{0,64},{1,65},{2,66},{3,67},{4,68},{5,69},{6,70},{7,71},{8,72},{9,... | collective-permute-start | bytes 86024 | tf_op jit(solution)/shard_map/ppermute | solution.py:198
  69.3 4.6 %collective-permute-start.12 = (f32[16,448]{1,0:T(8,128)S(1)}, f32[16,448]{1,0:T(8,128)S(1)}, u32[]{:S(2)}, u32[]{:S(2)}) collective-permute-start(f32[16,448]{1,0:T(8,128)S(1)} %get-tuple-element.55), channel_id=1, source_target_pairs={{0,112},{1,113},{2,114},{3,115},{4,116},{5,117},{6,118},{7,119},{8... | collective-permute-start | bytes 86024 | tf_op jit(solution)/shard_map/ppermute | solution.py:198
  74.0 9.8 %collective-permute-start.13 = (f32[16,448]{1,0:T(8,128)S(1)}, f32[16,448]{1,0:T(8,128)S(1)}, u32[]{:S(2)}, u32[]{:S(2)}) collective-permute-start(f32[16,448]{1,0:T(8,128)S(1)} %get-tuple-element.57), channel_id=1, source_target_pairs={{0,1},{1,2},{2,3},{3,4},{4,5},{5,6},{6,7},{7,64},{8,9},{9,10},{10,... | collective-permute-start | bytes 86024 | tf_op jit(solution)/shard_map/ppermute | solution.py:198
  76.0 7.9 %collective-permute-start.14 = (f32[16,448]{1,0:T(8,128)S(1)}, f32[16,448]{1,0:T(8,128)S(1)}, u32[]{:S(2)}, u32[]{:S(2)}) collective-permute-start(f32[16,448]{1,0:T(8,128)S(1)} %get-tuple-element.58), channel_id=1, source_target_pairs={{0,119},{1,0},{2,1},{3,2},{4,3},{5,4},{6,5},{7,6},{8,127},{9,8},{1... | collective-permute-start | bytes 86024 | tf_op jit(solution)/shard_map/ppermute | solution.py:198
  80.8 3.1 %collective-permute-start.15 = (f32[16,448]{1,0:T(8,128)S(1)}, f32[16,448]{1,0:T(8,128)S(1)}, u32[]{:S(2)}, u32[]{:S(2)}) collective-permute-start(f32[16,448]{1,0:T(8,128)S(1)} %get-tuple-element.59), channel_id=1, source_target_pairs={{0,64},{1,65},{2,66},{3,67},{4,68},{5,69},{6,70},{7,71},{8,72},{9,... | collective-permute-start | bytes 86024 | tf_op jit(solution)/shard_map/ppermute | solution.py:198
  82.9 4.6 %collective-permute-start.16 = (f32[16,448]{1,0:T(8,128)S(1)}, f32[16,448]{1,0:T(8,128)S(1)}, u32[]{:S(2)}, u32[]{:S(2)}) collective-permute-start(f32[16,448]{1,0:T(8,128)S(1)} %get-tuple-element.60), channel_id=1, source_target_pairs={{0,112},{1,113},{2,114},{3,115},{4,116},{5,117},{6,118},{7,119},{8... | collective-permute-start | bytes 86024 | tf_op jit(solution)/shard_map/ppermute | solution.py:198
  82.9 4.5 %copy-start = (f32[55,55]{1,0:T(8,128)S(1)}, f32[55,55]{1,0:T(8,128)}, u32[]{:S(2)}) copy-start(f32[55,55]{1,0:T(8,128)} %vloc.1) | copy-start | bytes 36304
  88.6 17.3 %collective-permute-start.17 = (f32[8,55,256]{2,1,0:T(8,128)S(1)}, f32[8,55,256]{2,1,0:T(8,128)S(1)}, u32[]{:S(2)}, u32[]{:S(2)}) collective-permute-start(f32[8,55,256]{2,1,0:T(8,128)S(1)} %shard_map.82), channel_id=1, source_target_pairs={{0,0},{1,1},{2,2},{3,3},{4,4},{5,5},{6,6},{7,7},{8,64},{9,65},{10,... | collective-permute-start | bytes 1351688 | tf_op jit(solution)/shard_map/ppermute | solution.py:247

commit v2 on v1

--- a/solution.py
+++ b/solution.py
@@ -11,9 +11,8 @@
 STEPS = 4
 AXES = ("member", "x", "yh", "z")
 LEV = 55
-ROWS = 56
 MEM = 8
-FIELDS = MEM * ROWS
+FIELDS = LEV * MEM
 CELLS = 256
 RIM = 16
 GHOSTS = 4 * RIM
@@ -43,7 +42,7 @@
 WEST = sorted((b, a) for a, b in EAST)
 SOUTH = pairs(lambda x, yh, l, z, core: (x + core, yh, l, z, 1 - core))
 NORTH = sorted((b, a) for a, b in SOUTH)
-ROUTES = (EAST, WEST, SOUTH, NORTH)
+ROUTES = (EAST, SOUTH, WEST, NORTH)
 ORDER = (0, 2, 1, 3)
 
 
@@ -65,11 +64,15 @@
     return total
 
 
-def pack_kernel(member, grad, table, out):
-    piece = jnp.concatenate([grad[...], jnp.zeros((4 * RIM - LEV, 32), F32)], axis=0)
-    out[0, 0:RIM, :] = jnp.concatenate(
-        [piece[g * RIM : (g + 1) * RIM] for g in range(4)], axis=1
-    )
+def pack_kernel(member, count, grad, kappa, named, sends, out, table):
+    table[0:6, :] = named[...].astype(F32)
+    table[6:7, :] = kappa[...]
+    row = [sends[d : d + 1, :].astype(F32) for d in range(4)]
+    row.append(jnp.full((1, 128 - GHOSTS), count[0].astype(F32)))
+    table[7:8, 0:128] = jnp.concatenate(row, axis=1)
+    table[7:8, 128:] = jnp.zeros((1, 128), F32)
+    piece = jnp.concatenate([grad[...], jnp.zeros((32, 64 - LEV), F32)], axis=1)
+    out[0, 0:RIM, :] = jnp.concatenate([piece[0:RIM], piece[RIM:]], axis=1)
     row = table[pl.ds(member[0], 1), :]
     out[0, RIM:, :] = jnp.concatenate(
         [row[:, :128], row[:, 128:], jnp.zeros((SLOT - RIM - 2, 128), F32)], axis=0
@@ -79,26 +82,21 @@
 
 
 def rims_out(rims, outs):
-    for d in range(4):
-        outs[d][...] = rims[d * RIM : (d + 1) * RIM]
+    for d, out in zip(ORDER, outs):
+        out[...] = rims[d * RIM : (d + 1) * RIM]
+
+
+def joined(arrived):
+    return jnp.concatenate([arrived[d][...] for d in ORDER], axis=0)
 
 
 def first_kernel(core, slots, pert, r0, r1, r2, r3, x_out, adj_out, sel_out, rows_out):
     base = core[0] * MEM
-    lane = lax.broadcasted_iota(jnp.int32, (RIM, 128), 1)
-    halves = [[], []]
-    for g in range(4):
-        for half in range(2):
-            total = jnp.zeros((RIM, 128), F32)
-            for i in range(4):
-                piece = slots[base + half * 4 + i, 0:RIM, :]
-                shift = (32 * (i - g)) % 128
-                moved = pltpu.roll(piece, shift, 1) if shift else piece
-                total = jnp.where(lane // 32 == i, moved, total)
-            halves[half].append(total)
-    grad = jnp.concatenate(
-        [jnp.concatenate(halves[0], axis=0), jnp.concatenate(halves[1], axis=0)], axis=1
-    )
+    cells = []
+    for m in range(MEM):
+        two = slots[base + m, 0:RIM, :]
+        cells += [two, pltpu.roll(two, 64, 1)]
+    grad = jnp.concatenate(cells, axis=0).T
 
     def table_row(j):
         two = slots[base + j, RIM : RIM + 8, :]
@@ -119,18 +117,13 @@
     sel = (sends == lax.broadcasted_iota(jnp.int32, (GHOSTS, CELLS), 1)).astype(F32)
     sel = sel.astype(BF16)
     sel_out[...] = sel
-    count = jnp.max(
-        jnp.where(lax.broadcasted_iota(jnp.int32, (1, 128), 1) == GHOSTS, misc[:, :128], 0.0),
-        axis=1,
-        keepdims=True,
-    ).astype(jnp.int32)
+    count = misc[:, GHOSTS : GHOSTS + 1].astype(jnp.int32)
     alive = (lax.broadcasted_iota(jnp.int32, (1, CELLS), 1) < count).astype(F32)
     rows_out[...] = jnp.concatenate(
         [kappa, 1.0 - degree * kappa, alive, jnp.zeros((5, CELLS), F32)], axis=0
     )
-    for m in range(MEM):
-        x_out[m * ROWS : m * ROWS + LEV, :] = pert[m] * grad[0:LEV]
-        x_out[m * ROWS + LEV : (m + 1) * ROWS, :] = jnp.zeros((1, CELLS), F32)
+    for l in range(LEV):
+        x_out[l * MEM : (l + 1) * MEM, :] = pert[l * MEM : (l + 1) * MEM, :] * grad[l : l + 1]
     rims = exact_dot(sel, kappa * x_out[...], ((1,), (1,)))
     rims_out(rims, (r0, r1, r2, r3))
 
@@ -154,13 +147,13 @@
 
 
 def rim_kernel(b, gsel, ksel, i0, i1, i2, i3, r0, r1, r2, r3):
-    came = jnp.concatenate([i0[...], i1[...], i2[...], i3[...]], axis=0)
+    came = joined((i0, i1, i2, i3))
     rims = b[...] + ksel[:, 0:1] * exact_dot(gsel[...], came, ((1,), (0,)))
     rims_out(rims, (r0, r1, r2, r3))
 
 
 def arrive(y, adj, i0, i1, i2, i3):
-    came = jnp.concatenate([i0[...], i1[...], i2[...], i3[...]], axis=0)
+    came = joined((i0, i1, i2, i3))
     return y[...] + exact_dot(came.T, adj[CELLS:, :], ((1,), (0,)))
 
 
@@ -168,55 +161,61 @@
     stay(arrive(y, adj, i0, i1, i2, i3), adj, sel, rows, y_out, b_out)
 
 
-def last_kernel(y, adj, rows, vloc, i0, i1, i2, i3, out):
-    x = arrive(y, adj, i0, i1, i2, i3)
-    mix = vloc[...].T
-    for m in range(MEM):
-        part = x[m * ROWS : m * ROWS + LEV] * rows[2:3, :]
-        out[m] = jnp.dot(
-            mix, part, precision=lax.Precision.HIGHEST, preferred_element_type=F32
-        )
+def mix_kernel(vloc, out):
+    level = lax.broadcasted_iota(jnp.int32, (FIELDS, 128), 0) // MEM
+    spread = (level == lax.broadcasted_iota(jnp.int32, (FIELDS, 128), 1)).astype(BF16)
+    wide = exact_dot(spread[:, 0:LEV], vloc[...].T, ((1,), (0,)))
+    full = exact_dot(wide, spread[:, 0:LEV], ((1,), (1,)))
+    row = lax.broadcasted_iota(jnp.int32, (FIELDS, FIELDS), 0) % MEM
+    column = lax.broadcasted_iota(jnp.int32, (FIELDS, FIELDS), 1) % MEM
+    out[...] = jnp.where(row == column, full, 0.0)
+
+
+def last_kernel(y, adj, rows, mix, i0, i1, i2, i3, out):
+    x = arrive(y, adj, i0, i1, i2, i3) * rows[2:3, :]
+    out[...] = jnp.dot(
+        mix[...], x, precision=lax.Precision.HIGHEST, preferred_element_type=F32
+    )
 
 
 VM = pl.BlockSpec(memory_space=pltpu.VMEM)
 SM = pl.BlockSpec(memory_space=pltpu.SMEM)
 
 
-def call(kernel, shapes, args, scalars=0, flops=10**8):
+def call(kernel, shapes, args, scalars=0, flops=10**8, scratch=()):
     specs = [SM] * scalars + [VM] * (len(args) - scalars)
     return pl.pallas_call(
         kernel,
         out_shape=[jax.ShapeDtypeStruct(s, t) for s, t in shapes],
         in_specs=specs,
         out_specs=[VM] * len(shapes),
+        scratch_shapes=list(scratch),
         cost_estimate=pl.CostEstimate(flops=flops, bytes_accessed=10**6, transcendentals=0),
         compiler_params=pltpu.CompilerParams(vmem_limit_bytes=32 * 1024 * 1024),
     )(*args)
 
 
 def exchange(rims):
-    came = {d: lax.ppermute(rims[d], AXES, ROUTES[d]) for d in ORDER}
-    return [came[d] for d in range(4)]
+    return [lax.ppermute(rims[d], AXES, ROUTES[d]) for d in range(4)]
 
 
 def local(perturbations, gradient, kappa, vloc, neighbors, send_lists, counts):
-    pert = lax.ppermute(perturbations, AXES, SWAP)
+    fields = perturbations.transpose(1, 0, 2).reshape(FIELDS, CELLS)
+    pert = lax.ppermute(fields, AXES, SWAP)
     member = lax.axis_index("member")
-    misc = jnp.concatenate(
-        [
-            send_lists.reshape(GHOSTS),
-            counts.reshape(1),
-            jnp.zeros((CELLS - GHOSTS - 1,), jnp.int32),
-        ]
-    )
-    table = jnp.concatenate(
-        [neighbors.astype(F32), kappa.reshape(1, CELLS), misc.reshape(1, CELLS).astype(F32)]
-    )
     (slots,) = call(
         pack_kernel,
         [((16, SLOT, 128), F32)],
-        (member.reshape(1), gradient.reshape(LEV, 32), table),
-        scalars=1,
+        (
+            member.reshape(1),
+            counts,
+            gradient.reshape(LEV, 32).T,
+            kappa.reshape(1, CELLS),
+            neighbors,
+            send_lists,
+        ),
+        scalars=2,
+        scratch=[pltpu.VMEM((8, CELLS), F32)],
     )
     slots = lax.all_to_all(slots, ("yh", "member"), 0, 0)
     rim_shapes = [((RIM, FIELDS), F32)] * 4
@@ -241,10 +240,10 @@
         y, *b = call(stay_kernel, shapes, (y, adj, sel, rows, *came))
         b = b[0] if b else None
         came = exchange(rims)
-    (out,) = call(
-        last_kernel, [((MEM, LEV, CELLS), F32)], (y, adj, rows, vloc, *came)
-    )
-    return lax.ppermute(out, AXES, SWAP)
+    (mix,) = call(mix_kernel, [((FIELDS, FIELDS), F32)], (vloc,))
+    (out,) = call(last_kernel, [state], (y, adj, rows, mix, *came))
+    out = lax.ppermute(out, AXES, SWAP)
+    return out.reshape(LEV, MEM, CELLS).transpose(1, 0, 2)
 
 
 def solution(mesh):

time: 107 us -> 100 us (0.935)
  the two profiles are of different devices: /device:TPU:7 before, /device:TPU:1 now
where the time goes in v2:
time: 100 us; the launch traced here: 99.6 us
  starting transfers between devices  62.1 us (62%)
  waiting for transfers between devices  24.9 us (25%)
  Pallas kernels  8.8 us (9%)
  local copies, waits for them, and re-layouts  2.81 us (3%)
    ppermute x16, starting transfers between devices, exchange(): return [lax.ppermute(rims[d], AXES, ROUTES[d]) for d in range(4)]  44 us
    ppermute x1, waiting for transfers between devices, local(): out = lax.ppermute(out, AXES, SWAP)  12.8 us
    all_to_all x1, waiting for transfers between devices, local(): slots = lax.all_to_all(slots, ('yh', 'member'), 0, 0)  11.4 us
    ppermute x1, starting transfers between devices, local(): pert = lax.ppermute(fields, AXES, SWAP)  8.96 us
    pallas_call x11, Pallas kernels, call(): pl.pallas_call(kernel, out_shape=[jax.ShapeDtypeStruct(s, t) for s, t in...  8.8 us
    ppermute x1, starting transfers between devices, local(): out = lax.ppermute(out, AXES, SWAP)  5.73 us
    all_to_all x1, starting transfers between devices, local(): slots = lax.all_to_all(slots, ('yh', 'member'), 0, 0)  3.42 us
    unnamed x11, local copies, waits for them, and re-layouts  2.81 us
  transfers between devices with their start and end apart: 19, of which 4 were waited for; matrix products, arithmetic and copies ran while one was open for 0% of the time, Pallas kernels for 6%

profile of v2, /device:TPU:1, one launch (start us, length us, event | category | flops | bytes accessed | tf_op | source)
XLA Modules:
  0.0 99.6 jit_solution(12652136448572241857)
XLA Ops:
  0.0 0.0 copy-start.1
  0.0 9.0 %collective-permute-start = (f32[440,256]{1,0:T(8,128)}, f32[440,256]{1,0:T(8,128)S(1)}, u32[]{:S(2)}, u32[]{:S(2)}) collective-permute-start(f32[440,256]{1,0:T(8,128)} %bitcast.15), channel_id=1, source_target_pairs={{0,0},{1,1},{2,2},{3,3},{4,4},{5,5},{6,6},{7,7},{8,64},{9,65},{10,... | collective-permute-start | bytes 1351688 | tf_op jit(solution)/shard_map/ppermute | solution.py:204
  9.6 0.0 copy-start.4
  9.6 0.0 copy-done.1
  9.6 0.7 copy-done.4
  10.3 0.0 copy-start.2
  10.3 0.7 copy-done.2
  11.0 0.0 copy-start.3
  11.0 0.7 copy-done.3
  11.7 0.8 shard_map.73
  12.4 3.4 %all-to-all-start = ((f32[16,24,128]{2,1,0:T(8,128)}), f32[16,24,128]{2,1,0:T(8,128)S(1)}, u32[]{:S(2)}, u32[]{:S(2)}) async-start(f32[16,24,128]{2,1,0:T(8,128)} %shard_map.73), calls=%async_computation | async-start | bytes 393216 | tf_op jit(solution)/shard_map/all_to_all | solution.py:220
  15.9 11.4 %all-to-all-done.slots = f32[16,24,128]{2,1,0:T(8,128)S(1)} async-done(((f32[16,24,128]{2,1,0:T(8,128)}), f32[16,24,128]{2,1,0:T(8,128)S(1)}, u32[]{:S(2)}, u32[]{:S(2)}) %all-to-all-start) | async-done | bytes 196640 | tf_op jit(solution)/shard_map/all_to_all | solution.py:220
  27.3 0.0 collective-permute-done.pert
  27.3 0.9 shard_map.74
  28.3 2.9 %collective-permute-start.1 = (f32[16,440]{1,0:T(8,128)S(1)}, f32[16,440]{1,0:T(8,128)S(1)}, u32[]{:S(2)}, u32[]{:S(2)}) collective-permute-start(f32[16,440]{1,0:T(8,128)S(1)} %get-tuple-element.38), channel_id=1, source_target_pairs={{0,1},{1,2},{2,3},{3,4},{4,5},{5,6},{6,7},{7,64},{8,9},{9,10},{10,... | collective-permute-start | bytes 84488 | tf_op jit(solution)/shard_map/ppermute | solution.py:199
  31.2 1.3 %collective-permute-start.2 = (f32[16,440]{1,0:T(8,128)S(1)}, f32[16,440]{1,0:T(8,128)S(1)}, u32[]{:S(2)}, u32[]{:S(2)}) collective-permute-start(f32[16,440]{1,0:T(8,128)S(1)} %get-tuple-element.39), channel_id=1, source_target_pairs={{0,64},{1,65},{2,66},{3,67},{4,68},{5,69},{6,70},{7,71},{8,72},{9,... | collective-permute-start | bytes 84488 | tf_op jit(solution)/shard_map/ppermute | solution.py:199
  32.4 7.7 %collective-permute-start.3 = (f32[16,440]{1,0:T(8,128)S(1)}, f32[16,440]{1,0:T(8,128)S(1)}, u32[]{:S(2)}, u32[]{:S(2)}) collective-permute-start(f32[16,440]{1,0:T(8,128)S(1)} %get-tuple-element.40), channel_id=1, source_target_pairs={{0,119},{1,0},{2,1},{3,2},{4,3},{5,4},{6,5},{7,6},{8,127},{9,8},{1... | collective-permute-start | bytes 84488 | tf_op jit(solution)/shard_map/ppermute | solution.py:199
  40.1 2.2 %collective-permute-start.4 = (f32[16,440]{1,0:T(8,128)S(1)}, f32[16,440]{1,0:T(8,128)S(1)}, u32[]{:S(2)}, u32[]{:S(2)}) collective-permute-start(f32[16,440]{1,0:T(8,128)S(1)} %get-tuple-element.41), channel_id=1, source_target_pairs={{0,112},{1,113},{2,114},{3,115},{4,116},{5,117},{6,118},{7,119},{8... | collective-permute-start | bytes 84488 | tf_op jit(solution)/shard_map/ppermute | solution.py:199
  42.4 0.9 shard_map.75
  43.3 0.0 collective-permute-done.1.i0
  43.3 0.0 collective-permute-done.2.i1
  43.3 0.0 collective-permute-done.3.i2
  43.3 0.5 collective-permute-done.4.i3
  43.8 0.2 shard_map.77
  44.0 1.9 %collective-permute-start.5 = (f32[16,440]{1,0:T(8,128)S(1)}, f32[16,440]{1,0:T(8,128)S(1)}, u32[]{:S(2)}, u32[]{:S(2)}) collective-permute-start(f32[16,440]{1,0:T(8,128)S(1)} %get-tuple-element.46), channel_id=1, source_target_pairs={{0,1},{1,2},{2,3},{3,4},{4,5},{5,6},{6,7},{7,64},{8,9},{9,10},{10,... | collective-permute-start | bytes 84488 | tf_op jit(solution)/shard_map/ppermute | solution.py:199
  45.9 0.0 collective-permute-start.6
  46.0 4.9 %collective-permute-start.7 = (f32[16,440]{1,0:T(8,128)S(1)}, f32[16,440]{1,0:T(8,128)S(1)}, u32[]{:S(2)}, u32[]{:S(2)}) collective-permute-start(f32[16,440]{1,0:T(8,128)S(1)} %get-tuple-element.48), channel_id=1, source_target_pairs={{0,119},{1,0},{2,1},{3,2},{4,3},{5,4},{6,5},{7,6},{8,127},{9,8},{1... | collective-permute-start | bytes 84488 | tf_op jit(solution)/shard_map/ppermute | solution.py:199
  50.8 2.9 %collective-permute-start.8 = (f32[16,440]{1,0:T(8,128)S(1)}, f32[16,440]{1,0:T(8,128)S(1)}, u32[]{:S(2)}, u32[]{:S(2)}) collective-permute-start(f32[16,440]{1,0:T(8,128)S(1)} %get-tuple-element.49), channel_id=1, source_target_pairs={{0,112},{1,113},{2,114},{3,115},{4,116},{5,117},{6,118},{7,119},{8... | collective-permute-start | bytes 84488 | tf_op jit(solution)/shard_map/ppermute | solution.py:199
  53.8 1.2 %shard_map.76 = (f32[440,256]{1,0:T(8,128)S(1)}, f32[64,440]{1,0:T(8,128)S(1)}) custom-call(f32[440,256]{1,0:T(8,128)S(1)} %get-tuple-element.37.y, bf16[320,256]{1,0:T(8,128)(2,1)S(1)} %get-tuple-element.34.adj, bf16[64,256]{1,0:T(8,128)(2,1)S(1)} %get-tuple-element.35.sel, f32[8,256]{1,0:T(8,128)S(1)} %get-tuple-element.36.rows, ...), custom_call_target="tpu_custom_call" | custom-call | flops 100000000 | bytes 1000000 | tf_op jit(solution)/shard_map/pallas_call | solution.py:187
  54.9 0.0 collective-permute-done.5.i0
  54.9 0.0 collective-permute-done.6.i1
  54.9 0.0 collective-permute-done.7.i2
  55.0 0.1 collective-permute-done.8.i3
  55.1 0.2 shard_map.79
  55.3 1.9 %collective-permute-start.9 = (f32[16,440]{1,0:T(8,128)S(1)}, f32[16,440]{1,0:T(8,128)S(1)}, u32[]{:S(2)}, u32[]{:S(2)}) collective-permute-start(f32[16,440]{1,0:T(8,128)S(1)} %get-tuple-element.52), channel_id=1, source_target_pairs={{0,1},{1,2},{2,3},{3,4},{4,5},{5,6},{6,7},{7,64},{8,9},{9,10},{10,... | collective-permute-start | bytes 84488 | tf_op jit(solution)/shard_map/ppermute | solution.py:199
  57.2 0.0 collective-permute-start.10
  57.2 4.9 %collective-permute-start.11 = (f32[16,440]{1,0:T(8,128)S(1)}, f32[16,440]{1,0:T(8,128)S(1)}, u32[]{:S(2)}, u32[]{:S(2)}) collective-permute-start(f32[16,440]{1,0:T(8,128)S(1)} %get-tuple-element.54), channel_id=1, source_target_pairs={{0,119},{1,0},{2,1},{3,2},{4,3},{5,4},{6,5},{7,6},{8,127},{9,8},{1... | collective-permute-start | bytes 84488 | tf_op jit(solution)/shard_map/ppermute | solution.py:199
  62.1 3.2 %collective-permute-start.12 = (f32[16,440]{1,0:T(8,128)S(1)}, f32[16,440]{1,0:T(8,128)S(1)}, u32[]{:S(2)}, u32[]{:S(2)}) collective-permute-start(f32[16,440]{1,0:T(8,128)S(1)} %get-tuple-element.55), channel_id=1, source_target_pairs={{0,112},{1,113},{2,114},{3,115},{4,116},{5,117},{6,118},{7,119},{8... | collective-permute-start | bytes 84488 | tf_op jit(solution)/shard_map/ppermute | solution.py:199
  65.3 1.2 %shard_map.78 = (f32[440,256]{1,0:T(8,128)S(1)}, f32[64,440]{1,0:T(8,128)S(1)}) custom-call(f32[440,256]{1,0:T(8,128)S(1)} %get-tuple-element.42.y, bf16[320,256]{1,0:T(8,128)(2,1)S(1)} %get-tuple-element.34.adj, bf16[64,256]{1,0:T(8,128)(2,1)S(1)} %get-tuple-element.35.sel, f32[8,256]{1,0:T(8,128)S(1)} %get-tuple-element.36.rows, ...), custom_call_target="tpu_custom_call" | custom-call | flops 100000000 | bytes 1000000 | tf_op jit(solution)/shard_map/pallas_call | solution.py:187
  66.5 0.0 collective-permute-done.9.i0
  66.5 0.0 collective-permute-done.10.i1
  66.5 0.0 collective-permute-done.11.i2
  66.5 0.0 collective-permute-done.12.i3
  66.5 0.0 copy-start
  66.5 0.2 shard_map.82
  66.8 1.9 %collective-permute-start.13 = (f32[16,440]{1,0:T(8,128)S(1)}, f32[16,440]{1,0:T(8,128)S(1)}, u32[]{:S(2)}, u32[]{:S(2)}) collective-permute-start(f32[16,440]{1,0:T(8,128)S(1)} %get-tuple-element.57), channel_id=1, source_target_pairs={{0,1},{1,2},{2,3},{3,4},{4,5},{5,6},{6,7},{7,64},{8,9},{9,10},{10,... | collective-permute-start | bytes 84488 | tf_op jit(solution)/shard_map/ppermute | solution.py:199
  68.7 0.0 collective-permute-start.14
  68.7 4.9 %collective-permute-start.15 = (f32[16,440]{1,0:T(8,128)S(1)}, f32[16,440]{1,0:T(8,128)S(1)}, u32[]{:S(2)}, u32[]{:S(2)}) collective-permute-start(f32[16,440]{1,0:T(8,128)S(1)} %get-tuple-element.59), channel_id=1, source_target_pairs={{0,119},{1,0},{2,1},{3,2},{4,3},{5,4},{6,5},{7,6},{8,127},{9,8},{1... | collective-permute-start | bytes 84488 | tf_op jit(solution)/shard_map/ppermute | solution.py:199
  73.6 3.3 %collective-permute-start.16 = (f32[16,440]{1,0:T(8,128)S(1)}, f32[16,440]{1,0:T(8,128)S(1)}, u32[]{:S(2)}, u32[]{:S(2)}) collective-permute-start(f32[16,440]{1,0:T(8,128)S(1)} %get-tuple-element.60), channel_id=1, source_target_pairs={{0,112},{1,113},{2,114},{3,115},{4,116},{5,117},{6,118},{7,119},{8... | collective-permute-start | bytes 84488 | tf_op jit(solution)/shard_map/ppermute | solution.py:199
  76.9 0.0 copy-done
  76.9 0.9 shard_map.81.mix
  77.8 0.9 shard_map.80.y
  78.7 0.0 collective-permute-done.13.i0
  78.8 0.0 collective-permute-done.14.i1
  78.8 0.0 collective-permute-done.15.i2
  78.8 0.0 collective-permute-done.16.i3
  78.8 1.5 %shard_map.83 = f32[440,256]{1,0:T(8,128)S(1)} custom-call(f32[440,256]{1,0:T(8,128)S(1)} %shard_map.80.y, bf16[320,256]{1,0:T(8,128)(2,1)S(1)} %get-tuple-element.34.adj, f32[8,256]{1,0:T(8,128)S(1)} %get-tuple-element.36.rows, f32[440,440]{1,0:T(8,128)S(1)} %shard_map.81.mix, f32[16,440]{1,0:T(8,128)S(1)} %collective-permute-done.13.i0, ...), custom_call_target="tpu_custom_call" | custom-call | flops 100000000 | bytes 1000000 | tf_op jit(solution)/shard_map/pallas_call | solution.py:187
  80.3 5.7 %collective-permute-start.17 = (f32[440,256]{1,0:T(8,128)S(1)}, f32[440,256]{1,0:T(8,128)S(1)}, u32[]{:S(2)}, u32[]{:S(2)}) collective-permute-start(f32[440,256]{1,0:T(8,128)S(1)} %shard_map.83), channel_id=1, source_target_pairs={{0,0},{1,1},{2,2},{3,3},{4,4},{5,5},{6,6},{7,7},{8,64},{9,65},{10,... | collective-permute-start | bytes 1351688 | tf_op jit(solution)/shard_map/ppermute | solution.py:245
  86.1 12.8 %collective-permute-done.17 = f32[440,256]{1,0:T(8,128)S(1)} collective-permute-done((f32[440,256]{1,0:T(8,128)S(1)}, f32[440,256]{1,0:T(8,128)S(1)}, u32[]{:S(2)}, u32[]{:S(2)}) %collective-permute-start.17) | collective-permute-done | bytes 450592 | tf_op jit(solution)/shard_map/ppermute | solution.py:245
  98.8 0.8 copy.10
Async XLA Ops:
  0.0 9.6 %copy-start.1 = (f32[55,1,32]{0,2,1:T(8,128)S(1)}, f32[55,1,32]{0,2,1:T(8,128)}, u32[]{:S(2)}) copy-start(f32[55,1,32]{0,2,1:T(8,128)} %param.8) | copy-start | bytes 21124
  0.0 27.3 %collective-permute-start = (f32[440,256]{1,0:T(8,128)}, f32[440,256]{1,0:T(8,128)S(1)}, u32[]{:S(2)}, u32[]{:S(2)}) collective-permute-start(f32[440,256]{1,0:T(8,128)} %bitcast.15), channel_id=1, source_target_pairs={{0,0},{1,1},{2,2},{3,3},{4,4},{5,5},{6,6},{7,7},{8,64},{9,65},{10,... | collective-permute-start | bytes 1351688 | tf_op jit(solution)/shard_map/ppermute | solution.py:204
  9.6 0.7 copy-start.4
  10.3 0.7 copy-start.2
  11.0 0.7 copy-start.3
  12.4 14.9 %all-to-all-start = ((f32[16,24,128]{2,1,0:T(8,128)}), f32[16,24,128]{2,1,0:T(8,128)S(1)}, u32[]{:S(2)}, u32[]{:S(2)}) async-start(f32[16,24,128]{2,1,0:T(8,128)} %shard_map.73), calls=%async_computation | async-start | bytes 393216 | tf_op jit(solution)/shard_map/all_to_all | solution.py:220
  28.3 15.0 %collective-permute-start.1 = (f32[16,440]{1,0:T(8,128)S(1)}, f32[16,440]{1,0:T(8,128)S(1)}, u32[]{:S(2)}, u32[]{:S(2)}) collective-permute-start(f32[16,440]{1,0:T(8,128)S(1)} %get-tuple-element.38), channel_id=1, source_target_pairs={{0,1},{1,2},{2,3},{3,4},{4,5},{5,6},{6,7},{7,64},{8,9},{9,10},{10,... | collective-permute-start | bytes 84488 | tf_op jit(solution)/shard_map/ppermute | solution.py:199
  31.2 12.1 %collective-permute-start.2 = (f32[16,440]{1,0:T(8,128)S(1)}, f32[16,440]{1,0:T(8,128)S(1)}, u32[]{:S(2)}, u32[]{:S(2)}) collective-permute-start(f32[16,440]{1,0:T(8,128)S(1)} %get-tuple-element.39), channel_id=1, source_target_pairs={{0,64},{1,65},{2,66},{3,67},{4,68},{5,69},{6,70},{7,71},{8,72},{9,... | collective-permute-start | bytes 84488 | tf_op jit(solution)/shard_map/ppermute | solution.py:199
  32.4 10.8 %collective-permute-start.3 = (f32[16,440]{1,0:T(8,128)S(1)}, f32[16,440]{1,0:T(8,128)S(1)}, u32[]{:S(2)}, u32[]{:S(2)}) collective-permute-start(f32[16,440]{1,0:T(8,128)S(1)} %get-tuple-element.40), channel_id=1, source_target_pairs={{0,119},{1,0},{2,1},{3,2},{4,3},{5,4},{6,5},{7,6},{8,127},{9,8},{1... | collective-permute-start | bytes 84488 | tf_op jit(solution)/shard_map/ppermute | solution.py:199
  40.1 3.7 %collective-permute-start.4 = (f32[16,440]{1,0:T(8,128)S(1)}, f32[16,440]{1,0:T(8,128)S(1)}, u32[]{:S(2)}, u32[]{:S(2)}) collective-permute-start(f32[16,440]{1,0:T(8,128)S(1)} %get-tuple-element.41), channel_id=1, source_target_pairs={{0,112},{1,113},{2,114},{3,115},{4,116},{5,117},{6,118},{7,119},{8... | collective-permute-start | bytes 84488 | tf_op jit(solution)/shard_map/ppermute | solution.py:199
  44.0 10.9 %collective-permute-start.5 = (f32[16,440]{1,0:T(8,128)S(1)}, f32[16,440]{1,0:T(8,128)S(1)}, u32[]{:S(2)}, u32[]{:S(2)}) collective-permute-start(f32[16,440]{1,0:T(8,128)S(1)} %get-tuple-element.46), channel_id=1, source_target_pairs={{0,1},{1,2},{2,3},{3,4},{4,5},{5,6},{6,7},{7,64},{8,9},{9,10},{10,... | collective-permute-start | bytes 84488 | tf_op jit(solution)/shard_map/ppermute | solution.py:199
  45.9 9.0 %collective-permute-start.6 = (f32[16,440]{1,0:T(8,128)S(1)}, f32[16,440]{1,0:T(8,128)S(1)}, u32[]{:S(2)}, u32[]{:S(2)}) collective-permute-start(f32[16,440]{1,0:T(8,128)S(1)} %get-tuple-element.47), channel_id=1, source_target_pairs={{0,64},{1,65},{2,66},{3,67},{4,68},{5,69},{6,70},{7,71},{8,72},{9,... | collective-permute-start | bytes 84488 | tf_op jit(solution)/shard_map/ppermute | solution.py:199
  46.0 9.0 %collective-permute-start.7 = (f32[16,440]{1,0:T(8,128)S(1)}, f32[16,440]{1,0:T(8,128)S(1)}, u32[]{:S(2)}, u32[]{:S(2)}) collective-permute-start(f32[16,440]{1,0:T(8,128)S(1)} %get-tuple-element.48), channel_id=1, source_target_pairs={{0,119},{1,0},{2,1},{3,2},{4,3},{5,4},{6,5},{7,6},{8,127},{9,8},{1... | collective-permute-start | bytes 84488 | tf_op jit(solution)/shard_map/ppermute | solution.py:199
  50.8 4.3 %collective-permute-start.8 = (f32[16,440]{1,0:T(8,128)S(1)}, f32[16,440]{1,0:T(8,128)S(1)}, u32[]{:S(2)}, u32[]{:S(2)}) collective-permute-start(f32[16,440]{1,0:T(8,128)S(1)} %get-tuple-element.49), channel_id=1, source_target_pairs={{0,112},{1,113},{2,114},{3,115},{4,116},{5,117},{6,118},{7,119},{8... | collective-permute-start | bytes 84488 | tf_op jit(solution)/shard_map/ppermute | solution.py:199
  55.3 11.2 %collective-permute-start.9 = (f32[16,440]{1,0:T(8,128)S(1)}, f32[16,440]{1,0:T(8,128)S(1)}, u32[]{:S(2)}, u32[]{:S(2)}) collective-permute-start(f32[16,440]{1,0:T(8,128)S(1)} %get-tuple-element.52), channel_id=1, source_target_pairs={{0,1},{1,2},{2,3},{3,4},{4,5},{5,6},{6,7},{7,64},{8,9},{9,10},{10,... | collective-permute-start | bytes 84488 | tf_op jit(solution)/shard_map/ppermute | solution.py:199
  57.2 9.3 %collective-permute-start.10 = (f32[16,440]{1,0:T(8,128)S(1)}, f32[16,440]{1,0:T(8,128)S(1)}, u32[]{:S(2)}, u32[]{:S(2)}) collective-permute-start(f32[16,440]{1,0:T(8,128)S(1)} %get-tuple-element.53), channel_id=1, source_target_pairs={{0,64},{1,65},{2,66},{3,67},{4,68},{5,69},{6,70},{7,71},{8,72},{9,... | collective-permute-start | bytes 84488 | tf_op jit(solution)/shard_map/ppermute | solution.py:199
  57.2 9.3 %collective-permute-start.11 = (f32[16,440]{1,0:T(8,128)S(1)}, f32[16,440]{1,0:T(8,128)S(1)}, u32[]{:S(2)}, u32[]{:S(2)}) collective-permute-start(f32[16,440]{1,0:T(8,128)S(1)} %get-tuple-element.54), channel_id=1, source_target_pairs={{0,119},{1,0},{2,1},{3,2},{4,3},{5,4},{6,5},{7,6},{8,127},{9,8},{1... | collective-permute-start | bytes 84488 | tf_op jit(solution)/shard_map/ppermute | solution.py:199
  62.1 4.4 %collective-permute-start.12 = (f32[16,440]{1,0:T(8,128)S(1)}, f32[16,440]{1,0:T(8,128)S(1)}, u32[]{:S(2)}, u32[]{:S(2)}) collective-permute-start(f32[16,440]{1,0:T(8,128)S(1)} %get-tuple-element.55), channel_id=1, source_target_pairs={{0,112},{1,113},{2,114},{3,115},{4,116},{5,117},{6,118},{7,119},{8... | collective-permute-start | bytes 84488 | tf_op jit(solution)/shard_map/ppermute | solution.py:199
  66.5 10.4 %copy-start = (f32[55,55]{1,0:T(8,128)S(1)}, f32[55,55]{1,0:T(8,128)}, u32[]{:S(2)}) copy-start(f32[55,55]{1,0:T(8,128)} %vloc.1) | copy-start | bytes 36304
  66.8 12.0 %collective-permute-start.13 = (f32[16,440]{1,0:T(8,128)S(1)}, f32[16,440]{1,0:T(8,128)S(1)}, u32[]{:S(2)}, u32[]{:S(2)}) collective-permute-start(f32[16,440]{1,0:T(8,128)S(1)} %get-tuple-element.57), channel_id=1, source_target_pairs={{0,1},{1,2},{2,3},{3,4},{4,5},{5,6},{6,7},{7,64},{8,9},{9,10},{10,... | collective-permute-start | bytes 84488 | tf_op jit(solution)/shard_map/ppermute | solution.py:199
  68.7 10.1 %collective-permute-start.14 = (f32[16,440]{1,0:T(8,128)S(1)}, f32[16,440]{1,0:T(8,128)S(1)}, u32[]{:S(2)}, u32[]{:S(2)}) collective-permute-start(f32[16,440]{1,0:T(8,128)S(1)} %get-tuple-element.58), channel_id=1, source_target_pairs={{0,64},{1,65},{2,66},{3,67},{4,68},{5,69},{6,70},{7,71},{8,72},{9,... | collective-permute-start | bytes 84488 | tf_op jit(solution)/shard_map/ppermute | solution.py:199
  68.7 10.1 %collective-permute-start.15 = (f32[16,440]{1,0:T(8,128)S(1)}, f32[16,440]{1,0:T(8,128)S(1)}, u32[]{:S(2)}, u32[]{:S(2)}) collective-permute-start(f32[16,440]{1,0:T(8,128)S(1)} %get-tuple-element.59), channel_id=1, source_target_pairs={{0,119},{1,0},{2,1},{3,2},{4,3},{5,4},{6,5},{7,6},{8,127},{9,8},{1... | collective-permute-start | bytes 84488 | tf_op jit(solution)/shard_map/ppermute | solution.py:199
  73.6 5.2 %collective-permute-start.16 = (f32[16,440]{1,0:T(8,128)S(1)}, f32[16,440]{1,0:T(8,128)S(1)}, u32[]{:S(2)}, u32[]{:S(2)}) collective-permute-start(f32[16,440]{1,0:T(8,128)S(1)} %get-tuple-element.60), channel_id=1, source_target_pairs={{0,112},{1,113},{2,114},{3,115},{4,116},{5,117},{6,118},{7,119},{8... | collective-permute-start | bytes 84488 | tf_op jit(solution)/shard_map/ppermute | solution.py:199
  80.3 18.5 %collective-permute-start.17 = (f32[440,256]{1,0:T(8,128)S(1)}, f32[440,256]{1,0:T(8,128)S(1)}, u32[]{:S(2)}, u32[]{:S(2)}) collective-permute-start(f32[440,256]{1,0:T(8,128)S(1)} %shard_map.83), channel_id=1, source_target_pairs={{0,0},{1,1},{2,2},{3,3},{4,4},{5,5},{6,6},{7,7},{8,64},{9,65},{10,... | collective-permute-start | bytes 1351688 | tf_op jit(solution)/shard_map/ppermute | solution.py:245

commit v3 on v2

v3 whole, which is shorter than its diff:
```python
import itertools

import jax
import jax.numpy as jnp
from jax import lax
from jax.experimental import pallas as pl
from jax.experimental.pallas import tpu as pltpu
from jax.sharding import Mesh
from jax.sharding import PartitionSpec as P

STEPS = 4
AXES = ("member", "x", "yh", "z")
LEV = 55
MEM = 8
FIELDS = LEV * MEM
CELLS = 256
RIM = 16
GHOSTS = 4 * RIM
NULL = CELLS + GHOSTS
F32 = jnp.float32
BF16 = jnp.bfloat16


def flat(x, yh, l, z, core):
    return (l * 2 + core) * 64 + (x % 4) * 16 + yh * 8 + z % 8


def pairs(move):
    every = itertools.product(range(4), range(2), range(4), range(8), range(2))
    return sorted((flat(*c), flat(*move(*c))) for c in every)


def next_column(x, yh, l, z, core):
    if z < 7:
        return x, yh, l, z + 1, core
    return x + core, yh, l, 0, 1 - core


def near(x, yh, l, z, core):
    y = (l + 2 + 4 * core) % 8
    return x, y // 4, y % 4, z, yh


GO = pairs(near)
BACK = sorted((b, a) for a, b in GO)
EAST = pairs(next_column)
WEST = sorted((b, a) for a, b in EAST)
SOUTH = pairs(lambda x, yh, l, z, core: (x + core, yh, l, z, 1 - core))
NORTH = sorted((b, a) for a, b in SOUTH)
ROUTES = (EAST, SOUTH, WEST, NORTH)
ORDER = (0, 2, 1, 3)
HOME = dict(BACK)


def homeward(route):
    return [(a, HOME[b]) for a, b in route]


def split(value, count):
    parts = []
    for _ in range(count):
        parts.append(value.astype(BF16))
        value = value - parts[-1].astype(F32)
    return parts


def exact_dot(left, right, dims, count=2):
    split_left = left.dtype == F32
    total = None
    for part in reversed(split(left if split_left else right, count)):
        a, b = (part, right) if split_left else (left, part)
        term = lax.dot_general(a, b, (dims, ((), ())), preferred_element_type=F32)
        total = term if total is None else total + term
    return total


def chosen(sends):
    column = jnp.broadcast_to(sends, (128, 128)).T[0:GHOSTS].astype(jnp.int32)
    slots = lax.broadcasted_iota(jnp.int32, (GHOSTS, CELLS), 1)
    return (jnp.concatenate([column, column], axis=1) == slots).astype(F32).astype(BF16)


def named_cells(table, adj, rows, kappa):
    ids = lax.broadcasted_iota(jnp.int32, (NULL, CELLS), 0)
    total = jnp.zeros((NULL, CELLS), F32)
    degree = jnp.zeros((1, CELLS), F32)
    for j in range(6):
        named = table[j : j + 1, :].astype(jnp.int32)
        total = total + (ids == named).astype(F32)
        degree = degree + (named < NULL).astype(F32)
    adj[...] = total.astype(BF16)
    rows[...] = jnp.concatenate(
        [kappa, 1.0 - degree * kappa, jnp.zeros((6, CELLS), F32)], axis=0
    )


def pack_kernel(member, grad_in, kappa_in, named_in, sends_in, slots, table, *scratch):
    *held, done = scratch
    copies = [
        pltpu.make_async_copy(here, there, done.at[i])
        for i, (here, there) in enumerate(zip((grad_in, kappa_in, named_in, sends_in), held))
    ]
    for copy in copies:
        copy.start()
    for copy in copies:
        copy.wait()
    grad, kappa, named, sends = held
    table[0:6, :] = named[...].astype(F32)
    table[6:7, :] = kappa[...]
    row = [sends[d : d + 1, :].astype(F32) for d in range(4)]
    row.append(jnp.zeros((1, CELLS - GHOSTS), F32))
    table[7:8, :] = jnp.concatenate(row, axis=1)
    row = table[pl.ds(member[0], 1), :]
    row = jnp.concatenate([row[:, i * 16 : (i + 1) * 16] for i in range(16)], axis=0)
    end = jnp.zeros((RIM, 1), F32)
    slots[0] = jnp.concatenate(
        [grad[0:RIM, :], row[:, 0:8], end, grad[RIM:, :], row[:, 8:16], end], axis=1
    )
    for s in range(1, 16):
        slots[s] = slots[0]


def gathered(core, slots):
    cells = []
    for m in range(MEM):
        two = slots[core[0] * MEM + m]
        cells += [two, pltpu.roll(two, 64, 1)]
    return jnp.concatenate(cells, axis=0)


def table_rows(cells, count):
    size = count * 32
    r = lax.broadcasted_iota(jnp.int32, (size, CELLS), 0)
    c = lax.broadcasted_iota(jnp.int32, (size, CELLS), 1)
    wide = jnp.concatenate([cells[:, LEV : LEV + 8]] * 32, axis=1)
    wide = jnp.where((c // 16 == r % 16) & (c // 8 % 2 == r // 16 % 2), wide, 0.0)
    row = lax.broadcasted_iota(jnp.int32, (16, size), 0)
    cell = lax.broadcasted_iota(jnp.int32, (16, size), 1)
    pick = (row == cell // 32).astype(F32).astype(BF16)
    return exact_dot(pick, wide, ((1,), (0,)), 3)[0:8]


def rims_out(rims, outs):
    for d, out in zip(ORDER, outs):
        out[...] = rims[d * RIM : (d + 1) * RIM]


def joined(arrived):
    return jnp.concatenate([arrived[d][...] for d in ORDER], axis=0)


def first_kernel(core, slots, fields, r0, r1, r2, r3, x, cells_out, table_out):
    cells = gathered(core, slots)
    cells_out[...] = cells
    grad = cells.T
    table = table_rows(cells[192:], 2)
    table_out[...] = table
    for l in range(LEV):
        x[l * MEM : (l + 1) * MEM, :] = fields[l * MEM : (l + 1) * MEM, :] * grad[l : l + 1]
    sel = chosen(table[1:2, :128])
    rims_out(exact_dot(sel, table[0:1, :] * x[...], ((1,), (1,))), (r0, r1, r2, r3))


def stay(x, adj, rows):
    kappa = rows[0:1, :]
    return x * rows[1:2, :] + exact_dot(kappa * x, adj[0:CELLS, :], ((1,), (0,)))


def stay_out(x, adj, sel, rows, y_out, b_out):
    y = stay(x, adj, rows)
    y_out[...] = y
    b_out[...] = exact_dot(sel[...], rows[0:1, :] * y, ((1,), (1,)))


def first_stay_kernel(x, cells, table, y_out, b_out, adj, sel, rows, gsel, ksel):
    named_cells(table_rows(cells[0:192, :], 6), adj, rows, table[0:1, :])
    sel[...] = chosen(table[1:2, :128])
    stay_out(x[...], adj, sel, rows, y_out, b_out)
    gsel[...] = lax.dot_general(
        sel[...], adj[CELLS:, :], (((1,), (1,)), ((), ())), preferred_element_type=F32
    ).astype(BF16)
    kappa = jnp.broadcast_to(table[0:1, :], (128, CELLS))
    ksel[...] = exact_dot(sel[...], kappa, ((1,), (1,)), 3)


def last_rim_kernel(b, gsel, ksel, i3, i0, i1, i2, *outs):
    rim_kernel(b, gsel, ksel, i0, i1, i2, i3, *outs)


def rim_kernel(b, gsel, ksel, i0, i1, i2, i3, r0, r1, r2, r3, came_out):
    came = joined((i0, i1, i2, i3))
    came_out[...] = came
    rims = b[...] + ksel[:, 0:1] * exact_dot(gsel[...], came, ((1,), (0,)), 3)
    rims_out(rims, (r0, r1, r2, r3))


def arrive(y, ghosts, came):
    return y[...] + exact_dot(came.T, ghosts, ((1,), (0,)))


def stay_kernel(y, adj, sel, rows, came, y_out, b_out):
    x = arrive(y, adj[CELLS:, :], came[...])
    stay_out(x, adj, sel, rows, y_out, b_out)


def dot_split(left, right):
    total = jnp.dot(left[1], right[0], preferred_element_type=F32)
    total = total + jnp.dot(left[0], right[1], preferred_element_type=F32)
    return total + jnp.dot(left[0], right[0], preferred_element_type=F32)


def last_stay_kernel(y, adj, rows, mix_high, mix_low, came, out):
    x = arrive(y, adj[CELLS:, :], came[...])
    out[...] = dot_split((mix_high[...], mix_low[...]), split(stay(x, adj, rows), 2))


def mixed_sides(first, second, ghosts, back_high, back_low):
    came = jnp.concatenate([first[...], second[...]], axis=0)
    rims = dot_split(split(came, 2), (back_high[...], back_low[...]))
    return exact_dot(rims.T, ghosts, ((1,), (0,)))


def near_sides_kernel(y, adj, back_high, back_low, south, north, out):
    ghosts = adj[CELLS + 2 * RIM :, :]
    out[...] = y[...] + mixed_sides(south, north, ghosts, back_high, back_low)


def home_sides_kernel(ghosts, back_high, back_low, east, west, out):
    out[...] = mixed_sides(east, west, ghosts[...], back_high, back_low)


def home_kernel(vloc, named, mix_high, mix_low, back_high, back_low, ghosts):
    level = lax.broadcasted_iota(jnp.int32, (FIELDS, 128), 0) // MEM
    spread = level == lax.broadcasted_iota(jnp.int32, (FIELDS, 128), 1)
    spread = spread.astype(F32).astype(BF16)[:, 0:LEV]
    row = lax.broadcasted_iota(jnp.int32, (FIELDS, FIELDS), 0) % MEM
    column = lax.broadcasted_iota(jnp.int32, (FIELDS, FIELDS), 1) % MEM
    for square, outs in ((vloc[...].T, (mix_high, mix_low)), (vloc[...], (back_high, back_low))):
        wide = exact_dot(spread, square, ((1,), (0,)), 3)
        full = exact_dot(wide, spread, ((1,), (1,)), 3)
        for out, part in zip(outs, split(jnp.where(row == column, full, 0.0), 2)):
            out[...] = part
    ids = lax.broadcasted_iota(jnp.int32, (2 * RIM, CELLS), 0) + CELLS
    total = jnp.zeros((2 * RIM, CELLS), F32)
    for j in range(6):
        total = total + (ids == named[j : j + 1, :]).astype(F32)
    ghosts[...] = total.astype(BF16)


def last_kernel(count, y, sides, out):
    alive = lax.broadcasted_iota(jnp.int32, (1, CELLS), 1) < count[0]
    out[...] = jnp.where(alive, y[...] + sides[...], 0.0)


VM = pl.BlockSpec(memory_space=pltpu.VMEM)
SM = pl.BlockSpec(memory_space=pltpu.SMEM)


def call(kernel, shapes, args, scalars=0, flops=10**8, scratch=(), rest=VM):
    specs = [SM] * scalars + [rest] * (len(args) - scalars)
    return pl.pallas_call(
        kernel,
        out_shape=[jax.ShapeDtypeStruct(s, t) for s, t in shapes],
        in_specs=specs,
        out_specs=[VM] * len(shapes),
        scratch_shapes=list(scratch),
        cost_estimate=pl.CostEstimate(flops=flops, bytes_accessed=10**6, transcendentals=0),
        compiler_params=pltpu.CompilerParams(vmem_limit_bytes=32 * 1024 * 1024),
    )(*args)


def exchange(rims):
    return [lax.ppermute(rim, AXES, route) for rim, route in zip(rims, ROUTES)]


def local(perturbations, gradient, kappa, vloc, neighbors, send_lists, counts):
    fields = perturbations.transpose(1, 0, 2).reshape(FIELDS, CELLS)
    state = ((FIELDS, CELLS), F32)
    border = ((GHOSTS, FIELDS), F32)
    rim_shapes = [((RIM, FIELDS), F32)] * 4
    member = lax.axis_index("member")
    (slots,) = call(
        pack_kernel,
        [((16, RIM, 128), F32)],
        (
            member.reshape(1),
            gradient.reshape(LEV, 32).T,
            kappa.reshape(1, CELLS),
            neighbors,
            send_lists,
        ),
        scalars=1,
        scratch=[
            pltpu.VMEM((8, CELLS), F32),
            pltpu.VMEM((32, LEV), F32),
            pltpu.VMEM((1, CELLS), F32),
            pltpu.VMEM((6, CELLS), jnp.int32),
            pltpu.VMEM((4, RIM), jnp.int32),
            pltpu.SemaphoreType.DMA((4,)),
        ],
        rest=pl.BlockSpec(memory_space=pltpu.HBM),
    )
    slots, fields = lax.optimization_barrier((slots, fields))
    fields = lax.ppermute(fields, AXES, GO)
    slots = lax.all_to_all(slots, ("yh", "member"), 0, 0)
    *rims, x, cells, table = call(
        first_kernel,
        rim_shapes + [state, ((CELLS, 128), F32), ((8, CELLS), F32)],
        ((member % 2).reshape(1), slots, fields),
        scalars=1,
    )
    came = exchange(rims)
    y, b, adj, sel, rows, gsel, ksel = call(
        first_stay_kernel,
        [
            state,
            border,
            ((NULL, CELLS), BF16),
            ((GHOSTS, CELLS), BF16),
            ((8, CELLS), F32),
            ((GHOSTS, GHOSTS), BF16),
            ((GHOSTS, 128), F32),
        ],
        (x, cells, table),
    )
    square = ((FIELDS, FIELDS), BF16)
    mix_high, mix_low, back_high, back_low, ghosts = call(
        home_kernel, [square] * 4 + [((2 * RIM, CELLS), BF16)], (vloc, neighbors)
    )
    for step in range(1, STEPS - 1):
        *rims, came = call(rim_kernel, rim_shapes + [border], (b, gsel, ksel, *came))
        y, b = call(stay_kernel, [state, border], (y, adj, sel, rows, came))
        came = exchange(rims)
    east, south, west, north, came = call(
        last_rim_kernel, rim_shapes + [border], (b, gsel, ksel, came[3], *came[:3])
    )
    (y,) = call(last_stay_kernel, [state], (y, adj, rows, mix_high, mix_low, came))
    south = lax.ppermute(south, AXES, SOUTH)
    north = lax.ppermute(north, AXES, NORTH)
    (y,) = call(near_sides_kernel, [state], (y, adj, back_high, back_low, south, north))
    y, east, west = lax.optimization_barrier((y, east, west))
    y = lax.ppermute(y, AXES, BACK)
    east = lax.ppermute(east, AXES, homeward(EAST))
    west = lax.ppermute(west, AXES, homeward(WEST))
    (sides,) = call(home_sides_kernel, [state], (ghosts, back_high, back_low, east, west))
    (out,) = call(last_kernel, [state], (counts, y, sides), scalars=1)
    return out.reshape(LEV, MEM, CELLS).transpose(1, 0, 2)


def solution(mesh):
    parts = Mesh(mesh.devices.reshape(8, 4, 2, 8), AXES)
    patch = ("x", "yh", "z")
    return jax.shard_map(
        local,
        mesh=parts,
        in_specs=(
            P("member", None, patch),
            P(None, patch, "member"),
            P(patch),
            P(),
            P(None, patch),
            P(None, patch),
            P(patch),
        ),
        out_specs=P("member", None, patch),
        check_vma=False,
    )
```

time: 100 us -> 90.5 us (0.905)
  waiting for transfers between devices: 24.9 us -> 14.7 us
  local copies, waits for them, and re-layouts: 2.81 us -> 1.43 us
  Pallas kernels: 8.8 us -> 9.93 us
    ppermute x18, waiting for transfers between devices: 13.5 us -> 5.19 us  [the longest x1 2.74 us: local(): east = lax.ppermute(east, AXES, homeward(EAST))]
    all_to_all x1, starting transfers between devices: 3.42 us -> 5.46 us  [local(): slots = lax.all_to_all(slots, ('yh', 'member'), 0, 0)]
    all_to_all x1, waiting for transfers between devices: 11.4 us -> 9.51 us  [local(): slots = lax.all_to_all(slots, ('yh', 'member'), 0, 0)]
    unnamed x11 -> x10, local copies, waits for them, and re-layouts: 2.81 us -> 1.43 us
    ppermute x18, starting transfers between devices: 58.7 us -> 57.4 us  [the longest x12 34.1 us: exchange(): return [lax.ppermute(rim, AXES, route) for rim, route in zip(rims, ROUTES)]]
    pallas_call x11 -> x13, Pallas kernels: 8.8 us -> 9.93 us  [call(): pl.pallas_call(kernel, out_shape=[jax.ShapeDtypeStruct(s, t) for s, t in...]
  transfers between devices with their start and end apart: 19 -> 19, of which waited for: 4 -> 5; matrix products, arithmetic and copies ran while one was open for 0% -> 0% of each run, Pallas kernels for 6% -> 7%
where the time goes in v3:
time: 90.5 us; the launch traced here: 89.9 us
  starting transfers between devices  62.9 us (70%)
  waiting for transfers between devices  14.7 us (16%)
  Pallas kernels  9.93 us (11%)
  local copies, waits for them, and re-layouts  1.43 us (2%)
  between operations  0.96 us (1%)
    ppermute x12, starting transfers between devices, exchange(): return [lax.ppermute(rim, AXES, route) for rim, route in zip(rims, ROUTES)]  34.1 us
    pallas_call x13, Pallas kernels, call(): pl.pallas_call(kernel, out_shape=[jax.ShapeDtypeStruct(s, t) for s, t in...  9.93 us
    all_to_all x1, waiting for transfers between devices, local(): slots = lax.all_to_all(slots, ('yh', 'member'), 0, 0)  9.51 us
    ppermute x1, starting transfers between devices, local(): fields = lax.ppermute(fields, AXES, GO)  7.27 us
    ppermute x1, starting transfers between devices, local(): y = lax.ppermute(y, AXES, BACK)  6.51 us
    ppermute x1, starting transfers between devices, local(): west = lax.ppermute(west, AXES, homeward(WEST))  6.09 us
    all_to_all x1, starting transfers between devices, local(): slots = lax.all_to_all(slots, ('yh', 'member'), 0, 0)  5.46 us
    ppermute x1, waiting for transfers between devices, local(): east = lax.ppermute(east, AXES, homeward(EAST))  2.74 us
  transfers between devices with their start and end apart: 19, of which 5 were waited for; matrix products, arithmetic and copies ran while one was open for 0% of the time, Pallas kernels for 7%

profile of v3, /device:TPU:1, one launch (start us, length us, event | category | flops | bytes accessed | tf_op | source)
XLA Modules:
  0.0 89.9 jit_solution(11295590817009293044)
XLA Ops:
  0.0 0.0 copy-start.2
  0.0 0.0 copy-start.3
  0.0 0.0 copy-start.4
  0.0 0.7 copy-done.2
  0.7 0.0 copy-done.3
  0.7 0.0 copy-done.4
  0.7 0.0 copy-start.1
  0.7 0.7 copy-done.1
  1.4 0.9 %shard_map.73 = f32[16,16,128]{2,1,0:T(8,128)} custom-call(s32[1]{0:T(128)} %bitcast.1.member, f32[32,55]{1,0:T(8,128)S(1)} %bitcast.12, f32[1,256]{1,0:T(1,128)S(1)} %bitcast.13, s32[6,256]{1,0:T(8,128)S(1)} %copy-done.2, s32[4,16]{1,0:T(4,128)S(1)} %copy-done.3), custom_call_target="tpu_custom_call" | custom-call | flops 100000000 | bytes 1000000 | tf_op jit(solution)/shard_map/pallas_call | solution.py:261
  2.4 7.3 %collective-permute-start = (f32[440,256]{1,0:T(8,128)}, f32[440,256]{1,0:T(8,128)S(1)}, u32[]{:S(2)}, u32[]{:S(2)}) collective-permute-start(f32[440,256]{1,0:T(8,128)} %bitcast.14), channel_id=1, source_target_pairs={{0,256},{1,257},{2,258},{3,259},{4,260},{5,261},{6,262},{7,263},{8... | collective-permute-start | bytes 1351688 | tf_op jit(solution)/shard_map/ppermute | solution.py:304
  9.7 5.5 %all-to-all-start = ((f32[16,16,128]{2,1,0:T(8,128)}), f32[16,16,128]{2,1,0:T(8,128)S(1)}, u32[]{:S(2)}, u32[]{:S(2)}) async-start(f32[16,16,128]{2,1,0:T(8,128)} %shard_map.73), calls=%async_computation | async-start | bytes 262144 | tf_op jit(solution)/shard_map/all_to_all | solution.py:305
  15.1 9.5 %all-to-all-done.slots = f32[16,16,128]{2,1,0:T(8,128)S(1)} async-done(((f32[16,16,128]{2,1,0:T(8,128)}), f32[16,16,128]{2,1,0:T(8,128)S(1)}, u32[]{:S(2)}, u32[]{:S(2)}) %all-to-all-start) | async-done | bytes 131104 | tf_op jit(solution)/shard_map/all_to_all | solution.py:305
  24.6 0.0 collective-permute-done.fields
  24.6 0.7 shard_map.74
  25.3 3.3 %collective-permute-start.1 = (f32[16,440]{1,0:T(8,128)S(1)}, f32[16,440]{1,0:T(8,128)S(1)}, u32[]{:S(2)}, u32[]{:S(2)}) collective-permute-start(f32[16,440]{1,0:T(8,128)S(1)} %get-tuple-element.60), channel_id=1, source_target_pairs={{0,1},{1,2},{2,3},{3,4},{4,5},{5,6},{6,7},{7,64},{8,9},{9,10},{10,... | collective-permute-start | bytes 84488 | tf_op jit(solution)/shard_map/ppermute | solution.py:273
  28.6 1.4 %collective-permute-start.2 = (f32[16,440]{1,0:T(8,128)S(1)}, f32[16,440]{1,0:T(8,128)S(1)}, u32[]{:S(2)}, u32[]{:S(2)}) collective-permute-start(f32[16,440]{1,0:T(8,128)S(1)} %get-tuple-element.61), channel_id=1, source_target_pairs={{0,64},{1,65},{2,66},{3,67},{4,68},{5,69},{6,70},{7,71},{8,72},{9,... | collective-permute-start | bytes 84488 | tf_op jit(solution)/shard_map/ppermute | solution.py:273
  30.0 7.6 %collective-permute-start.3 = (f32[16,440]{1,0:T(8,128)S(1)}, f32[16,440]{1,0:T(8,128)S(1)}, u32[]{:S(2)}, u32[]{:S(2)}) collective-permute-start(f32[16,440]{1,0:T(8,128)S(1)} %get-tuple-element.62), channel_id=1, source_target_pairs={{0,119},{1,0},{2,1},{3,2},{4,3},{5,4},{6,5},{7,6},{8,127},{9,8},{1... | collective-permute-start | bytes 84488 | tf_op jit(solution)/shard_map/ppermute | solution.py:273
  37.6 2.3 %collective-permute-start.4 = (f32[16,440]{1,0:T(8,128)S(1)}, f32[16,440]{1,0:T(8,128)S(1)}, u32[]{:S(2)}, u32[]{:S(2)}) collective-permute-start(f32[16,440]{1,0:T(8,128)S(1)} %get-tuple-element.63), channel_id=1, source_target_pairs={{0,112},{1,113},{2,114},{3,115},{4,116},{5,117},{6,118},{7,119},{8... | collective-permute-start | bytes 84488 | tf_op jit(solution)/shard_map/ppermute | solution.py:273
  39.9 1.5 %shard_map.75 = (f32[440,256]{1,0:T(8,128)S(1)}, f32[64,440]{1,0:T(8,128)S(1)}, bf16[320,256]{1,0:T(8,128)(2,1)S(1)}, bf16[64,256]{1,0:T(8,128)(2,1)S(1)}, f32[8...) custom-call(f32[440,256]{1,0:T(8,128)S(1)} %get-tuple-element.50.x, ...), custom_call_target="tpu_custom_call" | custom-call | flops 100000000 | bytes 1000000 | tf_op jit(solution)/shard_map/pallas_call | solution.py:261
  41.4 0.0 collective-permute-done.1.i0
  41.4 0.0 collective-permute-done.2.i1
  41.4 0.0 collective-permute-done.3.i2
  41.4 0.0 collective-permute-done.4.i3
  41.4 0.2 shard_map.76
  41.6 1.9 %collective-permute-start.5 = (f32[16,440]{1,0:T(8,128)S(1)}, f32[16,440]{1,0:T(8,128)S(1)}, u32[]{:S(2)}, u32[]{:S(2)}) collective-permute-start(f32[16,440]{1,0:T(8,128)S(1)} %get-tuple-element.67), channel_id=1, source_target_pairs={{0,1},{1,2},{2,3},{3,4},{4,5},{5,6},{6,7},{7,64},{8,9},{9,10},{10,... | collective-permute-start | bytes 84488 | tf_op jit(solution)/shard_map/ppermute | solution.py:273
  43.6 0.0 collective-permute-start.6
  43.6 4.9 %collective-permute-start.7 = (f32[16,440]{1,0:T(8,128)S(1)}, f32[16,440]{1,0:T(8,128)S(1)}, u32[]{:S(2)}, u32[]{:S(2)}) collective-permute-start(f32[16,440]{1,0:T(8,128)S(1)} %get-tuple-element.69), channel_id=1, source_target_pairs={{0,119},{1,0},{2,1},{3,2},{4,3},{5,4},{6,5},{7,6},{8,127},{9,8},{1... | collective-permute-start | bytes 84488 | tf_op jit(solution)/shard_map/ppermute | solution.py:273
  48.4 2.8 %collective-permute-start.8 = (f32[16,440]{1,0:T(8,128)S(1)}, f32[16,440]{1,0:T(8,128)S(1)}, u32[]{:S(2)}, u32[]{:S(2)}) collective-permute-start(f32[16,440]{1,0:T(8,128)S(1)} %get-tuple-element.70), channel_id=1, source_target_pairs={{0,112},{1,113},{2,114},{3,115},{4,116},{5,117},{6,118},{7,119},{8... | collective-permute-start | bytes 84488 | tf_op jit(solution)/shard_map/ppermute | solution.py:273
  51.2 0.8 shard_map.77
  52.1 0.0 collective-permute-done.5.i0
  52.1 0.0 collective-permute-done.6.i1
  52.1 0.0 collective-permute-done.7.i2
  52.1 0.5 collective-permute-done.8.i3
  52.7 0.2 shard_map.78
  52.9 1.9 %collective-permute-start.10 = (f32[16,440]{1,0:T(8,128)S(1)}, f32[16,440]{1,0:T(8,128)S(1)}, u32[]{:S(2)}, u32[]{:S(2)}) collective-permute-start(f32[16,440]{1,0:T(8,128)S(1)} %get-tuple-element.77), channel_id=1, source_target_pairs={{0,1},{1,2},{2,3},{3,4},{4,5},{5,6},{6,7},{7,64},{8,9},{9,10},{10,... | collective-permute-start | bytes 84488 | tf_op jit(solution)/shard_map/ppermute | solution.py:273
  54.8 0.0 collective-permute-start.11
  54.8 4.9 %collective-permute-start.12 = (f32[16,440]{1,0:T(8,128)S(1)}, f32[16,440]{1,0:T(8,128)S(1)}, u32[]{:S(2)}, u32[]{:S(2)}) collective-permute-start(f32[16,440]{1,0:T(8,128)S(1)} %get-tuple-element.79), channel_id=1, source_target_pairs={{0,119},{1,0},{2,1},{3,2},{4,3},{5,4},{6,5},{7,6},{8,127},{9,8},{1... | collective-permute-start | bytes 84488 | tf_op jit(solution)/shard_map/ppermute | solution.py:273
  59.7 3.1 %collective-permute-start.9 = (f32[16,440]{1,0:T(8,128)S(1)}, f32[16,440]{1,0:T(8,128)S(1)}, u32[]{:S(2)}, u32[]{:S(2)}) collective-permute-start(f32[16,440]{1,0:T(8,128)S(1)} %get-tuple-element.76), channel_id=1, source_target_pairs={{0,112},{1,113},{2,114},{3,115},{4,116},{5,117},{6,118},{7,119},{8... | collective-permute-start | bytes 84488 | tf_op jit(solution)/shard_map/ppermute | solution.py:273
  62.8 0.8 shard_map.79
  63.6 0.0 collective-permute-done.10.i0
  63.7 0.0 collective-permute-done.11.i1
  63.7 0.0 collective-permute-done.12.i2
  63.7 0.0 collective-permute-done.9.i3
  63.7 0.0 copy-start
  63.7 0.2 shard_map.81
  63.9 0.0 collective-permute-start.13
  63.9 1.5 %collective-permute-start.14 = (f32[16,440]{1,0:T(8,128)S(1)}, f32[16,440]{1,0:T(8,128)S(1)}, u32[]{:S(2)}, u32[]{:S(2)}) collective-permute-start(f32[16,440]{1,0:T(8,128)S(1)} %get-tuple-element.84), channel_id=1, source_target_pairs={{0,112},{1,113},{2,114},{3,115},{4,116},{5,117},{6,118},{7,119},{8... | collective-permute-start | bytes 84488 | tf_op jit(solution)/shard_map/ppermute | solution.py:339
  65.5 0.0 copy-done
  65.5 1.3 %shard_map.80 = (bf16[440,440]{1,0:T(8,128)(2,1)S(1)}, bf16[440,440]{1,0:T(8,128)(2,1)S(1)}, bf16[440,440]{1,0:T(8,128)(2,1)S(1)}, bf16[440,440]{1,0:T(8,128)(2,1)S(1)}, bf16[32,256]{1,0:T(8,128)(2,1)S(1)}) custom-call(f32[55,55]{1,0:T(8,128)S(1)} %copy-done, s32[6,256]{1,0:T(8,128)S(1)} %copy-done.2), custom_call_target="tpu_custom_call" | custom-call | flops 100000000 | bytes 1000000 | tf_op jit(solution)/shard_map/pallas_call | solution.py:261
  66.8 1.1 %shard_map.82.y = f32[440,256]{1,0:T(8,128)S(1)} custom-call(f32[440,256]{1,0:T(8,128)S(1)} %get-tuple-element.72.y, bf16[320,256]{1,0:T(8,128)(2,1)S(1)} %get-tuple-element.54.adj, f32[8,256]{1,0:T(8,128)S(1)} %get-tuple-element.56.rows, bf16[440,440]{1,0:T(8,128)(2,1)S(1)} %get-tuple-element.73.mix_high, bf16[440,440]{1,0:T(8,128)(2,1)S(1)} %get-tuple-element.74.mix_low, ...), custom_call_target="tpu_custom_call" | custom-call | flops 100000000 | bytes 1000000 | tf_op jit(solution)/shard_map/pallas_call | solution.py:261
  67.9 0.0 collective-permute-done.13.south
  67.9 0.0 collective-permute-done.14.north
  67.9 0.7 shard_map.83
  68.6 6.5 %collective-permute-start.15 = (f32[440,256]{1,0:T(8,128)S(1)}, f32[440,256]{1,0:T(8,128)S(1)}, u32[]{:S(2)}, u32[]{:S(2)}) collective-permute-start(f32[440,256]{1,0:T(8,128)S(1)} %shard_map.83), channel_id=1, source_target_pairs={{0,320},{1,321},{2,322},{3,323},{4,324},{5,325},{6,326},{7,327},{8... | collective-permute-start | bytes 1351688 | tf_op jit(solution)/shard_map/ppermute | solution.py:342
  75.1 1.9 %collective-permute-start.16 = (f32[16,440]{1,0:T(8,128)S(1)}, f32[16,440]{1,0:T(8,128)S(1)}, u32[]{:S(2)}, u32[]{:S(2)}) collective-permute-start(f32[16,440]{1,0:T(8,128)S(1)} %get-tuple-element.89), channel_id=1, source_target_pairs={{0,321},{1,322},{2,323},{3,324},{4,325},{5,326},{6,327},{7,328},{8... | collective-permute-start | bytes 84488 | tf_op jit(solution)/shard_map/ppermute | solution.py:343
  77.1 6.1 %collective-permute-start.17 = (f32[16,440]{1,0:T(8,128)S(1)}, f32[16,440]{1,0:T(8,128)S(1)}, u32[]{:S(2)}, u32[]{:S(2)}) collective-permute-start(f32[16,440]{1,0:T(8,128)S(1)} %get-tuple-element.90), channel_id=1, source_target_pairs={{0,383},{1,320},{2,321},{3,322},{4,323},{5,324},{6,325},{7,326},{8... | collective-permute-start | bytes 84488 | tf_op jit(solution)/shard_map/ppermute | solution.py:344
  83.8 2.7 %collective-permute-done.16.east = f32[16,440]{1,0:T(8,128)S(1)} collective-permute-done((f32[16,440]{1,0:T(8,128)S(1)}, f32[16,440]{1,0:T(8,128)S(1)}, u32[]{:S(2)}, u32[]{:S(2)}) %collective-permute-start.16) | collective-permute-done | bytes 28192 | tf_op jit(solution)/shard_map/ppermute | solution.py:343
  86.5 1.5 %collective-permute-done.17.west = f32[16,440]{1,0:T(8,128)S(1)} collective-permute-done((f32[16,440]{1,0:T(8,128)S(1)}, f32[16,440]{1,0:T(8,128)S(1)}, u32[]{:S(2)}, u32[]{:S(2)}) %collective-permute-start.17) | collective-permute-done | bytes 28192 | tf_op jit(solution)/shard_map/ppermute | solution.py:344
  88.0 0.7 shard_map.84.sides
  88.7 0.4 collective-permute-done.15.y
  89.1 0.8 shard_map.85
Async XLA Ops:
  0.0 0.7 copy-start.2
  0.0 0.7 copy-start.3
  0.0 0.7 copy-start.4
  0.7 0.7 copy-start.1
  2.4 22.3 %collective-permute-start = (f32[440,256]{1,0:T(8,128)}, f32[440,256]{1,0:T(8,128)S(1)}, u32[]{:S(2)}, u32[]{:S(2)}) collective-permute-start(f32[440,256]{1,0:T(8,128)} %bitcast.14), channel_id=1, source_target_pairs={{0,256},{1,257},{2,258},{3,259},{4,260},{5,261},{6,262},{7,263},{8... | collective-permute-start | bytes 1351688 | tf_op jit(solution)/shard_map/ppermute | solution.py:304
  9.7 15.0 %all-to-all-start = ((f32[16,16,128]{2,1,0:T(8,128)}), f32[16,16,128]{2,1,0:T(8,128)S(1)}, u32[]{:S(2)}, u32[]{:S(2)}) async-start(f32[16,16,128]{2,1,0:T(8,128)} %shard_map.73), calls=%async_computation | async-start | bytes 262144 | tf_op jit(solution)/shard_map/all_to_all | solution.py:305
  25.3 16.1 %collective-permute-start.1 = (f32[16,440]{1,0:T(8,128)S(1)}, f32[16,440]{1,0:T(8,128)S(1)}, u32[]{:S(2)}, u32[]{:S(2)}) collective-permute-start(f32[16,440]{1,0:T(8,128)S(1)} %get-tuple-element.60), channel_id=1, source_target_pairs={{0,1},{1,2},{2,3},{3,4},{4,5},{5,6},{6,7},{7,64},{8,9},{9,10},{10,... | collective-permute-start | bytes 84488 | tf_op jit(solution)/shard_map/ppermute | solution.py:273
  28.6 12.8 %collective-permute-start.2 = (f32[16,440]{1,0:T(8,128)S(1)}, f32[16,440]{1,0:T(8,128)S(1)}, u32[]{:S(2)}, u32[]{:S(2)}) collective-permute-start(f32[16,440]{1,0:T(8,128)S(1)} %get-tuple-element.61), channel_id=1, source_target_pairs={{0,64},{1,65},{2,66},{3,67},{4,68},{5,69},{6,70},{7,71},{8,72},{9,... | collective-permute-start | bytes 84488 | tf_op jit(solution)/shard_map/ppermute | solution.py:273
  30.0 11.4 %collective-permute-start.3 = (f32[16,440]{1,0:T(8,128)S(1)}, f32[16,440]{1,0:T(8,128)S(1)}, u32[]{:S(2)}, u32[]{:S(2)}) collective-permute-start(f32[16,440]{1,0:T(8,128)S(1)} %get-tuple-element.62), channel_id=1, source_target_pairs={{0,119},{1,0},{2,1},{3,2},{4,3},{5,4},{6,5},{7,6},{8,127},{9,8},{1... | collective-permute-start | bytes 84488 | tf_op jit(solution)/shard_map/ppermute | solution.py:273
  37.6 3.8 %collective-permute-start.4 = (f32[16,440]{1,0:T(8,128)S(1)}, f32[16,440]{1,0:T(8,128)S(1)}, u32[]{:S(2)}, u32[]{:S(2)}) collective-permute-start(f32[16,440]{1,0:T(8,128)S(1)} %get-tuple-element.63), channel_id=1, source_target_pairs={{0,112},{1,113},{2,114},{3,115},{4,116},{5,117},{6,118},{7,119},{8... | collective-permute-start | bytes 84488 | tf_op jit(solution)/shard_map/ppermute | solution.py:273
  41.6 10.4 %collective-permute-start.5 = (f32[16,440]{1,0:T(8,128)S(1)}, f32[16,440]{1,0:T(8,128)S(1)}, u32[]{:S(2)}, u32[]{:S(2)}) collective-permute-start(f32[16,440]{1,0:T(8,128)S(1)} %get-tuple-element.67), channel_id=1, source_target_pairs={{0,1},{1,2},{2,3},{3,4},{4,5},{5,6},{6,7},{7,64},{8,9},{9,10},{10,... | collective-permute-start | bytes 84488 | tf_op jit(solution)/shard_map/ppermute | solution.py:273
  43.6 8.5 %collective-permute-start.6 = (f32[16,440]{1,0:T(8,128)S(1)}, f32[16,440]{1,0:T(8,128)S(1)}, u32[]{:S(2)}, u32[]{:S(2)}) collective-permute-start(f32[16,440]{1,0:T(8,128)S(1)} %get-tuple-element.68), channel_id=1, source_target_pairs={{0,64},{1,65},{2,66},{3,67},{4,68},{5,69},{6,70},{7,71},{8,72},{9,... | collective-permute-start | bytes 84488 | tf_op jit(solution)/shard_map/ppermute | solution.py:273
  43.6 8.5 %collective-permute-start.7 = (f32[16,440]{1,0:T(8,128)S(1)}, f32[16,440]{1,0:T(8,128)S(1)}, u32[]{:S(2)}, u32[]{:S(2)}) collective-permute-start(f32[16,440]{1,0:T(8,128)S(1)} %get-tuple-element.69), channel_id=1, source_target_pairs={{0,119},{1,0},{2,1},{3,2},{4,3},{5,4},{6,5},{7,6},{8,127},{9,8},{1... | collective-permute-start | bytes 84488 | tf_op jit(solution)/shard_map/ppermute | solution.py:273
  48.4 4.2 %collective-permute-start.8 = (f32[16,440]{1,0:T(8,128)S(1)}, f32[16,440]{1,0:T(8,128)S(1)}, u32[]{:S(2)}, u32[]{:S(2)}) collective-permute-start(f32[16,440]{1,0:T(8,128)S(1)} %get-tuple-element.70), channel_id=1, source_target_pairs={{0,112},{1,113},{2,114},{3,115},{4,116},{5,117},{6,118},{7,119},{8... | collective-permute-start | bytes 84488 | tf_op jit(solution)/shard_map/ppermute | solution.py:273
  52.9 10.8 %collective-permute-start.10 = (f32[16,440]{1,0:T(8,128)S(1)}, f32[16,440]{1,0:T(8,128)S(1)}, u32[]{:S(2)}, u32[]{:S(2)}) collective-permute-start(f32[16,440]{1,0:T(8,128)S(1)} %get-tuple-element.77), channel_id=1, source_target_pairs={{0,1},{1,2},{2,3},{3,4},{4,5},{5,6},{6,7},{7,64},{8,9},{9,10},{10,... | collective-permute-start | bytes 84488 | tf_op jit(solution)/shard_map/ppermute | solution.py:273
  54.8 8.9 %collective-permute-start.11 = (f32[16,440]{1,0:T(8,128)S(1)}, f32[16,440]{1,0:T(8,128)S(1)}, u32[]{:S(2)}, u32[]{:S(2)}) collective-permute-start(f32[16,440]{1,0:T(8,128)S(1)} %get-tuple-element.78), channel_id=1, source_target_pairs={{0,64},{1,65},{2,66},{3,67},{4,68},{5,69},{6,70},{7,71},{8,72},{9,... | collective-permute-start | bytes 84488 | tf_op jit(solution)/shard_map/ppermute | solution.py:273
  54.8 8.9 %collective-permute-start.12 = (f32[16,440]{1,0:T(8,128)S(1)}, f32[16,440]{1,0:T(8,128)S(1)}, u32[]{:S(2)}, u32[]{:S(2)}) collective-permute-start(f32[16,440]{1,0:T(8,128)S(1)} %get-tuple-element.79), channel_id=1, source_target_pairs={{0,119},{1,0},{2,1},{3,2},{4,3},{5,4},{6,5},{7,6},{8,127},{9,8},{1... | collective-permute-start | bytes 84488 | tf_op jit(solution)/shard_map/ppermute | solution.py:273
  59.7 4.0 %collective-permute-start.9 = (f32[16,440]{1,0:T(8,128)S(1)}, f32[16,440]{1,0:T(8,128)S(1)}, u32[]{:S(2)}, u32[]{:S(2)}) collective-permute-start(f32[16,440]{1,0:T(8,128)S(1)} %get-tuple-element.76), channel_id=1, source_target_pairs={{0,112},{1,113},{2,114},{3,115},{4,116},{5,117},{6,118},{7,119},{8... | collective-permute-start | bytes 84488 | tf_op jit(solution)/shard_map/ppermute | solution.py:273
  63.7 1.8 %copy-start = (f32[55,55]{1,0:T(8,128)S(1)}, f32[55,55]{1,0:T(8,128)}, u32[]{:S(2)}) copy-start(f32[55,55]{1,0:T(8,128)} %vloc.1) | copy-start | bytes 36304
  63.9 4.0 %collective-permute-start.13 = (f32[16,440]{1,0:T(8,128)S(1)}, f32[16,440]{1,0:T(8,128)S(1)}, u32[]{:S(2)}, u32[]{:S(2)}) collective-permute-start(f32[16,440]{1,0:T(8,128)S(1)} %get-tuple-element.83), channel_id=1, source_target_pairs={{0,64},{1,65},{2,66},{3,67},{4,68},{5,69},{6,70},{7,71},{8,72},{9,... | collective-permute-start | bytes 84488 | tf_op jit(solution)/shard_map/ppermute | solution.py:338
  63.9 4.0 %collective-permute-start.14 = (f32[16,440]{1,0:T(8,128)S(1)}, f32[16,440]{1,0:T(8,128)S(1)}, u32[]{:S(2)}, u32[]{:S(2)}) collective-permute-start(f32[16,440]{1,0:T(8,128)S(1)} %get-tuple-element.84), channel_id=1, source_target_pairs={{0,112},{1,113},{2,114},{3,115},{4,116},{5,117},{6,118},{7,119},{8... | collective-permute-start | bytes 84488 | tf_op jit(solution)/shard_map/ppermute | solution.py:339
  68.6 20.5 %collective-permute-start.15 = (f32[440,256]{1,0:T(8,128)S(1)}, f32[440,256]{1,0:T(8,128)S(1)}, u32[]{:S(2)}, u32[]{:S(2)}) collective-permute-start(f32[440,256]{1,0:T(8,128)S(1)} %shard_map.83), channel_id=1, source_target_pairs={{0,320},{1,321},{2,322},{3,323},{4,324},{5,325},{6,326},{7,327},{8... | collective-permute-start | bytes 1351688 | tf_op jit(solution)/shard_map/ppermute | solution.py:342
  75.1 11.4 %collective-permute-start.16 = (f32[16,440]{1,0:T(8,128)S(1)}, f32[16,440]{1,0:T(8,128)S(1)}, u32[]{:S(2)}, u32[]{:S(2)}) collective-permute-start(f32[16,440]{1,0:T(8,128)S(1)} %get-tuple-element.89), channel_id=1, source_target_pairs={{0,321},{1,322},{2,323},{3,324},{4,325},{5,326},{6,327},{7,328},{8... | collective-permute-start | bytes 84488 | tf_op jit(solution)/shard_map/ppermute | solution.py:343
  77.1 11.0 %collective-permute-start.17 = (f32[16,440]{1,0:T(8,128)S(1)}, f32[16,440]{1,0:T(8,128)S(1)}, u32[]{:S(2)}, u32[]{:S(2)}) collective-permute-start(f32[16,440]{1,0:T(8,128)S(1)} %get-tuple-element.90), channel_id=1, source_target_pairs={{0,383},{1,320},{2,321},{3,322},{4,323},{5,324},{6,325},{7,326},{8... | collective-permute-start | bytes 84488 | tf_op jit(solution)/shard_map/ppermute | solution.py:344

commit v4 on v3

--- a/solution.py
+++ b/solution.py
@@ -94,30 +94,39 @@
     )
 
 
-def pack_kernel(member, grad_in, kappa_in, named_in, sends_in, slots, table, *scratch):
+def pack_kernel(grad_in, fields_in, kappa_in, named_in, sends_in, slots, out, *scratch):
     *held, done = scratch
+    given = (grad_in, fields_in, kappa_in, named_in, sends_in)
     copies = [
         pltpu.make_async_copy(here, there, done.at[i])
-        for i, (here, there) in enumerate(zip((grad_in, kappa_in, named_in, sends_in), held))
+        for i, (here, there) in enumerate(zip(given, held))
     ]
     for copy in copies:
         copy.start()
     for copy in copies:
         copy.wait()
-    grad, kappa, named, sends = held
-    table[0:6, :] = named[...].astype(F32)
-    table[6:7, :] = kappa[...]
+    grad, fields, kappa, named, sends = held
+    piece = jnp.concatenate([grad[...], jnp.zeros((32, 64 - LEV), F32)], axis=1)
+    slots[0] = jnp.concatenate([piece[0:RIM], piece[RIM:]], axis=1)
+    for s in range(1, 16):
+        slots[s] = slots[0]
     row = [sends[d : d + 1, :].astype(F32) for d in range(4)]
     row.append(jnp.zeros((1, CELLS - GHOSTS), F32))
-    table[7:8, :] = jnp.concatenate(row, axis=1)
-    row = table[pl.ds(member[0], 1), :]
-    row = jnp.concatenate([row[:, i * 16 : (i + 1) * 16] for i in range(16)], axis=0)
-    end = jnp.zeros((RIM, 1), F32)
-    slots[0] = jnp.concatenate(
-        [grad[0:RIM, :], row[:, 0:8], end, grad[RIM:, :], row[:, 8:16], end], axis=1
-    )
-    for s in range(1, 16):
-        slots[s] = slots[0]
+    row = jnp.concatenate(row, axis=1)
+    out[0:GHOSTS, :] = exact_dot(chosen(row[:, :128]), fields[...], ((1,), (1,)), 3)
+    out[GHOSTS:, 0:CELLS] = jnp.concatenate([named[...].astype(F32), kappa[...], row], axis=0)
+    out[GHOSTS:, CELLS:] = jnp.zeros((8, FIELDS - CELLS), F32)
+
+
+def near_kernel(load, adj, sel, rows, gsel, ksel):
+    table = load[GHOSTS:, 0:CELLS]
+    named_cells(table, adj, rows, table[6:7, :])
+    sel[...] = chosen(table[7:8, :128])
+    gsel[...] = lax.dot_general(
+        sel[...], adj[CELLS:, :], (((1,), (1,)), ((), ())), preferred_element_type=F32
+    ).astype(BF16)
+    kappa = jnp.broadcast_to(table[6:7, :], (128, CELLS))
+    ksel[...] = exact_dot(sel[...], kappa, ((1,), (1,)), 3)
 
 
 def gathered(core, slots):
@@ -128,18 +137,6 @@
     return jnp.concatenate(cells, axis=0)
 
 
-def table_rows(cells, count):
-    size = count * 32
-    r = lax.broadcasted_iota(jnp.int32, (size, CELLS), 0)
-    c = lax.broadcasted_iota(jnp.int32, (size, CELLS), 1)
-    wide = jnp.concatenate([cells[:, LEV : LEV + 8]] * 32, axis=1)
-    wide = jnp.where((c // 16 == r % 16) & (c // 8 % 2 == r // 16 % 2), wide, 0.0)
-    row = lax.broadcasted_iota(jnp.int32, (16, size), 0)
-    cell = lax.broadcasted_iota(jnp.int32, (16, size), 1)
-    pick = (row == cell // 32).astype(F32).astype(BF16)
-    return exact_dot(pick, wide, ((1,), (0,)), 3)[0:8]
-
-
 def rims_out(rims, outs):
     for d, out in zip(ORDER, outs):
         out[...] = rims[d * RIM : (d + 1) * RIM]
@@ -149,16 +146,17 @@
     return jnp.concatenate([arrived[d][...] for d in ORDER], axis=0)
 
 
-def first_kernel(core, slots, fields, r0, r1, r2, r3, x, cells_out, table_out):
-    cells = gathered(core, slots)
-    cells_out[...] = cells
-    grad = cells.T
-    table = table_rows(cells[192:], 2)
-    table_out[...] = table
-    for l in range(LEV):
-        x[l * MEM : (l + 1) * MEM, :] = fields[l * MEM : (l + 1) * MEM, :] * grad[l : l + 1]
-    sel = chosen(table[1:2, :128])
-    rims_out(exact_dot(sel, table[0:1, :] * x[...], ((1,), (1,))), (r0, r1, r2, r3))
+def spread():
+    level = lax.broadcasted_iota(jnp.int32, (FIELDS, 128), 0) // MEM
+    return (level == lax.broadcasted_iota(jnp.int32, (FIELDS, 128), 1)).astype(F32).astype(BF16)
+
+
+def first_kernel(core, slots, load, sel, ksel, r0, r1, r2, r3):
+    grad = exact_dot(sel[...], gathered(core, slots), ((1,), (0,)), 3)
+    lane = lax.broadcasted_iota(jnp.int32, (GHOSTS, 128), 1)
+    grad = jnp.where(lane < LEV, grad, 0.0) * ksel[...]
+    grad = exact_dot(grad, spread(), ((1,), (1,)), 3)
+    rims_out(load[0:GHOSTS, :] * grad, (r0, r1, r2, r3))
 
 
 def stay(x, adj, rows):
@@ -172,19 +170,11 @@
     b_out[...] = exact_dot(sel[...], rows[0:1, :] * y, ((1,), (1,)))
 
 
-def first_stay_kernel(x, cells, table, y_out, b_out, adj, sel, rows, gsel, ksel):
-    named_cells(table_rows(cells[0:192, :], 6), adj, rows, table[0:1, :])
-    sel[...] = chosen(table[1:2, :128])
+def first_stay_kernel(core, slots, fields, adj, sel, rows, y_out, b_out, x):
+    grad = gathered(core, slots).T
+    for l in range(LEV):
+        x[l * MEM : (l + 1) * MEM, :] = fields[l * MEM : (l + 1) * MEM, :] * grad[l : l + 1]
     stay_out(x[...], adj, sel, rows, y_out, b_out)
-    gsel[...] = lax.dot_general(
-        sel[...], adj[CELLS:, :], (((1,), (1,)), ((), ())), preferred_element_type=F32
-    ).astype(BF16)
-    kappa = jnp.broadcast_to(table[0:1, :], (128, CELLS))
-    ksel[...] = exact_dot(sel[...], kappa, ((1,), (1,)), 3)
-
-
-def last_rim_kernel(b, gsel, ksel, i3, i0, i1, i2, *outs):
-    rim_kernel(b, gsel, ksel, i0, i1, i2, i3, *outs)
 
 
 def rim_kernel(b, gsel, ksel, i0, i1, i2, i3, r0, r1, r2, r3, came_out):
@@ -214,19 +204,20 @@
     out[...] = dot_split((mix_high[...], mix_low[...]), split(stay(x, adj, rows), 2))
 
 
-def mixed_sides(first, second, ghosts, back_high, back_low):
+def mixed_rims(first, second, back_high, back_low):
     came = jnp.concatenate([first[...], second[...]], axis=0)
-    rims = dot_split(split(came, 2), (back_high[...], back_low[...]))
-    return exact_dot(rims.T, ghosts, ((1,), (0,)))
+    return dot_split(split(came, 2), (back_high[...], back_low[...]))
 
 
 def near_sides_kernel(y, adj, back_high, back_low, south, north, out):
-    ghosts = adj[CELLS + 2 * RIM :, :]
-    out[...] = y[...] + mixed_sides(south, north, ghosts, back_high, back_low)
-
-
-def home_sides_kernel(ghosts, back_high, back_low, east, west, out):
-    out[...] = mixed_sides(east, west, ghosts[...], back_high, back_low)
+    rims = mixed_rims(south, north, back_high, back_low)
+    out[...] = arrive(y, adj[CELLS + 2 * RIM :, :], rims)
+
+
+def mix_sides_kernel(back_high, back_low, east, west, east_out, west_out):
+    rims = mixed_rims(east, west, back_high, back_low)
+    east_out[...] = rims[0:RIM]
+    west_out[...] = rims[RIM:]
 
 
 def home_kernel(vloc, named, mix_high, mix_low, back_high, back_low, ghosts):
@@ -247,16 +238,17 @@
     ghosts[...] = total.astype(BF16)
 
 
-def last_kernel(count, y, sides, out):
+def last_kernel(count, y, ghosts, east, west, out):
     alive = lax.broadcasted_iota(jnp.int32, (1, CELLS), 1) < count[0]
-    out[...] = jnp.where(alive, y[...] + sides[...], 0.0)
+    rims = jnp.concatenate([east[...], west[...]], axis=0)
+    out[...] = jnp.where(alive, arrive(y, ghosts[...], rims), 0.0)
 
 
 VM = pl.BlockSpec(memory_space=pltpu.VMEM)
 SM = pl.BlockSpec(memory_space=pltpu.SMEM)
 
 
-def call(kernel, shapes, args, scalars=0, flops=10**8, scratch=(), rest=VM):
+def call(kernel, shapes, args, scalars=0, flops=10**8, scratch=(), rest=VM, vmem=32):
     specs = [SM] * scalars + [rest] * (len(args) - scalars)
     return pl.pallas_call(
         kernel,
@@ -265,7 +257,7 @@
         out_specs=[VM] * len(shapes),
         scratch_shapes=list(scratch),
         cost_estimate=pl.CostEstimate(flops=flops, bytes_accessed=10**6, transcendentals=0),
-        compiler_params=pltpu.CompilerParams(vmem_limit_bytes=32 * 1024 * 1024),
+        compiler_params=pltpu.CompilerParams(vmem_limit_bytes=vmem * 1024 * 1024),
     )(*args)
 
 
@@ -278,72 +270,78 @@
     state = ((FIELDS, CELLS), F32)
     border = ((GHOSTS, FIELDS), F32)
     rim_shapes = [((RIM, FIELDS), F32)] * 4
-    member = lax.axis_index("member")
-    (slots,) = call(
+    core = (lax.axis_index("member") % 2).reshape(1)
+    slots, load = call(
         pack_kernel,
-        [((16, RIM, 128), F32)],
+        [((16, RIM, 128), F32), ((GHOSTS + 8, FIELDS), F32)],
         (
-            member.reshape(1),
             gradient.reshape(LEV, 32).T,
+            fields,
             kappa.reshape(1, CELLS),
             neighbors,
             send_lists,
         ),
-        scalars=1,
         scratch=[
-            pltpu.VMEM((8, CELLS), F32),
             pltpu.VMEM((32, LEV), F32),
+            pltpu.VMEM((FIELDS, CELLS), F32),
             pltpu.VMEM((1, CELLS), F32),
             pltpu.VMEM((6, CELLS), jnp.int32),
             pltpu.VMEM((4, RIM), jnp.int32),
-            pltpu.SemaphoreType.DMA((4,)),
+            pltpu.SemaphoreType.DMA((5,)),
         ],
         rest=pl.BlockSpec(memory_space=pltpu.HBM),
-    )
-    slots, fields = lax.optimization_barrier((slots, fields))
-    fields = lax.ppermute(fields, AXES, GO)
+        vmem=60,
+    )
+    load = lax.ppermute(load, AXES, GO)
     slots = lax.all_to_all(slots, ("yh", "member"), 0, 0)
-    *rims, x, cells, table = call(
-        first_kernel,
-        rim_shapes + [state, ((CELLS, 128), F32), ((8, CELLS), F32)],
-        ((member % 2).reshape(1), slots, fields),
-        scalars=1,
-    )
-    came = exchange(rims)
-    y, b, adj, sel, rows, gsel, ksel = call(
-        first_stay_kernel,
+    square = ((FIELDS, FIELDS), BF16)
+    mix_high, mix_low, back_high, back_low, ghosts = call(
+        home_kernel, [square] * 4 + [((2 * RIM, CELLS), BF16)], (vloc, neighbors)
+    )
+    adj, sel, rows, gsel, ksel = call(
+        near_kernel,
         [
-            state,
-            border,
             ((NULL, CELLS), BF16),
             ((GHOSTS, CELLS), BF16),
             ((8, CELLS), F32),
             ((GHOSTS, GHOSTS), BF16),
             ((GHOSTS, 128), F32),
         ],
-        (x, cells, table),
-    )
-    square = ((FIELDS, FIELDS), BF16)
-    mix_high, mix_low, back_high, back_low, ghosts = call(
-        home_kernel, [square] * 4 + [((2 * RIM, CELLS), BF16)], (vloc, neighbors)
+        (load,),
+        flops=10**10,
+    )
+    gsel, fields = lax.optimization_barrier((gsel, fields))
+    fields = lax.ppermute(fields, AXES, GO)
+    rims = call(
+        first_kernel, rim_shapes, (core, slots, load, sel, ksel), scalars=1, flops=2*10**10
+    )
+    came = exchange(rims)
+    y, b = call(
+        first_stay_kernel,
+        [state, border],
+        (core, slots, fields, adj, sel, rows),
+        scalars=1,
+        scratch=[pltpu.VMEM((FIELDS, CELLS), F32)],
     )
     for step in range(1, STEPS - 1):
         *rims, came = call(rim_kernel, rim_shapes + [border], (b, gsel, ksel, *came))
         y, b = call(stay_kernel, [state, border], (y, adj, sel, rows, came))
         came = exchange(rims)
+        if step == 1:
+            came[0], ghosts = lax.optimization_barrier((came[0], ghosts))
     east, south, west, north, came = call(
-        last_rim_kernel, rim_shapes + [border], (b, gsel, ksel, came[3], *came[:3])
+        rim_kernel, rim_shapes + [border], (b, gsel, ksel, *came)
     )
     (y,) = call(last_stay_kernel, [state], (y, adj, rows, mix_high, mix_low, came))
     south = lax.ppermute(south, AXES, SOUTH)
     north = lax.ppermute(north, AXES, NORTH)
+    east, west = call(mix_sides_kernel, rim_shapes[:2], (back_high, back_low, east, west))
     (y,) = call(near_sides_kernel, [state], (y, adj, back_high, back_low, south, north))
     y, east, west = lax.optimization_barrier((y, east, west))
     y = lax.ppermute(y, AXES, BACK)
     east = lax.ppermute(east, AXES, homeward(EAST))
     west = lax.ppermute(west, AXES, homeward(WEST))
-    (sides,) = call(home_sides_kernel, [state], (ghosts, back_high, back_low, east, west))
-    (out,) = call(last_kernel, [state], (counts, y, sides), scalars=1)
+    (out,) = call(last_kernel, [state], (counts, y, ghosts, east, west), scalars=1)
     return out.reshape(LEV, MEM, CELLS).transpose(1, 0, 2)
 
 

time: 90.5 us -> 87 us (0.961)
  waiting for transfers between devices: 14.7 us -> 6.56 us
  starting transfers between devices: 62.9 us -> 66.9 us
  local copies, waits for them, and re-layouts: 1.43 us -> 0.45 us
    ppermute x0 -> x1, starting transfers between devices: none -> 7.27 us  [local(): load = lax.ppermute(load, AXES, GO)]
    all_to_all x1, waiting for transfers between devices: 9.51 us -> 2.51 us  [local(): slots = lax.all_to_all(slots, ('yh', 'member'), 0, 0)]
    ppermute x1, starting transfers between devices: 6.51 us -> 3.36 us  [local(): y = lax.ppermute(y, AXES, BACK)]
    ppermute x1, starting transfers between devices: 6.09 us -> 7.72 us  [local(): west = lax.ppermute(west, AXES, homeward(WEST))]
    ppermute x1, starting transfers between devices: 7.27 us -> 5.64 us  [local(): fields = lax.ppermute(fields, AXES, GO)]
    ppermute x1, waiting for transfers between devices: 1.47 us -> 0.01 us  [local(): west = lax.ppermute(west, AXES, homeward(WEST))]
    unnamed x10 -> x6, local copies, waits for them, and re-layouts: 1.43 us -> 0.45 us
    pallas_call x13 -> x14, Pallas kernels: 9.93 us -> 10.7 us  [call(): pl.pallas_call(kernel, out_shape=[jax.ShapeDtypeStruct(s, t) for s, t in...]
  transfers between devices with their start and end apart: 19 -> 20, of which waited for: 5 -> 5; matrix products, arithmetic and copies ran while one was open for 0% -> 0% of each run, Pallas kernels for 7% -> 7%
where the time goes in v4:
time: 87 us; the launch traced here: 85.6 us
  starting transfers between devices  66.9 us (77%)
  Pallas kernels  10.7 us (12%)
  waiting for transfers between devices  6.56 us (8%)
  between operations  0.97 us (1%)
    ppermute x12, starting transfers between devices, exchange(): return [lax.ppermute(rim, AXES, route) for rim, route in zip(rims, ROUTES)]  33.4 us
    pallas_call x14, Pallas kernels, call(): pl.pallas_call(kernel, out_shape=[jax.ShapeDtypeStruct(s, t) for s, t in...  10.7 us
    ppermute x1, starting transfers between devices, local(): west = lax.ppermute(west, AXES, homeward(WEST))  7.72 us
    ppermute x1, starting transfers between devices, local(): load = lax.ppermute(load, AXES, GO)  7.27 us
    ppermute x1, starting transfers between devices, local(): fields = lax.ppermute(fields, AXES, GO)  5.64 us
    all_to_all x1, starting transfers between devices, local(): slots = lax.all_to_all(slots, ('yh', 'member'), 0, 0)  5.46 us
    ppermute x1, starting transfers between devices, local(): y = lax.ppermute(y, AXES, BACK)  3.36 us
    ppermute x1, starting transfers between devices, local(): east = lax.ppermute(east, AXES, homeward(EAST))  2.65 us
  transfers between devices with their start and end apart: 20, of which 5 were waited for; matrix products, arithmetic and copies ran while one was open for 0% of the time, Pallas kernels for 7%

profile of v4, /device:TPU:1, one launch (start us, length us, event | category | flops | bytes accessed | tf_op | source)
XLA Modules:
  0.0 85.6 jit_solution(14423466917712594492)
XLA Ops:
  0.0 2.2 %shard_map.73 = (f32[16,16,128]{2,1,0:T(8,128)}, f32[72,440]{1,0:T(8,128)}) custom-call(f32[32,55]{1,0:T(8,128)} %bitcast.13, f32[440,256]{1,0:T(8,128)} %bitcast.11, f32[1,256]{1,0:T(1,128)} %bitcast.14, s32[6,256]{1,0:T(8,128)} %named.1, s32[4,16]{1,0:T(4,128)} %sends_in.1), custom_call_target="tpu_custom_call" | custom-call | flops 100000000 | bytes 1000000 | tf_op jit(solution)/shard_map/pallas_call | solution.py:253
  2.2 7.3 %collective-permute-start = (f32[72,440]{1,0:T(8,128)}, f32[72,440]{1,0:T(8,128)S(1)}, u32[]{:S(2)}, u32[]{:S(2)}) collective-permute-start(f32[72,440]{1,0:T(8,128)} %get-tuple-element.52), channel_id=1, source_target_pairs={{0,256},{1,257},{2,258},{3,259},{4,260},{5,261},{6,262},{7,263},{8... | collective-permute-start | bytes 380168 | tf_op jit(solution)/shard_map/ppermute | solution.py:295
  9.5 5.5 %all-to-all-start = ((f32[16,16,128]{2,1,0:T(8,128)}), f32[16,16,128]{2,1,0:T(8,128)S(1)}, u32[]{:S(2)}, u32[]{:S(2)}) async-start(f32[16,16,128]{2,1,0:T(8,128)} %get-tuple-element.51), calls=%async_computation | async-start | bytes 262144 | tf_op jit(solution)/shard_map/all_to_all | solution.py:296
  14.9 0.0 copy-start.2
  14.9 0.0 collective-permute-done.load
  14.9 0.6 shard_map.74
  15.5 0.4 copy-done.2
  15.9 5.6 %collective-permute-start.1 = (f32[440,256]{1,0:T(8,128)S(1)}, f32[440,256]{1,0:T(8,128)S(1)}, u32[]{:S(2)}, u32[]{:S(2)}) collective-permute-start(f32[440,256]{1,0:T(8,128)S(1)} %bitcast.12), channel_id=1, source_target_pairs={{0,256},{1,257},{2,258},{3,259},{4,260},{5,261},{6,262},{7,263},{8... | collective-permute-start | bytes 1351688 | tf_op jit(solution)/shard_map/ppermute | solution.py:314
  21.6 2.5 %all-to-all-done.slots = f32[16,16,128]{2,1,0:T(8,128)S(1)} async-done(((f32[16,16,128]{2,1,0:T(8,128)}), f32[16,16,128]{2,1,0:T(8,128)S(1)}, u32[]{:S(2)}, u32[]{:S(2)}) %all-to-all-start) | async-done | bytes 131104 | tf_op jit(solution)/shard_map/all_to_all | solution.py:296
  24.1 0.5 shard_map.76
  24.6 2.5 %collective-permute-start.2 = (f32[16,440]{1,0:T(8,128)S(1)}, f32[16,440]{1,0:T(8,128)S(1)}, u32[]{:S(2)}, u32[]{:S(2)}) collective-permute-start(f32[16,440]{1,0:T(8,128)S(1)} %get-tuple-element.62), channel_id=1, source_target_pairs={{0,1},{1,2},{2,3},{3,4},{4,5},{5,6},{6,7},{7,64},{8,9},{9,10},{10,... | collective-permute-start | bytes 84488 | tf_op jit(solution)/shard_map/ppermute | solution.py:265
  27.1 1.1 %collective-permute-start.3 = (f32[16,440]{1,0:T(8,128)S(1)}, f32[16,440]{1,0:T(8,128)S(1)}, u32[]{:S(2)}, u32[]{:S(2)}) collective-permute-start(f32[16,440]{1,0:T(8,128)S(1)} %get-tuple-element.63), channel_id=1, source_target_pairs={{0,64},{1,65},{2,66},{3,67},{4,68},{5,69},{6,70},{7,71},{8,72},{9,... | collective-permute-start | bytes 84488 | tf_op jit(solution)/shard_map/ppermute | solution.py:265
  28.1 7.9 %collective-permute-start.4 = (f32[16,440]{1,0:T(8,128)S(1)}, f32[16,440]{1,0:T(8,128)S(1)}, u32[]{:S(2)}, u32[]{:S(2)}) collective-permute-start(f32[16,440]{1,0:T(8,128)S(1)} %get-tuple-element.64), channel_id=1, source_target_pairs={{0,119},{1,0},{2,1},{3,2},{4,3},{5,4},{6,5},{7,6},{8,127},{9,8},{1... | collective-permute-start | bytes 84488 | tf_op jit(solution)/shard_map/ppermute | solution.py:265
  36.1 2.2 %collective-permute-start.5 = (f32[16,440]{1,0:T(8,128)S(1)}, f32[16,440]{1,0:T(8,128)S(1)}, u32[]{:S(2)}, u32[]{:S(2)}) collective-permute-start(f32[16,440]{1,0:T(8,128)S(1)} %get-tuple-element.65), channel_id=1, source_target_pairs={{0,112},{1,113},{2,114},{3,115},{4,116},{5,117},{6,118},{7,119},{8... | collective-permute-start | bytes 84488 | tf_op jit(solution)/shard_map/ppermute | solution.py:265
  38.3 0.0 collective-permute-done.1.fields
  38.3 0.7 shard_map.75
  39.1 0.0 collective-permute-done.2.i0
  39.1 0.0 collective-permute-done.3.i1
  39.1 0.0 collective-permute-done.4.i2
  39.1 0.4 collective-permute-done.5.i3
  39.5 0.0 copy-start
  39.5 0.0 copy-start.1
  39.5 0.2 shard_map.77
  39.7 1.9 %collective-permute-start.6 = (f32[16,440]{1,0:T(8,128)S(1)}, f32[16,440]{1,0:T(8,128)S(1)}, u32[]{:S(2)}, u32[]{:S(2)}) collective-permute-start(f32[16,440]{1,0:T(8,128)S(1)} %get-tuple-element.69), channel_id=1, source_target_pairs={{0,1},{1,2},{2,3},{3,4},{4,5},{5,6},{6,7},{7,64},{8,9},{9,10},{10,... | collective-permute-start | bytes 84488 | tf_op jit(solution)/shard_map/ppermute | solution.py:265
  41.7 0.0 collective-permute-start.7
  41.7 4.9 %collective-permute-start.8 = (f32[16,440]{1,0:T(8,128)S(1)}, f32[16,440]{1,0:T(8,128)S(1)}, u32[]{:S(2)}, u32[]{:S(2)}) collective-permute-start(f32[16,440]{1,0:T(8,128)S(1)} %get-tuple-element.73), channel_id=1, source_target_pairs={{0,119},{1,0},{2,1},{3,2},{4,3},{5,4},{6,5},{7,6},{8,127},{9,8},{1... | collective-permute-start | bytes 84488 | tf_op jit(solution)/shard_map/ppermute | solution.py:265
  46.5 3.2 %collective-permute-start.9 = (f32[16,440]{1,0:T(8,128)S(1)}, f32[16,440]{1,0:T(8,128)S(1)}, u32[]{:S(2)}, u32[]{:S(2)}) collective-permute-start(f32[16,440]{1,0:T(8,128)S(1)} %get-tuple-element.74), channel_id=1, source_target_pairs={{0,112},{1,113},{2,114},{3,115},{4,116},{5,117},{6,118},{7,119},{8... | collective-permute-start | bytes 84488 | tf_op jit(solution)/shard_map/ppermute | solution.py:265
  49.7 0.0 copy-done
  49.7 0.0 copy-done.1
  49.7 1.3 %shard_map.79 = (bf16[440,440]{1,0:T(8,128)(2,1)S(1)}, bf16[440,440]{1,0:T(8,128)(2,1)S(1)}, bf16[440,440]{1,0:T(8,128)(2,1)S(1)}, bf16[440,440]{1,0:T(8,128)(2,1)S(1)}, bf16[32,256]{1,0:T(8,128)(2,1)S(1)}) custom-call(f32[55,55]{1,0:T(8,128)S(1)} %copy-done.1, s32[6,256]{1,0:T(8,128)S(1)} %copy-done), custom_call_target="tpu_custom_call" | custom-call | flops 100000000 | bytes 1000000 | tf_op jit(solution)/shard_map/pallas_call | solution.py:253
  51.0 0.8 shard_map.78
  51.8 0.0 collective-permute-done.6.i0
  51.9 0.0 collective-permute-done.7.i1
  51.9 0.0 collective-permute-done.8.i2
  51.9 0.0 collective-permute-done.9.i3
  51.9 0.2 shard_map.80
  52.1 1.9 %collective-permute-start.10 = (f32[16,440]{1,0:T(8,128)S(1)}, f32[16,440]{1,0:T(8,128)S(1)}, u32[]{:S(2)}, u32[]{:S(2)}) collective-permute-start(f32[16,440]{1,0:T(8,128)S(1)} %get-tuple-element.80), channel_id=1, source_target_pairs={{0,1},{1,2},{2,3},{3,4},{4,5},{5,6},{6,7},{7,64},{8,9},{9,10},{10,... | collective-permute-start | bytes 84488 | tf_op jit(solution)/shard_map/ppermute | solution.py:265
  54.0 0.0 collective-permute-start.11
  54.0 4.9 %collective-permute-start.12 = (f32[16,440]{1,0:T(8,128)S(1)}, f32[16,440]{1,0:T(8,128)S(1)}, u32[]{:S(2)}, u32[]{:S(2)}) collective-permute-start(f32[16,440]{1,0:T(8,128)S(1)} %get-tuple-element.82), channel_id=1, source_target_pairs={{0,119},{1,0},{2,1},{3,2},{4,3},{5,4},{6,5},{7,6},{8,127},{9,8},{1... | collective-permute-start | bytes 84488 | tf_op jit(solution)/shard_map/ppermute | solution.py:265
  58.9 3.0 %collective-permute-start.13 = (f32[16,440]{1,0:T(8,128)S(1)}, f32[16,440]{1,0:T(8,128)S(1)}, u32[]{:S(2)}, u32[]{:S(2)}) collective-permute-start(f32[16,440]{1,0:T(8,128)S(1)} %get-tuple-element.83), channel_id=1, source_target_pairs={{0,112},{1,113},{2,114},{3,115},{4,116},{5,117},{6,118},{7,119},{8... | collective-permute-start | bytes 84488 | tf_op jit(solution)/shard_map/ppermute | solution.py:265
  61.9 0.8 shard_map.81
  62.7 0.0 collective-permute-done.10.i0
  62.7 0.0 collective-permute-done.11.i1
  62.7 0.0 collective-permute-done.12.i2
  62.8 0.0 collective-permute-done.13.i3
  62.8 0.2 shard_map.82
  63.0 0.0 collective-permute-start.14
  63.0 1.4 %collective-permute-start.15 = (f32[16,440]{1,0:T(8,128)S(1)}, f32[16,440]{1,0:T(8,128)S(1)}, u32[]{:S(2)}, u32[]{:S(2)}) collective-permute-start(f32[16,440]{1,0:T(8,128)S(1)} %get-tuple-element.88), channel_id=1, source_target_pairs={{0,112},{1,113},{2,114},{3,115},{4,116},{5,117},{6,118},{7,119},{8... | collective-permute-start | bytes 84488 | tf_op jit(solution)/shard_map/ppermute | solution.py:337
  64.4 0.3 shard_map.85
  64.7 1.1 %shard_map.83.y = f32[440,256]{1,0:T(8,128)S(1)} custom-call(f32[440,256]{1,0:T(8,128)S(1)} %get-tuple-element.76.y, bf16[320,256]{1,0:T(8,128)(2,1)S(1)} %get-tuple-element.55.adj, f32[8,256]{1,0:T(8,128)S(1)} %get-tuple-element.57.rows, bf16[440,440]{1,0:T(8,128)(2,1)S(1)} %get-tuple-element.77.mix_high, bf16[440,440]{1,0:T(8,128)(2,1)S(1)} %get-tuple-element.78.mix_low, ...), custom_call_target="tpu_custom_call" | custom-call | flops 100000000 | bytes 1000000 | tf_op jit(solution)/shard_map/pallas_call | solution.py:253
  65.8 0.0 collective-permute-done.14.south
  65.8 0.5 collective-permute-done.15.north
  66.3 0.7 shard_map.84
  67.0 3.4 %collective-permute-start.16 = (f32[440,256]{1,0:T(8,128)S(1)}, f32[440,256]{1,0:T(8,128)S(1)}, u32[]{:S(2)}, u32[]{:S(2)}) collective-permute-start(f32[440,256]{1,0:T(8,128)S(1)} %shard_map.84), channel_id=1, source_target_pairs={{0,320},{1,321},{2,322},{3,323},{4,324},{5,325},{6,326},{7,327},{8... | collective-permute-start | bytes 1351688 | tf_op jit(solution)/shard_map/ppermute | solution.py:341
  70.4 2.6 %collective-permute-start.17 = (f32[16,440]{1,0:T(8,128)S(1)}, f32[16,440]{1,0:T(8,128)S(1)}, u32[]{:S(2)}, u32[]{:S(2)}) collective-permute-start(f32[16,440]{1,0:T(8,128)S(1)} %get-tuple-element.95), channel_id=1, source_target_pairs={{0,321},{1,322},{2,323},{3,324},{4,325},{5,326},{6,327},{7,328},{8... | collective-permute-start | bytes 84488 | tf_op jit(solution)/shard_map/ppermute | solution.py:342
  73.0 7.7 %collective-permute-start.18 = (f32[16,440]{1,0:T(8,128)S(1)}, f32[16,440]{1,0:T(8,128)S(1)}, u32[]{:S(2)}, u32[]{:S(2)}) collective-permute-start(f32[16,440]{1,0:T(8,128)S(1)} %get-tuple-element.96), channel_id=1, source_target_pairs={{0,383},{1,320},{2,321},{3,322},{4,323},{5,324},{6,325},{7,326},{8... | collective-permute-start | bytes 84488 | tf_op jit(solution)/shard_map/ppermute | solution.py:343
  81.4 1.9 %collective-permute-done.17.east = f32[16,440]{1,0:T(8,128)S(1)} collective-permute-done((f32[16,440]{1,0:T(8,128)S(1)}, f32[16,440]{1,0:T(8,128)S(1)}, u32[]{:S(2)}, u32[]{:S(2)}) %collective-permute-start.17) | collective-permute-done | bytes 28192 | tf_op jit(solution)/shard_map/ppermute | solution.py:342
  83.3 0.0 collective-permute-done.18.west
  83.3 1.2 %collective-permute-done.16.y = f32[440,256]{1,0:T(8,128)S(1)} collective-permute-done((f32[440,256]{1,0:T(8,128)S(1)}, f32[440,256]{1,0:T(8,128)S(1)}, u32[]{:S(2)}, u32[]{:S(2)}) %collective-permute-start.16) | collective-permute-done | bytes 450592 | tf_op jit(solution)/shard_map/ppermute | solution.py:341
  84.5 1.1 %shard_map.86 = f32[440,256]{1,0:T(8,128)} custom-call(s32[1]{0:T(128)S(6)} %copy.8.count, f32[440,256]{1,0:T(8,128)S(1)} %collective-permute-done.16.y, bf16[32,256]{1,0:T(8,128)(2,1)S(1)} %get-tuple-element.94.ghosts, f32[16,440]{1,0:T(8,128)S(1)} %collective-permute-done.17.east, f32[16,440]{1,0:T(8,128)S(1)} %collective-permute-done.18.west), custom_call_target="tpu_custom_call" | custom-call | flops 100000000 | bytes 1000000 | tf_op jit(solution)/shard_map/pallas_call | solution.py:253
Async XLA Ops:
  2.2 12.7 %collective-permute-start = (f32[72,440]{1,0:T(8,128)}, f32[72,440]{1,0:T(8,128)S(1)}, u32[]{:S(2)}, u32[]{:S(2)}) collective-permute-start(f32[72,440]{1,0:T(8,128)} %get-tuple-element.52), channel_id=1, source_target_pairs={{0,256},{1,257},{2,258},{3,259},{4,260},{5,261},{6,262},{7,263},{8... | collective-permute-start | bytes 380168 | tf_op jit(solution)/shard_map/ppermute | solution.py:295
  9.5 14.6 %all-to-all-start = ((f32[16,16,128]{2,1,0:T(8,128)}), f32[16,16,128]{2,1,0:T(8,128)S(1)}, u32[]{:S(2)}, u32[]{:S(2)}) async-start(f32[16,16,128]{2,1,0:T(8,128)} %get-tuple-element.51), calls=%async_computation | async-start | bytes 262144 | tf_op jit(solution)/shard_map/all_to_all | solution.py:296
  14.9 1.0 %copy-start.2 = (f32[8,55,256]{2,0,1:T(8,128)S(1)}, f32[8,55,256]{2,0,1:T(8,128)}, u32[]{:S(2)}) copy-start(f32[8,55,256]{2,0,1:T(8,128)} %param.7) | copy-start | bytes 1351684
  15.9 22.4 %collective-permute-start.1 = (f32[440,256]{1,0:T(8,128)S(1)}, f32[440,256]{1,0:T(8,128)S(1)}, u32[]{:S(2)}, u32[]{:S(2)}) collective-permute-start(f32[440,256]{1,0:T(8,128)S(1)} %bitcast.12), channel_id=1, source_target_pairs={{0,256},{1,257},{2,258},{3,259},{4,260},{5,261},{6,262},{7,263},{8... | collective-permute-start | bytes 1351688 | tf_op jit(solution)/shard_map/ppermute | solution.py:314
  24.6 14.5 %collective-permute-start.2 = (f32[16,440]{1,0:T(8,128)S(1)}, f32[16,440]{1,0:T(8,128)S(1)}, u32[]{:S(2)}, u32[]{:S(2)}) collective-permute-start(f32[16,440]{1,0:T(8,128)S(1)} %get-tuple-element.62), channel_id=1, source_target_pairs={{0,1},{1,2},{2,3},{3,4},{4,5},{5,6},{6,7},{7,64},{8,9},{9,10},{10,... | collective-permute-start | bytes 84488 | tf_op jit(solution)/shard_map/ppermute | solution.py:265
  27.1 12.0 %collective-permute-start.3 = (f32[16,440]{1,0:T(8,128)S(1)}, f32[16,440]{1,0:T(8,128)S(1)}, u32[]{:S(2)}, u32[]{:S(2)}) collective-permute-start(f32[16,440]{1,0:T(8,128)S(1)} %get-tuple-element.63), channel_id=1, source_target_pairs={{0,64},{1,65},{2,66},{3,67},{4,68},{5,69},{6,70},{7,71},{8,72},{9,... | collective-permute-start | bytes 84488 | tf_op jit(solution)/shard_map/ppermute | solution.py:265
  28.1 10.9 %collective-permute-start.4 = (f32[16,440]{1,0:T(8,128)S(1)}, f32[16,440]{1,0:T(8,128)S(1)}, u32[]{:S(2)}, u32[]{:S(2)}) collective-permute-start(f32[16,440]{1,0:T(8,128)S(1)} %get-tuple-element.64), channel_id=1, source_target_pairs={{0,119},{1,0},{2,1},{3,2},{4,3},{5,4},{6,5},{7,6},{8,127},{9,8},{1... | collective-permute-start | bytes 84488 | tf_op jit(solution)/shard_map/ppermute | solution.py:265
  36.1 3.4 %collective-permute-start.5 = (f32[16,440]{1,0:T(8,128)S(1)}, f32[16,440]{1,0:T(8,128)S(1)}, u32[]{:S(2)}, u32[]{:S(2)}) collective-permute-start(f32[16,440]{1,0:T(8,128)S(1)} %get-tuple-element.65), channel_id=1, source_target_pairs={{0,112},{1,113},{2,114},{3,115},{4,116},{5,117},{6,118},{7,119},{8... | collective-permute-start | bytes 84488 | tf_op jit(solution)/shard_map/ppermute | solution.py:265
  39.5 10.2 %copy-start = (s32[6,256]{1,0:T(8,128)S(1)}, s32[6,256]{1,0:T(8,128)}, u32[]{:S(2)}) copy-start(s32[6,256]{1,0:T(8,128)} %named.1) | copy-start | bytes 18436
  39.5 10.2 %copy-start.1 = (f32[55,55]{1,0:T(8,128)S(1)}, f32[55,55]{1,0:T(8,128)}, u32[]{:S(2)}) copy-start(f32[55,55]{1,0:T(8,128)} %vloc.1) | copy-start | bytes 36304
  39.7 12.1 %collective-permute-start.6 = (f32[16,440]{1,0:T(8,128)S(1)}, f32[16,440]{1,0:T(8,128)S(1)}, u32[]{:S(2)}, u32[]{:S(2)}) collective-permute-start(f32[16,440]{1,0:T(8,128)S(1)} %get-tuple-element.69), channel_id=1, source_target_pairs={{0,1},{1,2},{2,3},{3,4},{4,5},{5,6},{6,7},{7,64},{8,9},{9,10},{10,... | collective-permute-start | bytes 84488 | tf_op jit(solution)/shard_map/ppermute | solution.py:265
  41.7 10.2 %collective-permute-start.7 = (f32[16,440]{1,0:T(8,128)S(1)}, f32[16,440]{1,0:T(8,128)S(1)}, u32[]{:S(2)}, u32[]{:S(2)}) collective-permute-start(f32[16,440]{1,0:T(8,128)S(1)} %get-tuple-element.72), channel_id=1, source_target_pairs={{0,64},{1,65},{2,66},{3,67},{4,68},{5,69},{6,70},{7,71},{8,72},{9,... | collective-permute-start | bytes 84488 | tf_op jit(solution)/shard_map/ppermute | solution.py:265
  41.7 10.2 %collective-permute-start.8 = (f32[16,440]{1,0:T(8,128)S(1)}, f32[16,440]{1,0:T(8,128)S(1)}, u32[]{:S(2)}, u32[]{:S(2)}) collective-permute-start(f32[16,440]{1,0:T(8,128)S(1)} %get-tuple-element.73), channel_id=1, source_target_pairs={{0,119},{1,0},{2,1},{3,2},{4,3},{5,4},{6,5},{7,6},{8,127},{9,8},{1... | collective-permute-start | bytes 84488 | tf_op jit(solution)/shard_map/ppermute | solution.py:265
  46.5 5.3 %collective-permute-start.9 = (f32[16,440]{1,0:T(8,128)S(1)}, f32[16,440]{1,0:T(8,128)S(1)}, u32[]{:S(2)}, u32[]{:S(2)}) collective-permute-start(f32[16,440]{1,0:T(8,128)S(1)} %get-tuple-element.74), channel_id=1, source_target_pairs={{0,112},{1,113},{2,114},{3,115},{4,116},{5,117},{6,118},{7,119},{8... | collective-permute-start | bytes 84488 | tf_op jit(solution)/shard_map/ppermute | solution.py:265
  52.1 10.6 %collective-permute-start.10 = (f32[16,440]{1,0:T(8,128)S(1)}, f32[16,440]{1,0:T(8,128)S(1)}, u32[]{:S(2)}, u32[]{:S(2)}) collective-permute-start(f32[16,440]{1,0:T(8,128)S(1)} %get-tuple-element.80), channel_id=1, source_target_pairs={{0,1},{1,2},{2,3},{3,4},{4,5},{5,6},{6,7},{7,64},{8,9},{9,10},{10,... | collective-permute-start | bytes 84488 | tf_op jit(solution)/shard_map/ppermute | solution.py:265
  54.0 8.7 %collective-permute-start.11 = (f32[16,440]{1,0:T(8,128)S(1)}, f32[16,440]{1,0:T(8,128)S(1)}, u32[]{:S(2)}, u32[]{:S(2)}) collective-permute-start(f32[16,440]{1,0:T(8,128)S(1)} %get-tuple-element.81), channel_id=1, source_target_pairs={{0,64},{1,65},{2,66},{3,67},{4,68},{5,69},{6,70},{7,71},{8,72},{9,... | collective-permute-start | bytes 84488 | tf_op jit(solution)/shard_map/ppermute | solution.py:265
  54.0 8.7 %collective-permute-start.12 = (f32[16,440]{1,0:T(8,128)S(1)}, f32[16,440]{1,0:T(8,128)S(1)}, u32[]{:S(2)}, u32[]{:S(2)}) collective-permute-start(f32[16,440]{1,0:T(8,128)S(1)} %get-tuple-element.82), channel_id=1, source_target_pairs={{0,119},{1,0},{2,1},{3,2},{4,3},{5,4},{6,5},{7,6},{8,127},{9,8},{1... | collective-permute-start | bytes 84488 | tf_op jit(solution)/shard_map/ppermute | solution.py:265
  58.9 3.8 %collective-permute-start.13 = (f32[16,440]{1,0:T(8,128)S(1)}, f32[16,440]{1,0:T(8,128)S(1)}, u32[]{:S(2)}, u32[]{:S(2)}) collective-permute-start(f32[16,440]{1,0:T(8,128)S(1)} %get-tuple-element.83), channel_id=1, source_target_pairs={{0,112},{1,113},{2,114},{3,115},{4,116},{5,117},{6,118},{7,119},{8... | collective-permute-start | bytes 84488 | tf_op jit(solution)/shard_map/ppermute | solution.py:265
  63.0 2.9 %collective-permute-start.14 = (f32[16,440]{1,0:T(8,128)S(1)}, f32[16,440]{1,0:T(8,128)S(1)}, u32[]{:S(2)}, u32[]{:S(2)}) collective-permute-start(f32[16,440]{1,0:T(8,128)S(1)} %get-tuple-element.87), channel_id=1, source_target_pairs={{0,64},{1,65},{2,66},{3,67},{4,68},{5,69},{6,70},{7,71},{8,72},{9,... | collective-permute-start | bytes 84488 | tf_op jit(solution)/shard_map/ppermute | solution.py:336
  63.0 3.4 %collective-permute-start.15 = (f32[16,440]{1,0:T(8,128)S(1)}, f32[16,440]{1,0:T(8,128)S(1)}, u32[]{:S(2)}, u32[]{:S(2)}) collective-permute-start(f32[16,440]{1,0:T(8,128)S(1)} %get-tuple-element.88), channel_id=1, source_target_pairs={{0,112},{1,113},{2,114},{3,115},{4,116},{5,117},{6,118},{7,119},{8... | collective-permute-start | bytes 84488 | tf_op jit(solution)/shard_map/ppermute | solution.py:337
  67.0 17.5 %collective-permute-start.16 = (f32[440,256]{1,0:T(8,128)S(1)}, f32[440,256]{1,0:T(8,128)S(1)}, u32[]{:S(2)}, u32[]{:S(2)}) collective-permute-start(f32[440,256]{1,0:T(8,128)S(1)} %shard_map.84), channel_id=1, source_target_pairs={{0,320},{1,321},{2,322},{3,323},{4,324},{5,325},{6,326},{7,327},{8... | collective-permute-start | bytes 1351688 | tf_op jit(solution)/shard_map/ppermute | solution.py:341
  70.4 12.9 %collective-permute-start.17 = (f32[16,440]{1,0:T(8,128)S(1)}, f32[16,440]{1,0:T(8,128)S(1)}, u32[]{:S(2)}, u32[]{:S(2)}) collective-permute-start(f32[16,440]{1,0:T(8,128)S(1)} %get-tuple-element.95), channel_id=1, source_target_pairs={{0,321},{1,322},{2,323},{3,324},{4,325},{5,326},{6,327},{7,328},{8... | collective-permute-start | bytes 84488 | tf_op jit(solution)/shard_map/ppermute | solution.py:342
  73.0 10.2 %collective-permute-start.18 = (f32[16,440]{1,0:T(8,128)S(1)}, f32[16,440]{1,0:T(8,128)S(1)}, u32[]{:S(2)}, u32[]{:S(2)}) collective-permute-start(f32[16,440]{1,0:T(8,128)S(1)} %get-tuple-element.96), channel_id=1, source_target_pairs={{0,383},{1,320},{2,321},{3,322},{4,323},{5,324},{6,325},{7,326},{8... | collective-permute-start | bytes 84488 | tf_op jit(solution)/shard_map/ppermute | solution.py:343

commit v5 on v4

--- a/solution.py
+++ b/solution.py
@@ -293,11 +293,9 @@
         vmem=60,
     )
     load = lax.ppermute(load, AXES, GO)
+    load, fields = lax.optimization_barrier((load, fields))
+    fields = lax.ppermute(fields, AXES, GO)
     slots = lax.all_to_all(slots, ("yh", "member"), 0, 0)
-    square = ((FIELDS, FIELDS), BF16)
-    mix_high, mix_low, back_high, back_low, ghosts = call(
-        home_kernel, [square] * 4 + [((2 * RIM, CELLS), BF16)], (vloc, neighbors)
-    )
     adj, sel, rows, gsel, ksel = call(
         near_kernel,
         [
@@ -310,8 +308,12 @@
         (load,),
         flops=10**10,
     )
-    gsel, fields = lax.optimization_barrier((gsel, fields))
-    fields = lax.ppermute(fields, AXES, GO)
+    gsel, vloc = lax.optimization_barrier((gsel, vloc))
+    square = ((FIELDS, FIELDS), BF16)
+    mix_high, mix_low, back_high, back_low, ghosts = call(
+        home_kernel, [square] * 4 + [((2 * RIM, CELLS), BF16)], (vloc, neighbors)
+    )
+    sel, ghosts = lax.optimization_barrier((sel, ghosts))
     rims = call(
         first_kernel, rim_shapes, (core, slots, load, sel, ksel), scalars=1, flops=2*10**10
     )
@@ -327,8 +329,6 @@
         *rims, came = call(rim_kernel, rim_shapes + [border], (b, gsel, ksel, *came))
         y, b = call(stay_kernel, [state, border], (y, adj, sel, rows, came))
         came = exchange(rims)
-        if step == 1:
-            came[0], ghosts = lax.optimization_barrier((came[0], ghosts))
     east, south, west, north, came = call(
         rim_kernel, rim_shapes + [border], (b, gsel, ksel, *came)
     )

time: 87 us -> 86.6 us (level)
    all_to_all x1, waiting for transfers between devices: 2.51 us -> 1.2 us  [local(): slots = lax.all_to_all(slots, ('yh', 'member'), 0, 0)]
    ppermute x1, waiting for transfers between devices: 1.85 us -> 2.9 us  [local(): east = lax.ppermute(east, AXES, homeward(EAST))]
  transfers between devices with their start and end apart: 20 -> 20, of which waited for: 5 -> 6; matrix products, arithmetic and copies ran while one was open for 0% -> 0% of each run, Pallas kernels for 7% -> 7%
where the time goes in v5:
time: 86.6 us; the launch traced here: 85.4 us
  starting transfers between devices  66.9 us (77%)
  Pallas kernels  10.7 us (12%)
  waiting for transfers between devices  6.37 us (7%)
  between operations  0.98 us (1%)
    ppermute x12, starting transfers between devices, exchange(): return [lax.ppermute(rim, AXES, route) for rim, route in zip(rims, ROUTES)]  33.9 us
    pallas_call x14, Pallas kernels, call(): pl.pallas_call(kernel, out_shape=[jax.ShapeDtypeStruct(s, t) for s, t in...  10.7 us
    ppermute x1, starting transfers between devices, local(): load = lax.ppermute(load, AXES, GO)  7.27 us
    ppermute x1, starting transfers between devices, local(): west = lax.ppermute(west, AXES, homeward(WEST))  7.01 us
    ppermute x1, starting transfers between devices, local(): fields = lax.ppermute(fields, AXES, GO)  5.64 us
    all_to_all x1, starting transfers between devices, local(): slots = lax.all_to_all(slots, ('yh', 'member'), 0, 0)  5.46 us
    ppermute x1, starting transfers between devices, local(): y = lax.ppermute(y, AXES, BACK)  3.24 us
    ppermute x1, waiting for transfers between devices, local(): east = lax.ppermute(east, AXES, homeward(EAST))  2.9 us
  transfers between devices with their start and end apart: 20, of which 6 were waited for; matrix products, arithmetic and copies ran while one was open for 0% of the time, Pallas kernels for 7%

profile of v5, /device:TPU:1, one launch (start us, length us, event | category | flops | bytes accessed | tf_op | source)
XLA Modules:
  0.0 85.4 jit_solution(17046056826109855550)
XLA Ops:
  0.0 2.2 %shard_map.73 = (f32[16,16,128]{2,1,0:T(8,128)}, f32[72,440]{1,0:T(8,128)}) custom-call(f32[32,55]{1,0:T(8,128)} %bitcast.13, f32[440,256]{1,0:T(8,128)} %bitcast.11, f32[1,256]{1,0:T(1,128)} %bitcast.14, s32[6,256]{1,0:T(8,128)} %named.1, s32[4,16]{1,0:T(4,128)} %sends_in.1), custom_call_target="tpu_custom_call" | custom-call | flops 100000000 | bytes 1000000 | tf_op jit(solution)/shard_map/pallas_call | solution.py:253
  2.2 7.3 %collective-permute-start = (f32[72,440]{1,0:T(8,128)}, f32[72,440]{1,0:T(8,128)S(1)}, u32[]{:S(2)}, u32[]{:S(2)}) collective-permute-start(f32[72,440]{1,0:T(8,128)} %get-tuple-element.54), channel_id=1, source_target_pairs={{0,256},{1,257},{2,258},{3,259},{4,260},{5,261},{6,262},{7,263},{8... | collective-permute-start | bytes 380168 | tf_op jit(solution)/shard_map/ppermute | solution.py:295
  9.5 5.5 %all-to-all-start = ((f32[16,16,128]{2,1,0:T(8,128)}), f32[16,16,128]{2,1,0:T(8,128)S(1)}, u32[]{:S(2)}, u32[]{:S(2)}) async-start(f32[16,16,128]{2,1,0:T(8,128)} %get-tuple-element.53), calls=%async_computation | async-start | bytes 262144 | tf_op jit(solution)/shard_map/all_to_all | solution.py:298
  14.9 0.0 copy-start.2
  14.9 0.0 copy-start
  14.9 0.0 copy-start.1
  14.9 0.0 collective-permute-done.load
  15.0 0.6 shard_map.74
  15.5 0.4 copy-done.2
  15.9 5.6 %collective-permute-start.1 = (f32[440,256]{1,0:T(8,128)S(1)}, f32[440,256]{1,0:T(8,128)S(1)}, u32[]{:S(2)}, u32[]{:S(2)}) collective-permute-start(f32[440,256]{1,0:T(8,128)S(1)} %bitcast.12), channel_id=1, source_target_pairs={{0,256},{1,257},{2,258},{3,259},{4,260},{5,261},{6,262},{7,263},{8... | collective-permute-start | bytes 1351688 | tf_op jit(solution)/shard_map/ppermute | solution.py:297
  21.6 0.0 copy-done
  21.6 0.0 copy-done.1
  21.6 1.3 %shard_map.75 = (bf16[440,440]{1,0:T(8,128)(2,1)S(1)}, bf16[440,440]{1,0:T(8,128)(2,1)S(1)}, bf16[440,440]{1,0:T(8,128)(2,1)S(1)}, bf16[440,440]{1,0:T(8,128)(2,1)S(1)}, bf16[32,256]{1,0:T(8,128)(2,1)S(1)}) custom-call(f32[55,55]{1,0:T(8,128)S(1)} %copy-done.1, s32[6,256]{1,0:T(8,128)S(1)} %copy-done), custom_call_target="tpu_custom_call" | custom-call | flops 100000000 | bytes 1000000 | tf_op jit(solution)/shard_map/pallas_call | solution.py:253
  22.9 1.2 %all-to-all-done.slots = f32[16,16,128]{2,1,0:T(8,128)S(1)} async-done(((f32[16,16,128]{2,1,0:T(8,128)}), f32[16,16,128]{2,1,0:T(8,128)S(1)}, u32[]{:S(2)}, u32[]{:S(2)}) %all-to-all-start) | async-done | bytes 131104 | tf_op jit(solution)/shard_map/all_to_all | solution.py:298
  24.1 0.5 shard_map.77
  24.6 2.5 %collective-permute-start.2 = (f32[16,440]{1,0:T(8,128)S(1)}, f32[16,440]{1,0:T(8,128)S(1)}, u32[]{:S(2)}, u32[]{:S(2)}) collective-permute-start(f32[16,440]{1,0:T(8,128)S(1)} %get-tuple-element.68), channel_id=1, source_target_pairs={{0,1},{1,2},{2,3},{3,4},{4,5},{5,6},{6,7},{7,64},{8,9},{9,10},{10,... | collective-permute-start | bytes 84488 | tf_op jit(solution)/shard_map/ppermute | solution.py:265
  27.1 1.1 %collective-permute-start.3 = (f32[16,440]{1,0:T(8,128)S(1)}, f32[16,440]{1,0:T(8,128)S(1)}, u32[]{:S(2)}, u32[]{:S(2)}) collective-permute-start(f32[16,440]{1,0:T(8,128)S(1)} %get-tuple-element.69), channel_id=1, source_target_pairs={{0,64},{1,65},{2,66},{3,67},{4,68},{5,69},{6,70},{7,71},{8,72},{9,... | collective-permute-start | bytes 84488 | tf_op jit(solution)/shard_map/ppermute | solution.py:265
  28.1 7.9 %collective-permute-start.4 = (f32[16,440]{1,0:T(8,128)S(1)}, f32[16,440]{1,0:T(8,128)S(1)}, u32[]{:S(2)}, u32[]{:S(2)}) collective-permute-start(f32[16,440]{1,0:T(8,128)S(1)} %get-tuple-element.70), channel_id=1, source_target_pairs={{0,119},{1,0},{2,1},{3,2},{4,3},{5,4},{6,5},{7,6},{8,127},{9,8},{1... | collective-permute-start | bytes 84488 | tf_op jit(solution)/shard_map/ppermute | solution.py:265
  36.1 2.2 %collective-permute-start.5 = (f32[16,440]{1,0:T(8,128)S(1)}, f32[16,440]{1,0:T(8,128)S(1)}, u32[]{:S(2)}, u32[]{:S(2)}) collective-permute-start(f32[16,440]{1,0:T(8,128)S(1)} %get-tuple-element.71), channel_id=1, source_target_pairs={{0,112},{1,113},{2,114},{3,115},{4,116},{5,117},{6,118},{7,119},{8... | collective-permute-start | bytes 84488 | tf_op jit(solution)/shard_map/ppermute | solution.py:265
  38.3 0.0 collective-permute-done.1.fields
  38.3 0.7 shard_map.76
  39.1 0.0 collective-permute-done.2.i0
  39.1 0.0 collective-permute-done.3.i1
  39.1 0.0 collective-permute-done.4.i2
  39.1 0.4 collective-permute-done.5.i3
  39.5 0.2 shard_map.78
  39.7 1.9 %collective-permute-start.6 = (f32[16,440]{1,0:T(8,128)S(1)}, f32[16,440]{1,0:T(8,128)S(1)}, u32[]{:S(2)}, u32[]{:S(2)}) collective-permute-start(f32[16,440]{1,0:T(8,128)S(1)} %get-tuple-element.75), channel_id=1, source_target_pairs={{0,1},{1,2},{2,3},{3,4},{4,5},{5,6},{6,7},{7,64},{8,9},{9,10},{10,... | collective-permute-start | bytes 84488 | tf_op jit(solution)/shard_map/ppermute | solution.py:265
  41.7 0.0 collective-permute-start.7
  41.7 4.9 %collective-permute-start.8 = (f32[16,440]{1,0:T(8,128)S(1)}, f32[16,440]{1,0:T(8,128)S(1)}, u32[]{:S(2)}, u32[]{:S(2)}) collective-permute-start(f32[16,440]{1,0:T(8,128)S(1)} %get-tuple-element.77), channel_id=1, source_target_pairs={{0,119},{1,0},{2,1},{3,2},{4,3},{5,4},{6,5},{7,6},{8,127},{9,8},{1... | collective-permute-start | bytes 84488 | tf_op jit(solution)/shard_map/ppermute | solution.py:265
  46.5 3.2 %collective-permute-start.9 = (f32[16,440]{1,0:T(8,128)S(1)}, f32[16,440]{1,0:T(8,128)S(1)}, u32[]{:S(2)}, u32[]{:S(2)}) collective-permute-start(f32[16,440]{1,0:T(8,128)S(1)} %get-tuple-element.78), channel_id=1, source_target_pairs={{0,112},{1,113},{2,114},{3,115},{4,116},{5,117},{6,118},{7,119},{8... | collective-permute-start | bytes 84488 | tf_op jit(solution)/shard_map/ppermute | solution.py:265
  49.7 0.8 shard_map.79
  50.5 0.0 collective-permute-done.6.i0
  50.6 0.0 collective-permute-done.7.i1
  50.6 0.0 collective-permute-done.8.i2
  50.6 0.2 collective-permute-done.9.i3
  50.8 0.2 shard_map.80
  51.0 1.9 %collective-permute-start.10 = (f32[16,440]{1,0:T(8,128)S(1)}, f32[16,440]{1,0:T(8,128)S(1)}, u32[]{:S(2)}, u32[]{:S(2)}) collective-permute-start(f32[16,440]{1,0:T(8,128)S(1)} %get-tuple-element.84), channel_id=1, source_target_pairs={{0,1},{1,2},{2,3},{3,4},{4,5},{5,6},{6,7},{7,64},{8,9},{9,10},{10,... | collective-permute-start | bytes 84488 | tf_op jit(solution)/shard_map/ppermute | solution.py:265
  52.9 0.0 collective-permute-start.11
  53.0 4.9 %collective-permute-start.12 = (f32[16,440]{1,0:T(8,128)S(1)}, f32[16,440]{1,0:T(8,128)S(1)}, u32[]{:S(2)}, u32[]{:S(2)}) collective-permute-start(f32[16,440]{1,0:T(8,128)S(1)} %get-tuple-element.86), channel_id=1, source_target_pairs={{0,119},{1,0},{2,1},{3,2},{4,3},{5,4},{6,5},{7,6},{8,127},{9,8},{1... | collective-permute-start | bytes 84488 | tf_op jit(solution)/shard_map/ppermute | solution.py:265
  57.8 3.5 %collective-permute-start.13 = (f32[16,440]{1,0:T(8,128)S(1)}, f32[16,440]{1,0:T(8,128)S(1)}, u32[]{:S(2)}, u32[]{:S(2)}) collective-permute-start(f32[16,440]{1,0:T(8,128)S(1)} %get-tuple-element.87), channel_id=1, source_target_pairs={{0,112},{1,113},{2,114},{3,115},{4,116},{5,117},{6,118},{7,119},{8... | collective-permute-start | bytes 84488 | tf_op jit(solution)/shard_map/ppermute | solution.py:265
  61.3 0.8 shard_map.81
  62.1 0.0 collective-permute-done.10.i0
  62.1 0.0 collective-permute-done.11.i1
  62.1 0.0 collective-permute-done.12.i2
  62.1 0.0 collective-permute-done.13.i3
  62.2 0.2 shard_map.82
  62.4 0.0 collective-permute-start.14
  62.4 1.6 %collective-permute-start.15 = (f32[16,440]{1,0:T(8,128)S(1)}, f32[16,440]{1,0:T(8,128)S(1)}, u32[]{:S(2)}, u32[]{:S(2)}) collective-permute-start(f32[16,440]{1,0:T(8,128)S(1)} %get-tuple-element.92), channel_id=1, source_target_pairs={{0,112},{1,113},{2,114},{3,115},{4,116},{5,117},{6,118},{7,119},{8... | collective-permute-start | bytes 84488 | tf_op jit(solution)/shard_map/ppermute | solution.py:337
  63.9 1.1 %shard_map.83.y = f32[440,256]{1,0:T(8,128)S(1)} custom-call(f32[440,256]{1,0:T(8,128)S(1)} %get-tuple-element.80.y, bf16[320,256]{1,0:T(8,128)(2,1)S(1)} %get-tuple-element.57.adj, f32[8,256]{1,0:T(8,128)S(1)} %get-tuple-element.63.rows, bf16[440,440]{1,0:T(8,128)(2,1)S(1)} %get-tuple-element.81.mix_high, bf16[440,440]{1,0:T(8,128)(2,1)S(1)} %get-tuple-element.82.mix_low, ...), custom_call_target="tpu_custom_call" | custom-call | flops 100000000 | bytes 1000000 | tf_op jit(solution)/shard_map/pallas_call | solution.py:253
  65.1 0.3 shard_map.85
  65.4 0.0 collective-permute-done.14.south
  65.4 0.9 %collective-permute-done.15.north = f32[16,440]{1,0:T(8,128)S(1)} collective-permute-done((f32[16,440]{1,0:T(8,128)S(1)}, f32[16,440]{1,0:T(8,128)S(1)}, u32[]{:S(2)}, u32[]{:S(2)}) %collective-permute-start.15) | collective-permute-done | bytes 28192 | tf_op jit(solution)/shard_map/ppermute | solution.py:337
  66.3 0.7 shard_map.84
  67.0 3.2 %collective-permute-start.16 = (f32[440,256]{1,0:T(8,128)S(1)}, f32[440,256]{1,0:T(8,128)S(1)}, u32[]{:S(2)}, u32[]{:S(2)}) collective-permute-start(f32[440,256]{1,0:T(8,128)S(1)} %shard_map.84), channel_id=1, source_target_pairs={{0,320},{1,321},{2,322},{3,323},{4,324},{5,325},{6,326},{7,327},{8... | collective-permute-start | bytes 1351688 | tf_op jit(solution)/shard_map/ppermute | solution.py:341
  70.2 2.8 %collective-permute-start.17 = (f32[16,440]{1,0:T(8,128)S(1)}, f32[16,440]{1,0:T(8,128)S(1)}, u32[]{:S(2)}, u32[]{:S(2)}) collective-permute-start(f32[16,440]{1,0:T(8,128)S(1)} %get-tuple-element.99), channel_id=1, source_target_pairs={{0,321},{1,322},{2,323},{3,324},{4,325},{5,326},{6,327},{7,328},{8... | collective-permute-start | bytes 84488 | tf_op jit(solution)/shard_map/ppermute | solution.py:342
  73.0 7.0 %collective-permute-start.18 = (f32[16,440]{1,0:T(8,128)S(1)}, f32[16,440]{1,0:T(8,128)S(1)}, u32[]{:S(2)}, u32[]{:S(2)}) collective-permute-start(f32[16,440]{1,0:T(8,128)S(1)} %get-tuple-element.100), channel_id=1, source_target_pairs={{0,383},{1,320},{2,321},{3,322},{4,323},{5,324},{6,325},{7,326},{8... | collective-permute-start | bytes 84488 | tf_op jit(solution)/shard_map/ppermute | solution.py:343
  80.7 2.9 %collective-permute-done.17.east = f32[16,440]{1,0:T(8,128)S(1)} collective-permute-done((f32[16,440]{1,0:T(8,128)S(1)}, f32[16,440]{1,0:T(8,128)S(1)}, u32[]{:S(2)}, u32[]{:S(2)}) %collective-permute-start.17) | collective-permute-done | bytes 28192 | tf_op jit(solution)/shard_map/ppermute | solution.py:342
  83.6 0.0 collective-permute-done.18.west
  83.6 0.7 collective-permute-done.16.y
  84.3 1.1 %shard_map.86 = f32[440,256]{1,0:T(8,128)} custom-call(s32[1]{0:T(128)S(6)} %copy.8.count, f32[440,256]{1,0:T(8,128)S(1)} %collective-permute-done.16.y, bf16[32,256]{1,0:T(8,128)(2,1)S(1)} %get-tuple-element.98.ghosts, f32[16,440]{1,0:T(8,128)S(1)} %collective-permute-done.17.east, f32[16,440]{1,0:T(8,128)S(1)} %collective-permute-done.18.west), custom_call_target="tpu_custom_call" | custom-call | flops 100000000 | bytes 1000000 | tf_op jit(solution)/shard_map/pallas_call | solution.py:253
Async XLA Ops:
  2.2 12.8 %collective-permute-start = (f32[72,440]{1,0:T(8,128)}, f32[72,440]{1,0:T(8,128)S(1)}, u32[]{:S(2)}, u32[]{:S(2)}) collective-permute-start(f32[72,440]{1,0:T(8,128)} %get-tuple-element.54), channel_id=1, source_target_pairs={{0,256},{1,257},{2,258},{3,259},{4,260},{5,261},{6,262},{7,263},{8... | collective-permute-start | bytes 380168 | tf_op jit(solution)/shard_map/ppermute | solution.py:295
  9.5 14.6 %all-to-all-start = ((f32[16,16,128]{2,1,0:T(8,128)}), f32[16,16,128]{2,1,0:T(8,128)S(1)}, u32[]{:S(2)}, u32[]{:S(2)}) async-start(f32[16,16,128]{2,1,0:T(8,128)} %get-tuple-element.53), calls=%async_computation | async-start | bytes 262144 | tf_op jit(solution)/shard_map/all_to_all | solution.py:298
  14.9 1.0 %copy-start.2 = (f32[8,55,256]{2,0,1:T(8,128)S(1)}, f32[8,55,256]{2,0,1:T(8,128)}, u32[]{:S(2)}) copy-start(f32[8,55,256]{2,0,1:T(8,128)} %param.7) | copy-start | bytes 1351684
  14.9 6.7 %copy-start = (s32[6,256]{1,0:T(8,128)S(1)}, s32[6,256]{1,0:T(8,128)}, u32[]{:S(2)}) copy-start(s32[6,256]{1,0:T(8,128)} %named.1) | copy-start | bytes 18436
  14.9 6.7 %copy-start.1 = (f32[55,55]{1,0:T(8,128)S(1)}, f32[55,55]{1,0:T(8,128)}, u32[]{:S(2)}) copy-start(f32[55,55]{1,0:T(8,128)} %vloc) | copy-start | bytes 36304
  15.9 22.4 %collective-permute-start.1 = (f32[440,256]{1,0:T(8,128)S(1)}, f32[440,256]{1,0:T(8,128)S(1)}, u32[]{:S(2)}, u32[]{:S(2)}) collective-permute-start(f32[440,256]{1,0:T(8,128)S(1)} %bitcast.12), channel_id=1, source_target_pairs={{0,256},{1,257},{2,258},{3,259},{4,260},{5,261},{6,262},{7,263},{8... | collective-permute-start | bytes 1351688 | tf_op jit(solution)/shard_map/ppermute | solution.py:297
  24.6 14.5 %collective-permute-start.2 = (f32[16,440]{1,0:T(8,128)S(1)}, f32[16,440]{1,0:T(8,128)S(1)}, u32[]{:S(2)}, u32[]{:S(2)}) collective-permute-start(f32[16,440]{1,0:T(8,128)S(1)} %get-tuple-element.68), channel_id=1, source_target_pairs={{0,1},{1,2},{2,3},{3,4},{4,5},{5,6},{6,7},{7,64},{8,9},{9,10},{10,... | collective-permute-start | bytes 84488 | tf_op jit(solution)/shard_map/ppermute | solution.py:265
  27.1 12.0 %collective-permute-start.3 = (f32[16,440]{1,0:T(8,128)S(1)}, f32[16,440]{1,0:T(8,128)S(1)}, u32[]{:S(2)}, u32[]{:S(2)}) collective-permute-start(f32[16,440]{1,0:T(8,128)S(1)} %get-tuple-element.69), channel_id=1, source_target_pairs={{0,64},{1,65},{2,66},{3,67},{4,68},{5,69},{6,70},{7,71},{8,72},{9,... | collective-permute-start | bytes 84488 | tf_op jit(solution)/shard_map/ppermute | solution.py:265
  28.1 10.9 %collective-permute-start.4 = (f32[16,440]{1,0:T(8,128)S(1)}, f32[16,440]{1,0:T(8,128)S(1)}, u32[]{:S(2)}, u32[]{:S(2)}) collective-permute-start(f32[16,440]{1,0:T(8,128)S(1)} %get-tuple-element.70), channel_id=1, source_target_pairs={{0,119},{1,0},{2,1},{3,2},{4,3},{5,4},{6,5},{7,6},{8,127},{9,8},{1... | collective-permute-start | bytes 84488 | tf_op jit(solution)/shard_map/ppermute | solution.py:265
  36.1 3.4 %collective-permute-start.5 = (f32[16,440]{1,0:T(8,128)S(1)}, f32[16,440]{1,0:T(8,128)S(1)}, u32[]{:S(2)}, u32[]{:S(2)}) collective-permute-start(f32[16,440]{1,0:T(8,128)S(1)} %get-tuple-element.71), channel_id=1, source_target_pairs={{0,112},{1,113},{2,114},{3,115},{4,116},{5,117},{6,118},{7,119},{8... | collective-permute-start | bytes 84488 | tf_op jit(solution)/shard_map/ppermute | solution.py:265
  39.7 10.8 %collective-permute-start.6 = (f32[16,440]{1,0:T(8,128)S(1)}, f32[16,440]{1,0:T(8,128)S(1)}, u32[]{:S(2)}, u32[]{:S(2)}) collective-permute-start(f32[16,440]{1,0:T(8,128)S(1)} %get-tuple-element.75), channel_id=1, source_target_pairs={{0,1},{1,2},{2,3},{3,4},{4,5},{5,6},{6,7},{7,64},{8,9},{9,10},{10,... | collective-permute-start | bytes 84488 | tf_op jit(solution)/shard_map/ppermute | solution.py:265
  41.7 8.9 %collective-permute-start.7 = (f32[16,440]{1,0:T(8,128)S(1)}, f32[16,440]{1,0:T(8,128)S(1)}, u32[]{:S(2)}, u32[]{:S(2)}) collective-permute-start(f32[16,440]{1,0:T(8,128)S(1)} %get-tuple-element.76), channel_id=1, source_target_pairs={{0,64},{1,65},{2,66},{3,67},{4,68},{5,69},{6,70},{7,71},{8,72},{9,... | collective-permute-start | bytes 84488 | tf_op jit(solution)/shard_map/ppermute | solution.py:265
  41.7 8.9 %collective-permute-start.8 = (f32[16,440]{1,0:T(8,128)S(1)}, f32[16,440]{1,0:T(8,128)S(1)}, u32[]{:S(2)}, u32[]{:S(2)}) collective-permute-start(f32[16,440]{1,0:T(8,128)S(1)} %get-tuple-element.77), channel_id=1, source_target_pairs={{0,119},{1,0},{2,1},{3,2},{4,3},{5,4},{6,5},{7,6},{8,127},{9,8},{1... | collective-permute-start | bytes 84488 | tf_op jit(solution)/shard_map/ppermute | solution.py:265
  46.5 4.3 %collective-permute-start.9 = (f32[16,440]{1,0:T(8,128)S(1)}, f32[16,440]{1,0:T(8,128)S(1)}, u32[]{:S(2)}, u32[]{:S(2)}) collective-permute-start(f32[16,440]{1,0:T(8,128)S(1)} %get-tuple-element.78), channel_id=1, source_target_pairs={{0,112},{1,113},{2,114},{3,115},{4,116},{5,117},{6,118},{7,119},{8... | collective-permute-start | bytes 84488 | tf_op jit(solution)/shard_map/ppermute | solution.py:265
  51.0 11.1 %collective-permute-start.10 = (f32[16,440]{1,0:T(8,128)S(1)}, f32[16,440]{1,0:T(8,128)S(1)}, u32[]{:S(2)}, u32[]{:S(2)}) collective-permute-start(f32[16,440]{1,0:T(8,128)S(1)} %get-tuple-element.84), channel_id=1, source_target_pairs={{0,1},{1,2},{2,3},{3,4},{4,5},{5,6},{6,7},{7,64},{8,9},{9,10},{10,... | collective-permute-start | bytes 84488 | tf_op jit(solution)/shard_map/ppermute | solution.py:265
  52.9 9.2 %collective-permute-start.11 = (f32[16,440]{1,0:T(8,128)S(1)}, f32[16,440]{1,0:T(8,128)S(1)}, u32[]{:S(2)}, u32[]{:S(2)}) collective-permute-start(f32[16,440]{1,0:T(8,128)S(1)} %get-tuple-element.85), channel_id=1, source_target_pairs={{0,64},{1,65},{2,66},{3,67},{4,68},{5,69},{6,70},{7,71},{8,72},{9,... | collective-permute-start | bytes 84488 | tf_op jit(solution)/shard_map/ppermute | solution.py:265
  53.0 9.2 %collective-permute-start.12 = (f32[16,440]{1,0:T(8,128)S(1)}, f32[16,440]{1,0:T(8,128)S(1)}, u32[]{:S(2)}, u32[]{:S(2)}) collective-permute-start(f32[16,440]{1,0:T(8,128)S(1)} %get-tuple-element.86), channel_id=1, source_target_pairs={{0,119},{1,0},{2,1},{3,2},{4,3},{5,4},{6,5},{7,6},{8,127},{9,8},{1... | collective-permute-start | bytes 84488 | tf_op jit(solution)/shard_map/ppermute | solution.py:265
  57.8 4.3 %collective-permute-start.13 = (f32[16,440]{1,0:T(8,128)S(1)}, f32[16,440]{1,0:T(8,128)S(1)}, u32[]{:S(2)}, u32[]{:S(2)}) collective-permute-start(f32[16,440]{1,0:T(8,128)S(1)} %get-tuple-element.87), channel_id=1, source_target_pairs={{0,112},{1,113},{2,114},{3,115},{4,116},{5,117},{6,118},{7,119},{8... | collective-permute-start | bytes 84488 | tf_op jit(solution)/shard_map/ppermute | solution.py:265
  62.4 3.0 %collective-permute-start.14 = (f32[16,440]{1,0:T(8,128)S(1)}, f32[16,440]{1,0:T(8,128)S(1)}, u32[]{:S(2)}, u32[]{:S(2)}) collective-permute-start(f32[16,440]{1,0:T(8,128)S(1)} %get-tuple-element.91), channel_id=1, source_target_pairs={{0,64},{1,65},{2,66},{3,67},{4,68},{5,69},{6,70},{7,71},{8,72},{9,... | collective-permute-start | bytes 84488 | tf_op jit(solution)/shard_map/ppermute | solution.py:336
  62.4 3.9 %collective-permute-start.15 = (f32[16,440]{1,0:T(8,128)S(1)}, f32[16,440]{1,0:T(8,128)S(1)}, u32[]{:S(2)}, u32[]{:S(2)}) collective-permute-start(f32[16,440]{1,0:T(8,128)S(1)} %get-tuple-element.92), channel_id=1, source_target_pairs={{0,112},{1,113},{2,114},{3,115},{4,116},{5,117},{6,118},{7,119},{8... | collective-permute-start | bytes 84488 | tf_op jit(solution)/shard_map/ppermute | solution.py:337
  67.0 17.3 %collective-permute-start.16 = (f32[440,256]{1,0:T(8,128)S(1)}, f32[440,256]{1,0:T(8,128)S(1)}, u32[]{:S(2)}, u32[]{:S(2)}) collective-permute-start(f32[440,256]{1,0:T(8,128)S(1)} %shard_map.84), channel_id=1, source_target_pairs={{0,320},{1,321},{2,322},{3,323},{4,324},{5,325},{6,326},{7,327},{8... | collective-permute-start | bytes 1351688 | tf_op jit(solution)/shard_map/ppermute | solution.py:341
  70.2 13.3 %collective-permute-start.17 = (f32[16,440]{1,0:T(8,128)S(1)}, f32[16,440]{1,0:T(8,128)S(1)}, u32[]{:S(2)}, u32[]{:S(2)}) collective-permute-start(f32[16,440]{1,0:T(8,128)S(1)} %get-tuple-element.99), channel_id=1, source_target_pairs={{0,321},{1,322},{2,323},{3,324},{4,325},{5,326},{6,327},{7,328},{8... | collective-permute-start | bytes 84488 | tf_op jit(solution)/shard_map/ppermute | solution.py:342
  73.0 10.6 %collective-permute-start.18 = (f32[16,440]{1,0:T(8,128)S(1)}, f32[16,440]{1,0:T(8,128)S(1)}, u32[]{:S(2)}, u32[]{:S(2)}) collective-permute-start(f32[16,440]{1,0:T(8,128)S(1)} %get-tuple-element.100), channel_id=1, source_target_pairs={{0,383},{1,320},{2,321},{3,322},{4,323},{5,324},{6,325},{7,326},{8... | collective-permute-start | bytes 84488 | tf_op jit(solution)/shard_map/ppermute | solution.py:343

commit v6 on v5

--- a/solution.py
+++ b/solution.py
@@ -103,17 +103,20 @@
     ]
     for copy in copies:
         copy.start()
-    for copy in copies:
-        copy.wait()
     grad, fields, kappa, named, sends = held
+    copies[0].wait()
     piece = jnp.concatenate([grad[...], jnp.zeros((32, 64 - LEV), F32)], axis=1)
     slots[0] = jnp.concatenate([piece[0:RIM], piece[RIM:]], axis=1)
     for s in range(1, 16):
         slots[s] = slots[0]
+    for copy in copies[2:]:
+        copy.wait()
     row = [sends[d : d + 1, :].astype(F32) for d in range(4)]
     row.append(jnp.zeros((1, CELLS - GHOSTS), F32))
     row = jnp.concatenate(row, axis=1)
-    out[0:GHOSTS, :] = exact_dot(chosen(row[:, :128]), fields[...], ((1,), (1,)), 3)
+    sel = chosen(row[:, :128])
+    copies[1].wait()
+    out[0:GHOSTS, :] = exact_dot(sel, fields[...], ((1,), (1,)))
     out[GHOSTS:, 0:CELLS] = jnp.concatenate([named[...].astype(F32), kappa[...], row], axis=0)
     out[GHOSTS:, CELLS:] = jnp.zeros((8, FIELDS - CELLS), F32)
 
@@ -238,23 +241,31 @@
     ghosts[...] = total.astype(BF16)
 
 
-def last_kernel(count, y, ghosts, east, west, out):
+def last_kernel(count, y, ghosts, east, west, out, held, done):
     alive = lax.broadcasted_iota(jnp.int32, (1, CELLS), 1) < count[0]
-    rims = jnp.concatenate([east[...], west[...]], axis=0)
-    out[...] = jnp.where(alive, arrive(y, ghosts[...], rims), 0.0)
+    rims = jnp.concatenate([east[...], west[...]], axis=0).T
+    copies = []
+    for i, first in enumerate(range(0, FIELDS, 112)):
+        part = pl.ds(first, min(112, FIELDS - first))
+        sides = exact_dot(rims[first : first + 112], ghosts[...], ((1,), (0,)))
+        held[part, :] = jnp.where(alive, y[part, :] + sides, 0.0)
+        copies.append(pltpu.make_async_copy(held.at[part], out.at[part], done.at[i]))
+        copies[-1].start()
+    for copy in copies:
+        copy.wait()
 
 
 VM = pl.BlockSpec(memory_space=pltpu.VMEM)
 SM = pl.BlockSpec(memory_space=pltpu.SMEM)
 
 
-def call(kernel, shapes, args, scalars=0, flops=10**8, scratch=(), rest=VM, vmem=32):
+def call(kernel, shapes, args, scalars=0, flops=10**8, scratch=(), rest=VM, vmem=32, outs=None):
     specs = [SM] * scalars + [rest] * (len(args) - scalars)
     return pl.pallas_call(
         kernel,
         out_shape=[jax.ShapeDtypeStruct(s, t) for s, t in shapes],
         in_specs=specs,
-        out_specs=[VM] * len(shapes),
+        out_specs=[outs or VM] * len(shapes),
         scratch_shapes=list(scratch),
         cost_estimate=pl.CostEstimate(flops=flops, bytes_accessed=10**6, transcendentals=0),
         compiler_params=pltpu.CompilerParams(vmem_limit_bytes=vmem * 1024 * 1024),
@@ -341,7 +352,14 @@
     y = lax.ppermute(y, AXES, BACK)
     east = lax.ppermute(east, AXES, homeward(EAST))
     west = lax.ppermute(west, AXES, homeward(WEST))
-    (out,) = call(last_kernel, [state], (counts, y, ghosts, east, west), scalars=1)
+    (out,) = call(
+        last_kernel,
+        [state],
+        (counts, y, ghosts, east, west),
+        scalars=1,
+        scratch=[pltpu.VMEM((FIELDS, CELLS), F32), pltpu.SemaphoreType.DMA((4,))],
+        outs=pl.BlockSpec(memory_space=pltpu.HBM),
+    )
     return out.reshape(LEV, MEM, CELLS).transpose(1, 0, 2)
 
 

time: 86.6 us -> 86.5 us (level)
  no operation moved by 1% of the time
where the time goes in v6:
time: 86.5 us; the launch traced here: 85.2 us
  starting transfers between devices  66.9 us (77%)
  Pallas kernels  10.6 us (12%)
  waiting for transfers between devices  6.37 us (7%)
  between operations  0.99 us (1%)
    ppermute x12, starting transfers between devices, exchange(): return [lax.ppermute(rim, AXES, route) for rim, route in zip(rims, ROUTES)]  33.9 us
    pallas_call x14, Pallas kernels, call(): pl.pallas_call(kernel, out_shape=[jax.ShapeDtypeStruct(s, t) for s, t in...  10.6 us
    ppermute x1, starting transfers between devices, local(): load = lax.ppermute(load, AXES, GO)  7.27 us
    ppermute x1, starting transfers between devices, local(): west = lax.ppermute(west, AXES, homeward(WEST))  7 us
    ppermute x1, starting transfers between devices, local(): fields = lax.ppermute(fields, AXES, GO)  5.64 us
    all_to_all x1, starting transfers between devices, local(): slots = lax.all_to_all(slots, ('yh', 'member'), 0, 0)  5.46 us
    ppermute x1, starting transfers between devices, local(): y = lax.ppermute(y, AXES, BACK)  3.24 us
    ppermute x1, waiting for transfers between devices, local(): east = lax.ppermute(east, AXES, homeward(EAST))  2.9 us
  transfers between devices with their start and end apart: 20, of which 6 were waited for; matrix products, arithmetic and copies ran while one was open for 0% of the time, Pallas kernels for 7%

profile of v6, /device:TPU:1, one launch (start us, length us, event | category | flops | bytes accessed | tf_op | source)
XLA Modules:
  0.0 85.2 jit_solution(14952358830358400337)
XLA Ops:
  0.0 2.1 %shard_map.73 = (f32[16,16,128]{2,1,0:T(8,128)}, f32[72,440]{1,0:T(8,128)}) custom-call(f32[32,55]{1,0:T(8,128)} %bitcast.13, f32[440,256]{1,0:T(8,128)} %bitcast.11, f32[1,256]{1,0:T(1,128)} %bitcast.14, s32[6,256]{1,0:T(8,128)} %named.1, s32[4,16]{1,0:T(4,128)} %sends_in.1), custom_call_target="tpu_custom_call" | custom-call | flops 100000000 | bytes 1000000 | tf_op jit(solution)/shard_map/pallas_call | solution.py:264
  2.1 7.3 %collective-permute-start = (f32[72,440]{1,0:T(8,128)}, f32[72,440]{1,0:T(8,128)S(1)}, u32[]{:S(2)}, u32[]{:S(2)}) collective-permute-start(f32[72,440]{1,0:T(8,128)} %get-tuple-element.54), channel_id=1, source_target_pairs={{0,256},{1,257},{2,258},{3,259},{4,260},{5,261},{6,262},{7,263},{8... | collective-permute-start | bytes 380168 | tf_op jit(solution)/shard_map/ppermute | solution.py:306
  9.4 5.5 %all-to-all-start = ((f32[16,16,128]{2,1,0:T(8,128)}), f32[16,16,128]{2,1,0:T(8,128)S(1)}, u32[]{:S(2)}, u32[]{:S(2)}) async-start(f32[16,16,128]{2,1,0:T(8,128)} %get-tuple-element.53), calls=%async_computation | async-start | bytes 262144 | tf_op jit(solution)/shard_map/all_to_all | solution.py:309
  14.8 0.0 copy-start.2
  14.8 0.0 copy-start
  14.8 0.0 copy-start.1
  14.8 0.0 collective-permute-done.load
  14.9 0.5 shard_map.74
  15.4 0.4 copy-done.2
  15.8 5.6 %collective-permute-start.1 = (f32[440,256]{1,0:T(8,128)S(1)}, f32[440,256]{1,0:T(8,128)S(1)}, u32[]{:S(2)}, u32[]{:S(2)}) collective-permute-start(f32[440,256]{1,0:T(8,128)S(1)} %bitcast.12), channel_id=1, source_target_pairs={{0,256},{1,257},{2,258},{3,259},{4,260},{5,261},{6,262},{7,263},{8... | collective-permute-start | bytes 1351688 | tf_op jit(solution)/shard_map/ppermute | solution.py:308
  21.5 0.0 copy-done
  21.5 0.0 copy-done.1
  21.5 1.3 %shard_map.75 = (bf16[440,440]{1,0:T(8,128)(2,1)S(1)}, bf16[440,440]{1,0:T(8,128)(2,1)S(1)}, bf16[440,440]{1,0:T(8,128)(2,1)S(1)}, bf16[440,440]{1,0:T(8,128)(2,1)S(1)}, bf16[32,256]{1,0:T(8,128)(2,1)S(1)}) custom-call(f32[55,55]{1,0:T(8,128)S(1)} %copy-done.1, s32[6,256]{1,0:T(8,128)S(1)} %copy-done), custom_call_target="tpu_custom_call" | custom-call | flops 100000000 | bytes 1000000 | tf_op jit(solution)/shard_map/pallas_call | solution.py:264
  22.8 1.2 %all-to-all-done.slots = f32[16,16,128]{2,1,0:T(8,128)S(1)} async-done(((f32[16,16,128]{2,1,0:T(8,128)}), f32[16,16,128]{2,1,0:T(8,128)S(1)}, u32[]{:S(2)}, u32[]{:S(2)}) %all-to-all-start) | async-done | bytes 131104 | tf_op jit(solution)/shard_map/all_to_all | solution.py:309
  24.0 0.5 shard_map.77
  24.5 2.5 %collective-permute-start.2 = (f32[16,440]{1,0:T(8,128)S(1)}, f32[16,440]{1,0:T(8,128)S(1)}, u32[]{:S(2)}, u32[]{:S(2)}) collective-permute-start(f32[16,440]{1,0:T(8,128)S(1)} %get-tuple-element.68), channel_id=1, source_target_pairs={{0,1},{1,2},{2,3},{3,4},{4,5},{5,6},{6,7},{7,64},{8,9},{9,10},{10,... | collective-permute-start | bytes 84488 | tf_op jit(solution)/shard_map/ppermute | solution.py:276
  27.0 1.1 %collective-permute-start.3 = (f32[16,440]{1,0:T(8,128)S(1)}, f32[16,440]{1,0:T(8,128)S(1)}, u32[]{:S(2)}, u32[]{:S(2)}) collective-permute-start(f32[16,440]{1,0:T(8,128)S(1)} %get-tuple-element.69), channel_id=1, source_target_pairs={{0,64},{1,65},{2,66},{3,67},{4,68},{5,69},{6,70},{7,71},{8,72},{9,... | collective-permute-start | bytes 84488 | tf_op jit(solution)/shard_map/ppermute | solution.py:276
  28.0 7.9 %collective-permute-start.4 = (f32[16,440]{1,0:T(8,128)S(1)}, f32[16,440]{1,0:T(8,128)S(1)}, u32[]{:S(2)}, u32[]{:S(2)}) collective-permute-start(f32[16,440]{1,0:T(8,128)S(1)} %get-tuple-element.70), channel_id=1, source_target_pairs={{0,119},{1,0},{2,1},{3,2},{4,3},{5,4},{6,5},{7,6},{8,127},{9,8},{1... | collective-permute-start | bytes 84488 | tf_op jit(solution)/shard_map/ppermute | solution.py:276
  36.0 2.2 %collective-permute-start.5 = (f32[16,440]{1,0:T(8,128)S(1)}, f32[16,440]{1,0:T(8,128)S(1)}, u32[]{:S(2)}, u32[]{:S(2)}) collective-permute-start(f32[16,440]{1,0:T(8,128)S(1)} %get-tuple-element.71), channel_id=1, source_target_pairs={{0,112},{1,113},{2,114},{3,115},{4,116},{5,117},{6,118},{7,119},{8... | collective-permute-start | bytes 84488 | tf_op jit(solution)/shard_map/ppermute | solution.py:276
  38.2 0.0 collective-permute-done.1.fields
  38.2 0.7 shard_map.76
  39.0 0.0 collective-permute-done.2.i0
  39.0 0.0 collective-permute-done.3.i1
  39.0 0.0 collective-permute-done.4.i2
  39.0 0.4 collective-permute-done.5.i3
  39.4 0.2 shard_map.78
  39.6 1.9 %collective-permute-start.6 = (f32[16,440]{1,0:T(8,128)S(1)}, f32[16,440]{1,0:T(8,128)S(1)}, u32[]{:S(2)}, u32[]{:S(2)}) collective-permute-start(f32[16,440]{1,0:T(8,128)S(1)} %get-tuple-element.75), channel_id=1, source_target_pairs={{0,1},{1,2},{2,3},{3,4},{4,5},{5,6},{6,7},{7,64},{8,9},{9,10},{10,... | collective-permute-start | bytes 84488 | tf_op jit(solution)/shard_map/ppermute | solution.py:276
  41.5 0.0 collective-permute-start.7
  41.6 4.9 %collective-permute-start.8 = (f32[16,440]{1,0:T(8,128)S(1)}, f32[16,440]{1,0:T(8,128)S(1)}, u32[]{:S(2)}, u32[]{:S(2)}) collective-permute-start(f32[16,440]{1,0:T(8,128)S(1)} %get-tuple-element.77), channel_id=1, source_target_pairs={{0,119},{1,0},{2,1},{3,2},{4,3},{5,4},{6,5},{7,6},{8,127},{9,8},{1... | collective-permute-start | bytes 84488 | tf_op jit(solution)/shard_map/ppermute | solution.py:276
  46.4 3.2 %collective-permute-start.9 = (f32[16,440]{1,0:T(8,128)S(1)}, f32[16,440]{1,0:T(8,128)S(1)}, u32[]{:S(2)}, u32[]{:S(2)}) collective-permute-start(f32[16,440]{1,0:T(8,128)S(1)} %get-tuple-element.78), channel_id=1, source_target_pairs={{0,112},{1,113},{2,114},{3,115},{4,116},{5,117},{6,118},{7,119},{8... | collective-permute-start | bytes 84488 | tf_op jit(solution)/shard_map/ppermute | solution.py:276
  49.6 0.8 shard_map.79
  50.4 0.0 collective-permute-done.6.i0
  50.5 0.0 collective-permute-done.7.i1
  50.5 0.0 collective-permute-done.8.i2
  50.5 0.2 collective-permute-done.9.i3
  50.7 0.2 shard_map.80
  50.9 1.9 %collective-permute-start.10 = (f32[16,440]{1,0:T(8,128)S(1)}, f32[16,440]{1,0:T(8,128)S(1)}, u32[]{:S(2)}, u32[]{:S(2)}) collective-permute-start(f32[16,440]{1,0:T(8,128)S(1)} %get-tuple-element.84), channel_id=1, source_target_pairs={{0,1},{1,2},{2,3},{3,4},{4,5},{5,6},{6,7},{7,64},{8,9},{9,10},{10,... | collective-permute-start | bytes 84488 | tf_op jit(solution)/shard_map/ppermute | solution.py:276
  52.8 0.0 collective-permute-start.11
  52.9 4.9 %collective-permute-start.12 = (f32[16,440]{1,0:T(8,128)S(1)}, f32[16,440]{1,0:T(8,128)S(1)}, u32[]{:S(2)}, u32[]{:S(2)}) collective-permute-start(f32[16,440]{1,0:T(8,128)S(1)} %get-tuple-element.86), channel_id=1, source_target_pairs={{0,119},{1,0},{2,1},{3,2},{4,3},{5,4},{6,5},{7,6},{8,127},{9,8},{1... | collective-permute-start | bytes 84488 | tf_op jit(solution)/shard_map/ppermute | solution.py:276
  57.7 3.5 %collective-permute-start.13 = (f32[16,440]{1,0:T(8,128)S(1)}, f32[16,440]{1,0:T(8,128)S(1)}, u32[]{:S(2)}, u32[]{:S(2)}) collective-permute-start(f32[16,440]{1,0:T(8,128)S(1)} %get-tuple-element.87), channel_id=1, source_target_pairs={{0,112},{1,113},{2,114},{3,115},{4,116},{5,117},{6,118},{7,119},{8... | collective-permute-start | bytes 84488 | tf_op jit(solution)/shard_map/ppermute | solution.py:276
  61.2 0.8 shard_map.81
  62.0 0.0 collective-permute-done.10.i0
  62.0 0.0 collective-permute-done.11.i1
  62.0 0.0 collective-permute-done.12.i2
  62.0 0.0 collective-permute-done.13.i3
  62.1 0.2 shard_map.82
  62.3 0.0 collective-permute-start.14
  62.3 1.6 %collective-permute-start.15 = (f32[16,440]{1,0:T(8,128)S(1)}, f32[16,440]{1,0:T(8,128)S(1)}, u32[]{:S(2)}, u32[]{:S(2)}) collective-permute-start(f32[16,440]{1,0:T(8,128)S(1)} %get-tuple-element.92), channel_id=1, source_target_pairs={{0,112},{1,113},{2,114},{3,115},{4,116},{5,117},{6,118},{7,119},{8... | collective-permute-start | bytes 84488 | tf_op jit(solution)/shard_map/ppermute | solution.py:348
  63.8 1.1 %shard_map.83.y = f32[440,256]{1,0:T(8,128)S(1)} custom-call(f32[440,256]{1,0:T(8,128)S(1)} %get-tuple-element.80.y, bf16[320,256]{1,0:T(8,128)(2,1)S(1)} %get-tuple-element.57.adj, f32[8,256]{1,0:T(8,128)S(1)} %get-tuple-element.63.rows, bf16[440,440]{1,0:T(8,128)(2,1)S(1)} %get-tuple-element.81.mix_high, bf16[440,440]{1,0:T(8,128)(2,1)S(1)} %get-tuple-element.82.mix_low, ...), custom_call_target="tpu_custom_call" | custom-call | flops 100000000 | bytes 1000000 | tf_op jit(solution)/shard_map/pallas_call | solution.py:264
  65.0 0.3 shard_map.85
  65.3 0.0 collective-permute-done.14.south
  65.3 0.9 %collective-permute-done.15.north = f32[16,440]{1,0:T(8,128)S(1)} collective-permute-done((f32[16,440]{1,0:T(8,128)S(1)}, f32[16,440]{1,0:T(8,128)S(1)}, u32[]{:S(2)}, u32[]{:S(2)}) %collective-permute-start.15) | collective-permute-done | bytes 28192 | tf_op jit(solution)/shard_map/ppermute | solution.py:348
  66.2 0.7 shard_map.84
  66.9 3.2 %collective-permute-start.16 = (f32[440,256]{1,0:T(8,128)S(1)}, f32[440,256]{1,0:T(8,128)S(1)}, u32[]{:S(2)}, u32[]{:S(2)}) collective-permute-start(f32[440,256]{1,0:T(8,128)S(1)} %shard_map.84), channel_id=1, source_target_pairs={{0,320},{1,321},{2,322},{3,323},{4,324},{5,325},{6,326},{7,327},{8... | collective-permute-start | bytes 1351688 | tf_op jit(solution)/shard_map/ppermute | solution.py:352
  70.1 2.8 %collective-permute-start.17 = (f32[16,440]{1,0:T(8,128)S(1)}, f32[16,440]{1,0:T(8,128)S(1)}, u32[]{:S(2)}, u32[]{:S(2)}) collective-permute-start(f32[16,440]{1,0:T(8,128)S(1)} %get-tuple-element.99), channel_id=1, source_target_pairs={{0,321},{1,322},{2,323},{3,324},{4,325},{5,326},{6,327},{7,328},{8... | collective-permute-start | bytes 84488 | tf_op jit(solution)/shard_map/ppermute | solution.py:353
  72.9 7.0 %collective-permute-start.18 = (f32[16,440]{1,0:T(8,128)S(1)}, f32[16,440]{1,0:T(8,128)S(1)}, u32[]{:S(2)}, u32[]{:S(2)}) collective-permute-start(f32[16,440]{1,0:T(8,128)S(1)} %get-tuple-element.100), channel_id=1, source_target_pairs={{0,383},{1,320},{2,321},{3,322},{4,323},{5,324},{6,325},{7,326},{8... | collective-permute-start | bytes 84488 | tf_op jit(solution)/shard_map/ppermute | solution.py:354
  80.6 2.9 %collective-permute-done.17.east = f32[16,440]{1,0:T(8,128)S(1)} collective-permute-done((f32[16,440]{1,0:T(8,128)S(1)}, f32[16,440]{1,0:T(8,128)S(1)}, u32[]{:S(2)}, u32[]{:S(2)}) %collective-permute-start.17) | collective-permute-done | bytes 28192 | tf_op jit(solution)/shard_map/ppermute | solution.py:353
  83.5 0.0 collective-permute-done.18.west
  83.5 0.7 collective-permute-done.16.y
  84.2 1.0 %shard_map.86 = f32[440,256]{1,0:T(8,128)} custom-call(s32[1]{0:T(128)S(6)} %copy.8.count, f32[440,256]{1,0:T(8,128)S(1)} %collective-permute-done.16.y, bf16[32,256]{1,0:T(8,128)(2,1)S(1)} %get-tuple-element.98.ghosts, f32[16,440]{1,0:T(8,128)S(1)} %collective-permute-done.17.east, f32[16,440]{1,0:T(8,128)S(1)} %collective-permute-done.18.west), custom_call_target="tpu_custom_call" | custom-call | flops 100000000 | bytes 1000000 | tf_op jit(solution)/shard_map/pallas_call | solution.py:264
Async XLA Ops:
  2.1 12.8 %collective-permute-start = (f32[72,440]{1,0:T(8,128)}, f32[72,440]{1,0:T(8,128)S(1)}, u32[]{:S(2)}, u32[]{:S(2)}) collective-permute-start(f32[72,440]{1,0:T(8,128)} %get-tuple-element.54), channel_id=1, source_target_pairs={{0,256},{1,257},{2,258},{3,259},{4,260},{5,261},{6,262},{7,263},{8... | collective-permute-start | bytes 380168 | tf_op jit(solution)/shard_map/ppermute | solution.py:306
  9.4 14.6 %all-to-all-start = ((f32[16,16,128]{2,1,0:T(8,128)}), f32[16,16,128]{2,1,0:T(8,128)S(1)}, u32[]{:S(2)}, u32[]{:S(2)}) async-start(f32[16,16,128]{2,1,0:T(8,128)} %get-tuple-element.53), calls=%async_computation | async-start | bytes 262144 | tf_op jit(solution)/shard_map/all_to_all | solution.py:309
  14.8 1.0 %copy-start.2 = (f32[8,55,256]{2,0,1:T(8,128)S(1)}, f32[8,55,256]{2,0,1:T(8,128)}, u32[]{:S(2)}) copy-start(f32[8,55,256]{2,0,1:T(8,128)} %param.7) | copy-start | bytes 1351684
  14.8 6.7 %copy-start = (s32[6,256]{1,0:T(8,128)S(1)}, s32[6,256]{1,0:T(8,128)}, u32[]{:S(2)}) copy-start(s32[6,256]{1,0:T(8,128)} %named.1) | copy-start | bytes 18436
  14.8 6.7 %copy-start.1 = (f32[55,55]{1,0:T(8,128)S(1)}, f32[55,55]{1,0:T(8,128)}, u32[]{:S(2)}) copy-start(f32[55,55]{1,0:T(8,128)} %vloc) | copy-start | bytes 36304
  15.8 22.4 %collective-permute-start.1 = (f32[440,256]{1,0:T(8,128)S(1)}, f32[440,256]{1,0:T(8,128)S(1)}, u32[]{:S(2)}, u32[]{:S(2)}) collective-permute-start(f32[440,256]{1,0:T(8,128)S(1)} %bitcast.12), channel_id=1, source_target_pairs={{0,256},{1,257},{2,258},{3,259},{4,260},{5,261},{6,262},{7,263},{8... | collective-permute-start | bytes 1351688 | tf_op jit(solution)/shard_map/ppermute | solution.py:308
  24.5 14.5 %collective-permute-start.2 = (f32[16,440]{1,0:T(8,128)S(1)}, f32[16,440]{1,0:T(8,128)S(1)}, u32[]{:S(2)}, u32[]{:S(2)}) collective-permute-start(f32[16,440]{1,0:T(8,128)S(1)} %get-tuple-element.68), channel_id=1, source_target_pairs={{0,1},{1,2},{2,3},{3,4},{4,5},{5,6},{6,7},{7,64},{8,9},{9,10},{10,... | collective-permute-start | bytes 84488 | tf_op jit(solution)/shard_map/ppermute | solution.py:276
  27.0 12.0 %collective-permute-start.3 = (f32[16,440]{1,0:T(8,128)S(1)}, f32[16,440]{1,0:T(8,128)S(1)}, u32[]{:S(2)}, u32[]{:S(2)}) collective-permute-start(f32[16,440]{1,0:T(8,128)S(1)} %get-tuple-element.69), channel_id=1, source_target_pairs={{0,64},{1,65},{2,66},{3,67},{4,68},{5,69},{6,70},{7,71},{8,72},{9,... | collective-permute-start | bytes 84488 | tf_op jit(solution)/shard_map/ppermute | solution.py:276
  28.0 10.9 %collective-permute-start.4 = (f32[16,440]{1,0:T(8,128)S(1)}, f32[16,440]{1,0:T(8,128)S(1)}, u32[]{:S(2)}, u32[]{:S(2)}) collective-permute-start(f32[16,440]{1,0:T(8,128)S(1)} %get-tuple-element.70), channel_id=1, source_target_pairs={{0,119},{1,0},{2,1},{3,2},{4,3},{5,4},{6,5},{7,6},{8,127},{9,8},{1... | collective-permute-start | bytes 84488 | tf_op jit(solution)/shard_map/ppermute | solution.py:276
  36.0 3.4 %collective-permute-start.5 = (f32[16,440]{1,0:T(8,128)S(1)}, f32[16,440]{1,0:T(8,128)S(1)}, u32[]{:S(2)}, u32[]{:S(2)}) collective-permute-start(f32[16,440]{1,0:T(8,128)S(1)} %get-tuple-element.71), channel_id=1, source_target_pairs={{0,112},{1,113},{2,114},{3,115},{4,116},{5,117},{6,118},{7,119},{8... | collective-permute-start | bytes 84488 | tf_op jit(solution)/shard_map/ppermute | solution.py:276
  39.6 10.8 %collective-permute-start.6 = (f32[16,440]{1,0:T(8,128)S(1)}, f32[16,440]{1,0:T(8,128)S(1)}, u32[]{:S(2)}, u32[]{:S(2)}) collective-permute-start(f32[16,440]{1,0:T(8,128)S(1)} %get-tuple-element.75), channel_id=1, source_target_pairs={{0,1},{1,2},{2,3},{3,4},{4,5},{5,6},{6,7},{7,64},{8,9},{9,10},{10,... | collective-permute-start | bytes 84488 | tf_op jit(solution)/shard_map/ppermute | solution.py:276
  41.5 8.9 %collective-permute-start.7 = (f32[16,440]{1,0:T(8,128)S(1)}, f32[16,440]{1,0:T(8,128)S(1)}, u32[]{:S(2)}, u32[]{:S(2)}) collective-permute-start(f32[16,440]{1,0:T(8,128)S(1)} %get-tuple-element.76), channel_id=1, source_target_pairs={{0,64},{1,65},{2,66},{3,67},{4,68},{5,69},{6,70},{7,71},{8,72},{9,... | collective-permute-start | bytes 84488 | tf_op jit(solution)/shard_map/ppermute | solution.py:276
  41.6 8.9 %collective-permute-start.8 = (f32[16,440]{1,0:T(8,128)S(1)}, f32[16,440]{1,0:T(8,128)S(1)}, u32[]{:S(2)}, u32[]{:S(2)}) collective-permute-start(f32[16,440]{1,0:T(8,128)S(1)} %get-tuple-element.77), channel_id=1, source_target_pairs={{0,119},{1,0},{2,1},{3,2},{4,3},{5,4},{6,5},{7,6},{8,127},{9,8},{1... | collective-permute-start | bytes 84488 | tf_op jit(solution)/shard_map/ppermute | solution.py:276
  46.4 4.3 %collective-permute-start.9 = (f32[16,440]{1,0:T(8,128)S(1)}, f32[16,440]{1,0:T(8,128)S(1)}, u32[]{:S(2)}, u32[]{:S(2)}) collective-permute-start(f32[16,440]{1,0:T(8,128)S(1)} %get-tuple-element.78), channel_id=1, source_target_pairs={{0,112},{1,113},{2,114},{3,115},{4,116},{5,117},{6,118},{7,119},{8... | collective-permute-start | bytes 84488 | tf_op jit(solution)/shard_map/ppermute | solution.py:276
  50.9 11.1 %collective-permute-start.10 = (f32[16,440]{1,0:T(8,128)S(1)}, f32[16,440]{1,0:T(8,128)S(1)}, u32[]{:S(2)}, u32[]{:S(2)}) collective-permute-start(f32[16,440]{1,0:T(8,128)S(1)} %get-tuple-element.84), channel_id=1, source_target_pairs={{0,1},{1,2},{2,3},{3,4},{4,5},{5,6},{6,7},{7,64},{8,9},{9,10},{10,... | collective-permute-start | bytes 84488 | tf_op jit(solution)/shard_map/ppermute | solution.py:276
  52.8 9.2 %collective-permute-start.11 = (f32[16,440]{1,0:T(8,128)S(1)}, f32[16,440]{1,0:T(8,128)S(1)}, u32[]{:S(2)}, u32[]{:S(2)}) collective-permute-start(f32[16,440]{1,0:T(8,128)S(1)} %get-tuple-element.85), channel_id=1, source_target_pairs={{0,64},{1,65},{2,66},{3,67},{4,68},{5,69},{6,70},{7,71},{8,72},{9,... | collective-permute-start | bytes 84488 | tf_op jit(solution)/shard_map/ppermute | solution.py:276
  52.9 9.2 %collective-permute-start.12 = (f32[16,440]{1,0:T(8,128)S(1)}, f32[16,440]{1,0:T(8,128)S(1)}, u32[]{:S(2)}, u32[]{:S(2)}) collective-permute-start(f32[16,440]{1,0:T(8,128)S(1)} %get-tuple-element.86), channel_id=1, source_target_pairs={{0,119},{1,0},{2,1},{3,2},{4,3},{5,4},{6,5},{7,6},{8,127},{9,8},{1... | collective-permute-start | bytes 84488 | tf_op jit(solution)/shard_map/ppermute | solution.py:276
  57.7 4.3 %collective-permute-start.13 = (f32[16,440]{1,0:T(8,128)S(1)}, f32[16,440]{1,0:T(8,128)S(1)}, u32[]{:S(2)}, u32[]{:S(2)}) collective-permute-start(f32[16,440]{1,0:T(8,128)S(1)} %get-tuple-element.87), channel_id=1, source_target_pairs={{0,112},{1,113},{2,114},{3,115},{4,116},{5,117},{6,118},{7,119},{8... | collective-permute-start | bytes 84488 | tf_op jit(solution)/shard_map/ppermute | solution.py:276
  62.3 3.0 %collective-permute-start.14 = (f32[16,440]{1,0:T(8,128)S(1)}, f32[16,440]{1,0:T(8,128)S(1)}, u32[]{:S(2)}, u32[]{:S(2)}) collective-permute-start(f32[16,440]{1,0:T(8,128)S(1)} %get-tuple-element.91), channel_id=1, source_target_pairs={{0,64},{1,65},{2,66},{3,67},{4,68},{5,69},{6,70},{7,71},{8,72},{9,... | collective-permute-start | bytes 84488 | tf_op jit(solution)/shard_map/ppermute | solution.py:347
  62.3 3.9 %collective-permute-start.15 = (f32[16,440]{1,0:T(8,128)S(1)}, f32[16,440]{1,0:T(8,128)S(1)}, u32[]{:S(2)}, u32[]{:S(2)}) collective-permute-start(f32[16,440]{1,0:T(8,128)S(1)} %get-tuple-element.92), channel_id=1, source_target_pairs={{0,112},{1,113},{2,114},{3,115},{4,116},{5,117},{6,118},{7,119},{8... | collective-permute-start | bytes 84488 | tf_op jit(solution)/shard_map/ppermute | solution.py:348
  66.9 17.3 %collective-permute-start.16 = (f32[440,256]{1,0:T(8,128)S(1)}, f32[440,256]{1,0:T(8,128)S(1)}, u32[]{:S(2)}, u32[]{:S(2)}) collective-permute-start(f32[440,256]{1,0:T(8,128)S(1)} %shard_map.84), channel_id=1, source_target_pairs={{0,320},{1,321},{2,322},{3,323},{4,324},{5,325},{6,326},{7,327},{8... | collective-permute-start | bytes 1351688 | tf_op jit(solution)/shard_map/ppermute | solution.py:352
  70.1 13.3 %collective-permute-start.17 = (f32[16,440]{1,0:T(8,128)S(1)}, f32[16,440]{1,0:T(8,128)S(1)}, u32[]{:S(2)}, u32[]{:S(2)}) collective-permute-start(f32[16,440]{1,0:T(8,128)S(1)} %get-tuple-element.99), channel_id=1, source_target_pairs={{0,321},{1,322},{2,323},{3,324},{4,325},{5,326},{6,327},{7,328},{8... | collective-permute-start | bytes 84488 | tf_op jit(solution)/shard_map/ppermute | solution.py:353
  72.9 10.6 %collective-permute-start.18 = (f32[16,440]{1,0:T(8,128)S(1)}, f32[16,440]{1,0:T(8,128)S(1)}, u32[]{:S(2)}, u32[]{:S(2)}) collective-permute-start(f32[16,440]{1,0:T(8,128)S(1)} %get-tuple-element.100), channel_id=1, source_target_pairs={{0,383},{1,320},{2,321},{3,322},{4,323},{5,324},{6,325},{7,326},{8... | collective-permute-start | bytes 84488 | tf_op jit(solution)/shard_map/ppermute | solution.py:354

commit v7 on v5

--- a/solution.py
+++ b/solution.py
@@ -47,8 +47,9 @@
 WEST = sorted((b, a) for a, b in EAST)
 SOUTH = pairs(lambda x, yh, l, z, core: (x + core, yh, l, z, 1 - core))
 NORTH = sorted((b, a) for a, b in SOUTH)
-ROUTES = (EAST, SOUTH, WEST, NORTH)
-ORDER = (0, 2, 1, 3)
+ROUTES = (SOUTH, EAST, WEST, NORTH)
+ORDER = (2, 0, 1, 3)
+PLACE = (1, 2, 0, 3)
 HOME = dict(BACK)
 
 
@@ -143,7 +144,7 @@
 
 
 def joined(arrived):
-    return jnp.concatenate([arrived[d][...] for d in ORDER], axis=0)
+    return jnp.concatenate([arrived[d][...] for d in PLACE], axis=0)
 
 
 def spread():
@@ -329,7 +330,7 @@
         *rims, came = call(rim_kernel, rim_shapes + [border], (b, gsel, ksel, *came))
         y, b = call(stay_kernel, [state, border], (y, adj, sel, rows, came))
         came = exchange(rims)
-    east, south, west, north, came = call(
+    south, east, west, north, came = call(
         rim_kernel, rim_shapes + [border], (b, gsel, ksel, *came)
     )
     (y,) = call(last_stay_kernel, [state], (y, adj, rows, mix_high, mix_low, came))

time: 86.6 us -> 86.6 us (level)
  no operation moved by 1% of the time
where the time goes in v7:
time: 86.6 us; the launch traced here: 85.2 us
  starting transfers between devices  67.2 us (78%)
  Pallas kernels  10.7 us (12%)
  waiting for transfers between devices  5.92 us (7%)
  between operations  0.99 us (1%)
    ppermute x12, starting transfers between devices, exchange(): return [lax.ppermute(rim, AXES, route) for rim, route in zip(rims, ROUTES)]  34 us
    pallas_call x14, Pallas kernels, call(): pl.pallas_call(kernel, out_shape=[jax.ShapeDtypeStruct(s, t) for s, t in...  10.7 us
    ppermute x1, starting transfers between devices, local(): load = lax.ppermute(load, AXES, GO)  7.27 us
    ppermute x1, starting transfers between devices, local(): west = lax.ppermute(west, AXES, homeward(WEST))  6.83 us
    ppermute x1, starting transfers between devices, local(): fields = lax.ppermute(fields, AXES, GO)  5.64 us
    all_to_all x1, starting transfers between devices, local(): slots = lax.all_to_all(slots, ('yh', 'member'), 0, 0)  5.46 us
    ppermute x1, starting transfers between devices, local(): y = lax.ppermute(y, AXES, BACK)  3.4 us
    ppermute x1, starting transfers between devices, local(): east = lax.ppermute(east, AXES, homeward(EAST))  2.96 us
  transfers between devices with their start and end apart: 20, of which 6 were waited for; matrix products, arithmetic and copies ran while one was open for 0% of the time, Pallas kernels for 7%

profile of v7, /device:TPU:1, one launch (start us, length us, event | category | flops | bytes accessed | tf_op | source)
XLA Modules:
  0.0 85.2 jit_solution(4171982626783215486)
XLA Ops:
  0.0 2.2 %shard_map.73 = (f32[16,16,128]{2,1,0:T(8,128)}, f32[72,440]{1,0:T(8,128)}) custom-call(f32[32,55]{1,0:T(8,128)} %bitcast.13, f32[440,256]{1,0:T(8,128)} %bitcast.11, f32[1,256]{1,0:T(1,128)} %bitcast.14, s32[6,256]{1,0:T(8,128)} %named.1, s32[4,16]{1,0:T(4,128)} %sends_in.1), custom_call_target="tpu_custom_call" | custom-call | flops 100000000 | bytes 1000000 | tf_op jit(solution)/shard_map/pallas_call | solution.py:254
  2.2 7.3 %collective-permute-start = (f32[72,440]{1,0:T(8,128)}, f32[72,440]{1,0:T(8,128)S(1)}, u32[]{:S(2)}, u32[]{:S(2)}) collective-permute-start(f32[72,440]{1,0:T(8,128)} %get-tuple-element.54), channel_id=1, source_target_pairs={{0,256},{1,257},{2,258},{3,259},{4,260},{5,261},{6,262},{7,263},{8... | collective-permute-start | bytes 380168 | tf_op jit(solution)/shard_map/ppermute | solution.py:296
  9.5 5.5 %all-to-all-start = ((f32[16,16,128]{2,1,0:T(8,128)}), f32[16,16,128]{2,1,0:T(8,128)S(1)}, u32[]{:S(2)}, u32[]{:S(2)}) async-start(f32[16,16,128]{2,1,0:T(8,128)} %get-tuple-element.53), calls=%async_computation | async-start | bytes 262144 | tf_op jit(solution)/shard_map/all_to_all | solution.py:299
  14.9 0.0 copy-start.2
  14.9 0.0 copy-start
  14.9 0.0 copy-start.1
  14.9 0.0 collective-permute-done.load
  15.0 0.6 shard_map.74
  15.5 0.4 copy-done.2
  15.9 5.6 %collective-permute-start.1 = (f32[440,256]{1,0:T(8,128)S(1)}, f32[440,256]{1,0:T(8,128)S(1)}, u32[]{:S(2)}, u32[]{:S(2)}) collective-permute-start(f32[440,256]{1,0:T(8,128)S(1)} %bitcast.12), channel_id=1, source_target_pairs={{0,256},{1,257},{2,258},{3,259},{4,260},{5,261},{6,262},{7,263},{8... | collective-permute-start | bytes 1351688 | tf_op jit(solution)/shard_map/ppermute | solution.py:298
  21.6 0.0 copy-done
  21.6 0.0 copy-done.1
  21.6 1.3 %shard_map.75 = (bf16[440,440]{1,0:T(8,128)(2,1)S(1)}, bf16[440,440]{1,0:T(8,128)(2,1)S(1)}, bf16[440,440]{1,0:T(8,128)(2,1)S(1)}, bf16[440,440]{1,0:T(8,128)(2,1)S(1)}, bf16[32,256]{1,0:T(8,128)(2,1)S(1)}) custom-call(f32[55,55]{1,0:T(8,128)S(1)} %copy-done.1, s32[6,256]{1,0:T(8,128)S(1)} %copy-done), custom_call_target="tpu_custom_call" | custom-call | flops 100000000 | bytes 1000000 | tf_op jit(solution)/shard_map/pallas_call | solution.py:254
  22.9 1.2 %all-to-all-done.slots = f32[16,16,128]{2,1,0:T(8,128)S(1)} async-done(((f32[16,16,128]{2,1,0:T(8,128)}), f32[16,16,128]{2,1,0:T(8,128)S(1)}, u32[]{:S(2)}, u32[]{:S(2)}) %all-to-all-start) | async-done | bytes 131104 | tf_op jit(solution)/shard_map/all_to_all | solution.py:299
  24.1 0.5 shard_map.77
  24.6 0.0 collective-permute-start.2
  24.6 3.2 %collective-permute-start.3 = (f32[16,440]{1,0:T(8,128)S(1)}, f32[16,440]{1,0:T(8,128)S(1)}, u32[]{:S(2)}, u32[]{:S(2)}) collective-permute-start(f32[16,440]{1,0:T(8,128)S(1)} %get-tuple-element.69), channel_id=1, source_target_pairs={{0,1},{1,2},{2,3},{3,4},{4,5},{5,6},{6,7},{7,64},{8,9},{9,10},{10,... | collective-permute-start | bytes 84488 | tf_op jit(solution)/shard_map/ppermute | solution.py:266
  27.8 8.2 %collective-permute-start.4 = (f32[16,440]{1,0:T(8,128)S(1)}, f32[16,440]{1,0:T(8,128)S(1)}, u32[]{:S(2)}, u32[]{:S(2)}) collective-permute-start(f32[16,440]{1,0:T(8,128)S(1)} %get-tuple-element.70), channel_id=1, source_target_pairs={{0,119},{1,0},{2,1},{3,2},{4,3},{5,4},{6,5},{7,6},{8,127},{9,8},{1... | collective-permute-start | bytes 84488 | tf_op jit(solution)/shard_map/ppermute | solution.py:266
  36.1 2.2 %collective-permute-start.5 = (f32[16,440]{1,0:T(8,128)S(1)}, f32[16,440]{1,0:T(8,128)S(1)}, u32[]{:S(2)}, u32[]{:S(2)}) collective-permute-start(f32[16,440]{1,0:T(8,128)S(1)} %get-tuple-element.71), channel_id=1, source_target_pairs={{0,112},{1,113},{2,114},{3,115},{4,116},{5,117},{6,118},{7,119},{8... | collective-permute-start | bytes 84488 | tf_op jit(solution)/shard_map/ppermute | solution.py:266
  38.3 0.0 collective-permute-done.1.fields
  38.3 0.7 shard_map.76
  39.1 0.0 collective-permute-done.2.i0
  39.1 0.0 collective-permute-done.3.i1
  39.1 0.0 collective-permute-done.4.i2
  39.1 0.4 collective-permute-done.5.i3
  39.5 0.2 shard_map.78
  39.7 0.0 collective-permute-start.6
  39.7 1.9 %collective-permute-start.7 = (f32[16,440]{1,0:T(8,128)S(1)}, f32[16,440]{1,0:T(8,128)S(1)}, u32[]{:S(2)}, u32[]{:S(2)}) collective-permute-start(f32[16,440]{1,0:T(8,128)S(1)} %get-tuple-element.76), channel_id=1, source_target_pairs={{0,1},{1,2},{2,3},{3,4},{4,5},{5,6},{6,7},{7,64},{8,9},{9,10},{10,... | collective-permute-start | bytes 84488 | tf_op jit(solution)/shard_map/ppermute | solution.py:266
  41.7 4.9 %collective-permute-start.8 = (f32[16,440]{1,0:T(8,128)S(1)}, f32[16,440]{1,0:T(8,128)S(1)}, u32[]{:S(2)}, u32[]{:S(2)}) collective-permute-start(f32[16,440]{1,0:T(8,128)S(1)} %get-tuple-element.77), channel_id=1, source_target_pairs={{0,119},{1,0},{2,1},{3,2},{4,3},{5,4},{6,5},{7,6},{8,127},{9,8},{1... | collective-permute-start | bytes 84488 | tf_op jit(solution)/shard_map/ppermute | solution.py:266
  46.5 3.2 %collective-permute-start.9 = (f32[16,440]{1,0:T(8,128)S(1)}, f32[16,440]{1,0:T(8,128)S(1)}, u32[]{:S(2)}, u32[]{:S(2)}) collective-permute-start(f32[16,440]{1,0:T(8,128)S(1)} %get-tuple-element.78), channel_id=1, source_target_pairs={{0,112},{1,113},{2,114},{3,115},{4,116},{5,117},{6,118},{7,119},{8... | collective-permute-start | bytes 84488 | tf_op jit(solution)/shard_map/ppermute | solution.py:266
  49.7 0.8 shard_map.79
  50.5 0.0 collective-permute-done.6.i0
  50.6 0.0 collective-permute-done.7.i1
  50.6 0.0 collective-permute-done.8.i2
  50.6 0.1 collective-permute-done.9.i3
  50.6 0.2 shard_map.80
  50.8 0.0 collective-permute-start.10
  50.9 1.9 %collective-permute-start.11 = (f32[16,440]{1,0:T(8,128)S(1)}, f32[16,440]{1,0:T(8,128)S(1)}, u32[]{:S(2)}, u32[]{:S(2)}) collective-permute-start(f32[16,440]{1,0:T(8,128)S(1)} %get-tuple-element.85), channel_id=1, source_target_pairs={{0,1},{1,2},{2,3},{3,4},{4,5},{5,6},{6,7},{7,64},{8,9},{9,10},{10,... | collective-permute-start | bytes 84488 | tf_op jit(solution)/shard_map/ppermute | solution.py:266
  52.8 4.9 %collective-permute-start.12 = (f32[16,440]{1,0:T(8,128)S(1)}, f32[16,440]{1,0:T(8,128)S(1)}, u32[]{:S(2)}, u32[]{:S(2)}) collective-permute-start(f32[16,440]{1,0:T(8,128)S(1)} %get-tuple-element.86), channel_id=1, source_target_pairs={{0,119},{1,0},{2,1},{3,2},{4,3},{5,4},{6,5},{7,6},{8,127},{9,8},{1... | collective-permute-start | bytes 84488 | tf_op jit(solution)/shard_map/ppermute | solution.py:266
  57.6 3.6 %collective-permute-start.13 = (f32[16,440]{1,0:T(8,128)S(1)}, f32[16,440]{1,0:T(8,128)S(1)}, u32[]{:S(2)}, u32[]{:S(2)}) collective-permute-start(f32[16,440]{1,0:T(8,128)S(1)} %get-tuple-element.87), channel_id=1, source_target_pairs={{0,112},{1,113},{2,114},{3,115},{4,116},{5,117},{6,118},{7,119},{8... | collective-permute-start | bytes 84488 | tf_op jit(solution)/shard_map/ppermute | solution.py:266
  61.3 0.8 shard_map.81
  62.1 0.0 collective-permute-done.10.i0
  62.1 0.0 collective-permute-done.11.i1
  62.1 0.0 collective-permute-done.12.i2
  62.1 0.0 collective-permute-done.13.i3
  62.2 0.2 shard_map.82
  62.4 0.0 collective-permute-start.14
  62.4 1.6 %collective-permute-start.15 = (f32[16,440]{1,0:T(8,128)S(1)}, f32[16,440]{1,0:T(8,128)S(1)}, u32[]{:S(2)}, u32[]{:S(2)}) collective-permute-start(f32[16,440]{1,0:T(8,128)S(1)} %get-tuple-element.92), channel_id=1, source_target_pairs={{0,112},{1,113},{2,114},{3,115},{4,116},{5,117},{6,118},{7,119},{8... | collective-permute-start | bytes 84488 | tf_op jit(solution)/shard_map/ppermute | solution.py:338
  63.9 1.1 %shard_map.83.y = f32[440,256]{1,0:T(8,128)S(1)} custom-call(f32[440,256]{1,0:T(8,128)S(1)} %get-tuple-element.80.y, bf16[320,256]{1,0:T(8,128)(2,1)S(1)} %get-tuple-element.57.adj, f32[8,256]{1,0:T(8,128)S(1)} %get-tuple-element.63.rows, bf16[440,440]{1,0:T(8,128)(2,1)S(1)} %get-tuple-element.81.mix_high, bf16[440,440]{1,0:T(8,128)(2,1)S(1)} %get-tuple-element.82.mix_low, ...), custom_call_target="tpu_custom_call" | custom-call | flops 100000000 | bytes 1000000 | tf_op jit(solution)/shard_map/pallas_call | solution.py:254
  65.1 0.3 shard_map.85
  65.4 0.0 collective-permute-done.14.south
  65.4 0.6 collective-permute-done.15.north
  66.0 0.7 shard_map.84
  66.7 3.4 %collective-permute-start.16 = (f32[440,256]{1,0:T(8,128)S(1)}, f32[440,256]{1,0:T(8,128)S(1)}, u32[]{:S(2)}, u32[]{:S(2)}) collective-permute-start(f32[440,256]{1,0:T(8,128)S(1)} %shard_map.84), channel_id=1, source_target_pairs={{0,320},{1,321},{2,322},{3,323},{4,324},{5,325},{6,326},{7,327},{8... | collective-permute-start | bytes 1351688 | tf_op jit(solution)/shard_map/ppermute | solution.py:342
  70.1 3.0 %collective-permute-start.17 = (f32[16,440]{1,0:T(8,128)S(1)}, f32[16,440]{1,0:T(8,128)S(1)}, u32[]{:S(2)}, u32[]{:S(2)}) collective-permute-start(f32[16,440]{1,0:T(8,128)S(1)} %get-tuple-element.99), channel_id=1, source_target_pairs={{0,321},{1,322},{2,323},{3,324},{4,325},{5,326},{6,327},{7,328},{8... | collective-permute-start | bytes 84488 | tf_op jit(solution)/shard_map/ppermute | solution.py:343
  73.0 6.8 %collective-permute-start.18 = (f32[16,440]{1,0:T(8,128)S(1)}, f32[16,440]{1,0:T(8,128)S(1)}, u32[]{:S(2)}, u32[]{:S(2)}) collective-permute-start(f32[16,440]{1,0:T(8,128)S(1)} %get-tuple-element.100), channel_id=1, source_target_pairs={{0,383},{1,320},{2,321},{3,322},{4,323},{5,324},{6,325},{7,326},{8... | collective-permute-start | bytes 84488 | tf_op jit(solution)/shard_map/ppermute | solution.py:344
  80.5 2.9 %collective-permute-done.17.east = f32[16,440]{1,0:T(8,128)S(1)} collective-permute-done((f32[16,440]{1,0:T(8,128)S(1)}, f32[16,440]{1,0:T(8,128)S(1)}, u32[]{:S(2)}, u32[]{:S(2)}) %collective-permute-start.17) | collective-permute-done | bytes 28192 | tf_op jit(solution)/shard_map/ppermute | solution.py:343
  83.4 0.0 collective-permute-done.18.west
  83.4 0.7 collective-permute-done.16.y
  84.1 1.1 %shard_map.86 = f32[440,256]{1,0:T(8,128)} custom-call(s32[1]{0:T(128)S(6)} %copy.8.count, f32[440,256]{1,0:T(8,128)S(1)} %collective-permute-done.16.y, bf16[32,256]{1,0:T(8,128)(2,1)S(1)} %get-tuple-element.98.ghosts, f32[16,440]{1,0:T(8,128)S(1)} %collective-permute-done.17.east, f32[16,440]{1,0:T(8,128)S(1)} %collective-permute-done.18.west), custom_call_target="tpu_custom_call" | custom-call | flops 100000000 | bytes 1000000 | tf_op jit(solution)/shard_map/pallas_call | solution.py:254
Async XLA Ops:
  2.2 12.8 %collective-permute-start = (f32[72,440]{1,0:T(8,128)}, f32[72,440]{1,0:T(8,128)S(1)}, u32[]{:S(2)}, u32[]{:S(2)}) collective-permute-start(f32[72,440]{1,0:T(8,128)} %get-tuple-element.54), channel_id=1, source_target_pairs={{0,256},{1,257},{2,258},{3,259},{4,260},{5,261},{6,262},{7,263},{8... | collective-permute-start | bytes 380168 | tf_op jit(solution)/shard_map/ppermute | solution.py:296
  9.5 14.6 %all-to-all-start = ((f32[16,16,128]{2,1,0:T(8,128)}), f32[16,16,128]{2,1,0:T(8,128)S(1)}, u32[]{:S(2)}, u32[]{:S(2)}) async-start(f32[16,16,128]{2,1,0:T(8,128)} %get-tuple-element.53), calls=%async_computation | async-start | bytes 262144 | tf_op jit(solution)/shard_map/all_to_all | solution.py:299
  14.9 1.0 %copy-start.2 = (f32[8,55,256]{2,0,1:T(8,128)S(1)}, f32[8,55,256]{2,0,1:T(8,128)}, u32[]{:S(2)}) copy-start(f32[8,55,256]{2,0,1:T(8,128)} %param.7) | copy-start | bytes 1351684
  14.9 6.7 %copy-start = (s32[6,256]{1,0:T(8,128)S(1)}, s32[6,256]{1,0:T(8,128)}, u32[]{:S(2)}) copy-start(s32[6,256]{1,0:T(8,128)} %named.1) | copy-start | bytes 18436
  14.9 6.7 %copy-start.1 = (f32[55,55]{1,0:T(8,128)S(1)}, f32[55,55]{1,0:T(8,128)}, u32[]{:S(2)}) copy-start(f32[55,55]{1,0:T(8,128)} %vloc) | copy-start | bytes 36304
  15.9 22.4 %collective-permute-start.1 = (f32[440,256]{1,0:T(8,128)S(1)}, f32[440,256]{1,0:T(8,128)S(1)}, u32[]{:S(2)}, u32[]{:S(2)}) collective-permute-start(f32[440,256]{1,0:T(8,128)S(1)} %bitcast.12), channel_id=1, source_target_pairs={{0,256},{1,257},{2,258},{3,259},{4,260},{5,261},{6,262},{7,263},{8... | collective-permute-start | bytes 1351688 | tf_op jit(solution)/shard_map/ppermute | solution.py:298
  24.6 14.5 %collective-permute-start.2 = (f32[16,440]{1,0:T(8,128)S(1)}, f32[16,440]{1,0:T(8,128)S(1)}, u32[]{:S(2)}, u32[]{:S(2)}) collective-permute-start(f32[16,440]{1,0:T(8,128)S(1)} %get-tuple-element.68), channel_id=1, source_target_pairs={{0,64},{1,65},{2,66},{3,67},{4,68},{5,69},{6,70},{7,71},{8,72},{9,... | collective-permute-start | bytes 84488 | tf_op jit(solution)/shard_map/ppermute | solution.py:266
  24.6 14.5 %collective-permute-start.3 = (f32[16,440]{1,0:T(8,128)S(1)}, f32[16,440]{1,0:T(8,128)S(1)}, u32[]{:S(2)}, u32[]{:S(2)}) collective-permute-start(f32[16,440]{1,0:T(8,128)S(1)} %get-tuple-element.69), channel_id=1, source_target_pairs={{0,1},{1,2},{2,3},{3,4},{4,5},{5,6},{6,7},{7,64},{8,9},{9,10},{10,... | collective-permute-start | bytes 84488 | tf_op jit(solution)/shard_map/ppermute | solution.py:266
  27.8 11.2 %collective-permute-start.4 = (f32[16,440]{1,0:T(8,128)S(1)}, f32[16,440]{1,0:T(8,128)S(1)}, u32[]{:S(2)}, u32[]{:S(2)}) collective-permute-start(f32[16,440]{1,0:T(8,128)S(1)} %get-tuple-element.70), channel_id=1, source_target_pairs={{0,119},{1,0},{2,1},{3,2},{4,3},{5,4},{6,5},{7,6},{8,127},{9,8},{1... | collective-permute-start | bytes 84488 | tf_op jit(solution)/shard_map/ppermute | solution.py:266
  36.1 3.4 %collective-permute-start.5 = (f32[16,440]{1,0:T(8,128)S(1)}, f32[16,440]{1,0:T(8,128)S(1)}, u32[]{:S(2)}, u32[]{:S(2)}) collective-permute-start(f32[16,440]{1,0:T(8,128)S(1)} %get-tuple-element.71), channel_id=1, source_target_pairs={{0,112},{1,113},{2,114},{3,115},{4,116},{5,117},{6,118},{7,119},{8... | collective-permute-start | bytes 84488 | tf_op jit(solution)/shard_map/ppermute | solution.py:266
  39.7 10.8 %collective-permute-start.6 = (f32[16,440]{1,0:T(8,128)S(1)}, f32[16,440]{1,0:T(8,128)S(1)}, u32[]{:S(2)}, u32[]{:S(2)}) collective-permute-start(f32[16,440]{1,0:T(8,128)S(1)} %get-tuple-element.75), channel_id=1, source_target_pairs={{0,64},{1,65},{2,66},{3,67},{4,68},{5,69},{6,70},{7,71},{8,72},{9,... | collective-permute-start | bytes 84488 | tf_op jit(solution)/shard_map/ppermute | solution.py:266
  39.7 10.8 %collective-permute-start.7 = (f32[16,440]{1,0:T(8,128)S(1)}, f32[16,440]{1,0:T(8,128)S(1)}, u32[]{:S(2)}, u32[]{:S(2)}) collective-permute-start(f32[16,440]{1,0:T(8,128)S(1)} %get-tuple-element.76), channel_id=1, source_target_pairs={{0,1},{1,2},{2,3},{3,4},{4,5},{5,6},{6,7},{7,64},{8,9},{9,10},{10,... | collective-permute-start | bytes 84488 | tf_op jit(solution)/shard_map/ppermute | solution.py:266
  41.7 8.9 %collective-permute-start.8 = (f32[16,440]{1,0:T(8,128)S(1)}, f32[16,440]{1,0:T(8,128)S(1)}, u32[]{:S(2)}, u32[]{:S(2)}) collective-permute-start(f32[16,440]{1,0:T(8,128)S(1)} %get-tuple-element.77), channel_id=1, source_target_pairs={{0,119},{1,0},{2,1},{3,2},{4,3},{5,4},{6,5},{7,6},{8,127},{9,8},{1... | collective-permute-start | bytes 84488 | tf_op jit(solution)/shard_map/ppermute | solution.py:266
  46.5 4.1 %collective-permute-start.9 = (f32[16,440]{1,0:T(8,128)S(1)}, f32[16,440]{1,0:T(8,128)S(1)}, u32[]{:S(2)}, u32[]{:S(2)}) collective-permute-start(f32[16,440]{1,0:T(8,128)S(1)} %get-tuple-element.78), channel_id=1, source_target_pairs={{0,112},{1,113},{2,114},{3,115},{4,116},{5,117},{6,118},{7,119},{8... | collective-permute-start | bytes 84488 | tf_op jit(solution)/shard_map/ppermute | solution.py:266
  50.8 11.3 %collective-permute-start.10 = (f32[16,440]{1,0:T(8,128)S(1)}, f32[16,440]{1,0:T(8,128)S(1)}, u32[]{:S(2)}, u32[]{:S(2)}) collective-permute-start(f32[16,440]{1,0:T(8,128)S(1)} %get-tuple-element.84), channel_id=1, source_target_pairs={{0,64},{1,65},{2,66},{3,67},{4,68},{5,69},{6,70},{7,71},{8,72},{9,... | collective-permute-start | bytes 84488 | tf_op jit(solution)/shard_map/ppermute | solution.py:266
  50.9 11.3 %collective-permute-start.11 = (f32[16,440]{1,0:T(8,128)S(1)}, f32[16,440]{1,0:T(8,128)S(1)}, u32[]{:S(2)}, u32[]{:S(2)}) collective-permute-start(f32[16,440]{1,0:T(8,128)S(1)} %get-tuple-element.85), channel_id=1, source_target_pairs={{0,1},{1,2},{2,3},{3,4},{4,5},{5,6},{6,7},{7,64},{8,9},{9,10},{10,... | collective-permute-start | bytes 84488 | tf_op jit(solution)/shard_map/ppermute | solution.py:266
  52.8 9.4 %collective-permute-start.12 = (f32[16,440]{1,0:T(8,128)S(1)}, f32[16,440]{1,0:T(8,128)S(1)}, u32[]{:S(2)}, u32[]{:S(2)}) collective-permute-start(f32[16,440]{1,0:T(8,128)S(1)} %get-tuple-element.86), channel_id=1, source_target_pairs={{0,119},{1,0},{2,1},{3,2},{4,3},{5,4},{6,5},{7,6},{8,127},{9,8},{1... | collective-permute-start | bytes 84488 | tf_op jit(solution)/shard_map/ppermute | solution.py:266
  57.6 4.5 %collective-permute-start.13 = (f32[16,440]{1,0:T(8,128)S(1)}, f32[16,440]{1,0:T(8,128)S(1)}, u32[]{:S(2)}, u32[]{:S(2)}) collective-permute-start(f32[16,440]{1,0:T(8,128)S(1)} %get-tuple-element.87), channel_id=1, source_target_pairs={{0,112},{1,113},{2,114},{3,115},{4,116},{5,117},{6,118},{7,119},{8... | collective-permute-start | bytes 84488 | tf_op jit(solution)/shard_map/ppermute | solution.py:266
  62.4 3.0 %collective-permute-start.14 = (f32[16,440]{1,0:T(8,128)S(1)}, f32[16,440]{1,0:T(8,128)S(1)}, u32[]{:S(2)}, u32[]{:S(2)}) collective-permute-start(f32[16,440]{1,0:T(8,128)S(1)} %get-tuple-element.91), channel_id=1, source_target_pairs={{0,64},{1,65},{2,66},{3,67},{4,68},{5,69},{6,70},{7,71},{8,72},{9,... | collective-permute-start | bytes 84488 | tf_op jit(solution)/shard_map/ppermute | solution.py:337
  62.4 3.6 %collective-permute-start.15 = (f32[16,440]{1,0:T(8,128)S(1)}, f32[16,440]{1,0:T(8,128)S(1)}, u32[]{:S(2)}, u32[]{:S(2)}) collective-permute-start(f32[16,440]{1,0:T(8,128)S(1)} %get-tuple-element.92), channel_id=1, source_target_pairs={{0,112},{1,113},{2,114},{3,115},{4,116},{5,117},{6,118},{7,119},{8... | collective-permute-start | bytes 84488 | tf_op jit(solution)/shard_map/ppermute | solution.py:338
  66.7 17.5 %collective-permute-start.16 = (f32[440,256]{1,0:T(8,128)S(1)}, f32[440,256]{1,0:T(8,128)S(1)}, u32[]{:S(2)}, u32[]{:S(2)}) collective-permute-start(f32[440,256]{1,0:T(8,128)S(1)} %shard_map.84), channel_id=1, source_target_pairs={{0,320},{1,321},{2,322},{3,323},{4,324},{5,325},{6,326},{7,327},{8... | collective-permute-start | bytes 1351688 | tf_op jit(solution)/shard_map/ppermute | solution.py:342
  70.1 13.4 %collective-permute-start.17 = (f32[16,440]{1,0:T(8,128)S(1)}, f32[16,440]{1,0:T(8,128)S(1)}, u32[]{:S(2)}, u32[]{:S(2)}) collective-permute-start(f32[16,440]{1,0:T(8,128)S(1)} %get-tuple-element.99), channel_id=1, source_target_pairs={{0,321},{1,322},{2,323},{3,324},{4,325},{5,326},{6,327},{7,328},{8... | collective-permute-start | bytes 84488 | tf_op jit(solution)/shard_map/ppermute | solution.py:343
  73.0 10.4 %collective-permute-start.18 = (f32[16,440]{1,0:T(8,128)S(1)}, f32[16,440]{1,0:T(8,128)S(1)}, u32[]{:S(2)}, u32[]{:S(2)}) collective-permute-start(f32[16,440]{1,0:T(8,128)S(1)} %get-tuple-element.100), channel_id=1, source_target_pairs={{0,383},{1,320},{2,321},{3,322},{4,323},{5,324},{6,325},{7,326},{8... | collective-permute-start | bytes 84488 | tf_op jit(solution)/shard_map/ppermute | solution.py:344

commit v8 on v6

--- a/solution.py
+++ b/solution.py
@@ -47,8 +47,9 @@
 WEST = sorted((b, a) for a, b in EAST)
 SOUTH = pairs(lambda x, yh, l, z, core: (x + core, yh, l, z, 1 - core))
 NORTH = sorted((b, a) for a, b in SOUTH)
-ROUTES = (EAST, SOUTH, WEST, NORTH)
-ORDER = (0, 2, 1, 3)
+ROUTES = (SOUTH, EAST, WEST, NORTH)
+ORDER = (2, 0, 1, 3)
+PLACE = (1, 2, 0, 3)
 HOME = dict(BACK)
 
 
@@ -146,7 +147,7 @@
 
 
 def joined(arrived):
-    return jnp.concatenate([arrived[d][...] for d in ORDER], axis=0)
+    return jnp.concatenate([arrived[d][...] for d in PLACE], axis=0)
 
 
 def spread():
@@ -340,7 +341,7 @@
         *rims, came = call(rim_kernel, rim_shapes + [border], (b, gsel, ksel, *came))
         y, b = call(stay_kernel, [state, border], (y, adj, sel, rows, came))
         came = exchange(rims)
-    east, south, west, north, came = call(
+    south, east, west, north, came = call(
         rim_kernel, rim_shapes + [border], (b, gsel, ksel, *came)
     )
     (y,) = call(last_stay_kernel, [state], (y, adj, rows, mix_high, mix_low, came))

time: 86.5 us -> 86.4 us (level)
  no operation moved by 1% of the time
where the time goes in v8:
time: 86.4 us; the launch traced here: 85.1 us
  starting transfers between devices  67.2 us (78%)
  Pallas kernels  10.6 us (12%)
  waiting for transfers between devices  5.92 us (7%)
  between operations  0.99 us (1%)
    ppermute x12, starting transfers between devices, exchange(): return [lax.ppermute(rim, AXES, route) for rim, route in zip(rims, ROUTES)]  34 us
    pallas_call x14, Pallas kernels, call(): pl.pallas_call(kernel, out_shape=[jax.ShapeDtypeStruct(s, t) for s, t in...  10.6 us
    ppermute x1, starting transfers between devices, local(): load = lax.ppermute(load, AXES, GO)  7.27 us
    ppermute x1, starting transfers between devices, local(): west = lax.ppermute(west, AXES, homeward(WEST))  6.82 us
    ppermute x1, starting transfers between devices, local(): fields = lax.ppermute(fields, AXES, GO)  5.64 us
    all_to_all x1, starting transfers between devices, local(): slots = lax.all_to_all(slots, ('yh', 'member'), 0, 0)  5.46 us
    ppermute x1, starting transfers between devices, local(): y = lax.ppermute(y, AXES, BACK)  3.4 us
    ppermute x1, starting transfers between devices, local(): east = lax.ppermute(east, AXES, homeward(EAST))  2.97 us
  transfers between devices with their start and end apart: 20, of which 6 were waited for; matrix products, arithmetic and copies ran while one was open for 0% of the time, Pallas kernels for 7%

profile of v8, /device:TPU:1, one launch (start us, length us, event | category | flops | bytes accessed | tf_op | source)
XLA Modules:
  0.0 85.1 jit_solution(14515814375667879304)
XLA Ops:
  0.0 2.1 %shard_map.73 = (f32[16,16,128]{2,1,0:T(8,128)}, f32[72,440]{1,0:T(8,128)}) custom-call(f32[32,55]{1,0:T(8,128)} %bitcast.13, f32[440,256]{1,0:T(8,128)} %bitcast.11, f32[1,256]{1,0:T(1,128)} %bitcast.14, s32[6,256]{1,0:T(8,128)} %named.1, s32[4,16]{1,0:T(4,128)} %sends_in.1), custom_call_target="tpu_custom_call" | custom-call | flops 100000000 | bytes 1000000 | tf_op jit(solution)/shard_map/pallas_call | solution.py:265
  2.1 7.3 %collective-permute-start = (f32[72,440]{1,0:T(8,128)}, f32[72,440]{1,0:T(8,128)S(1)}, u32[]{:S(2)}, u32[]{:S(2)}) collective-permute-start(f32[72,440]{1,0:T(8,128)} %get-tuple-element.54), channel_id=1, source_target_pairs={{0,256},{1,257},{2,258},{3,259},{4,260},{5,261},{6,262},{7,263},{8... | collective-permute-start | bytes 380168 | tf_op jit(solution)/shard_map/ppermute | solution.py:307
  9.4 5.5 %all-to-all-start = ((f32[16,16,128]{2,1,0:T(8,128)}), f32[16,16,128]{2,1,0:T(8,128)S(1)}, u32[]{:S(2)}, u32[]{:S(2)}) async-start(f32[16,16,128]{2,1,0:T(8,128)} %get-tuple-element.53), calls=%async_computation | async-start | bytes 262144 | tf_op jit(solution)/shard_map/all_to_all | solution.py:310
  14.8 0.0 copy-start.2
  14.8 0.0 copy-start
  14.8 0.0 copy-start.1
  14.8 0.0 collective-permute-done.load
  14.9 0.5 shard_map.74
  15.4 0.4 copy-done.2
  15.8 5.6 %collective-permute-start.1 = (f32[440,256]{1,0:T(8,128)S(1)}, f32[440,256]{1,0:T(8,128)S(1)}, u32[]{:S(2)}, u32[]{:S(2)}) collective-permute-start(f32[440,256]{1,0:T(8,128)S(1)} %bitcast.12), channel_id=1, source_target_pairs={{0,256},{1,257},{2,258},{3,259},{4,260},{5,261},{6,262},{7,263},{8... | collective-permute-start | bytes 1351688 | tf_op jit(solution)/shard_map/ppermute | solution.py:309
  21.5 0.0 copy-done
  21.5 0.0 copy-done.1
  21.5 1.3 %shard_map.75 = (bf16[440,440]{1,0:T(8,128)(2,1)S(1)}, bf16[440,440]{1,0:T(8,128)(2,1)S(1)}, bf16[440,440]{1,0:T(8,128)(2,1)S(1)}, bf16[440,440]{1,0:T(8,128)(2,1)S(1)}, bf16[32,256]{1,0:T(8,128)(2,1)S(1)}) custom-call(f32[55,55]{1,0:T(8,128)S(1)} %copy-done.1, s32[6,256]{1,0:T(8,128)S(1)} %copy-done), custom_call_target="tpu_custom_call" | custom-call | flops 100000000 | bytes 1000000 | tf_op jit(solution)/shard_map/pallas_call | solution.py:265
  22.8 1.2 %all-to-all-done.slots = f32[16,16,128]{2,1,0:T(8,128)S(1)} async-done(((f32[16,16,128]{2,1,0:T(8,128)}), f32[16,16,128]{2,1,0:T(8,128)S(1)}, u32[]{:S(2)}, u32[]{:S(2)}) %all-to-all-start) | async-done | bytes 131104 | tf_op jit(solution)/shard_map/all_to_all | solution.py:310
  24.0 0.5 shard_map.77
  24.5 0.0 collective-permute-start.2
  24.5 3.2 %collective-permute-start.3 = (f32[16,440]{1,0:T(8,128)S(1)}, f32[16,440]{1,0:T(8,128)S(1)}, u32[]{:S(2)}, u32[]{:S(2)}) collective-permute-start(f32[16,440]{1,0:T(8,128)S(1)} %get-tuple-element.69), channel_id=1, source_target_pairs={{0,1},{1,2},{2,3},{3,4},{4,5},{5,6},{6,7},{7,64},{8,9},{9,10},{10,... | collective-permute-start | bytes 84488 | tf_op jit(solution)/shard_map/ppermute | solution.py:277
  27.8 8.2 %collective-permute-start.4 = (f32[16,440]{1,0:T(8,128)S(1)}, f32[16,440]{1,0:T(8,128)S(1)}, u32[]{:S(2)}, u32[]{:S(2)}) collective-permute-start(f32[16,440]{1,0:T(8,128)S(1)} %get-tuple-element.70), channel_id=1, source_target_pairs={{0,119},{1,0},{2,1},{3,2},{4,3},{5,4},{6,5},{7,6},{8,127},{9,8},{1... | collective-permute-start | bytes 84488 | tf_op jit(solution)/shard_map/ppermute | solution.py:277
  36.0 2.2 %collective-permute-start.5 = (f32[16,440]{1,0:T(8,128)S(1)}, f32[16,440]{1,0:T(8,128)S(1)}, u32[]{:S(2)}, u32[]{:S(2)}) collective-permute-start(f32[16,440]{1,0:T(8,128)S(1)} %get-tuple-element.71), channel_id=1, source_target_pairs={{0,112},{1,113},{2,114},{3,115},{4,116},{5,117},{6,118},{7,119},{8... | collective-permute-start | bytes 84488 | tf_op jit(solution)/shard_map/ppermute | solution.py:277
  38.2 0.0 collective-permute-done.1.fields
  38.2 0.7 shard_map.76
  39.0 0.0 collective-permute-done.2.i0
  39.0 0.0 collective-permute-done.3.i1
  39.0 0.0 collective-permute-done.4.i2
  39.0 0.4 collective-permute-done.5.i3
  39.4 0.2 shard_map.78
  39.6 0.0 collective-permute-start.6
  39.6 1.9 %collective-permute-start.7 = (f32[16,440]{1,0:T(8,128)S(1)}, f32[16,440]{1,0:T(8,128)S(1)}, u32[]{:S(2)}, u32[]{:S(2)}) collective-permute-start(f32[16,440]{1,0:T(8,128)S(1)} %get-tuple-element.76), channel_id=1, source_target_pairs={{0,1},{1,2},{2,3},{3,4},{4,5},{5,6},{6,7},{7,64},{8,9},{9,10},{10,... | collective-permute-start | bytes 84488 | tf_op jit(solution)/shard_map/ppermute | solution.py:277
  41.6 4.9 %collective-permute-start.8 = (f32[16,440]{1,0:T(8,128)S(1)}, f32[16,440]{1,0:T(8,128)S(1)}, u32[]{:S(2)}, u32[]{:S(2)}) collective-permute-start(f32[16,440]{1,0:T(8,128)S(1)} %get-tuple-element.77), channel_id=1, source_target_pairs={{0,119},{1,0},{2,1},{3,2},{4,3},{5,4},{6,5},{7,6},{8,127},{9,8},{1... | collective-permute-start | bytes 84488 | tf_op jit(solution)/shard_map/ppermute | solution.py:277
  46.4 3.2 %collective-permute-start.9 = (f32[16,440]{1,0:T(8,128)S(1)}, f32[16,440]{1,0:T(8,128)S(1)}, u32[]{:S(2)}, u32[]{:S(2)}) collective-permute-start(f32[16,440]{1,0:T(8,128)S(1)} %get-tuple-element.78), channel_id=1, source_target_pairs={{0,112},{1,113},{2,114},{3,115},{4,116},{5,117},{6,118},{7,119},{8... | collective-permute-start | bytes 84488 | tf_op jit(solution)/shard_map/ppermute | solution.py:277
  49.6 0.8 shard_map.79
  50.4 0.0 collective-permute-done.6.i0
  50.5 0.0 collective-permute-done.7.i1
  50.5 0.0 collective-permute-done.8.i2
  50.5 0.1 collective-permute-done.9.i3
  50.5 0.2 shard_map.80
  50.7 0.0 collective-permute-start.10
  50.8 1.9 %collective-permute-start.11 = (f32[16,440]{1,0:T(8,128)S(1)}, f32[16,440]{1,0:T(8,128)S(1)}, u32[]{:S(2)}, u32[]{:S(2)}) collective-permute-start(f32[16,440]{1,0:T(8,128)S(1)} %get-tuple-element.85), channel_id=1, source_target_pairs={{0,1},{1,2},{2,3},{3,4},{4,5},{5,6},{6,7},{7,64},{8,9},{9,10},{10,... | collective-permute-start | bytes 84488 | tf_op jit(solution)/shard_map/ppermute | solution.py:277
  52.7 4.9 %collective-permute-start.12 = (f32[16,440]{1,0:T(8,128)S(1)}, f32[16,440]{1,0:T(8,128)S(1)}, u32[]{:S(2)}, u32[]{:S(2)}) collective-permute-start(f32[16,440]{1,0:T(8,128)S(1)} %get-tuple-element.86), channel_id=1, source_target_pairs={{0,119},{1,0},{2,1},{3,2},{4,3},{5,4},{6,5},{7,6},{8,127},{9,8},{1... | collective-permute-start | bytes 84488 | tf_op jit(solution)/shard_map/ppermute | solution.py:277
  57.5 3.6 %collective-permute-start.13 = (f32[16,440]{1,0:T(8,128)S(1)}, f32[16,440]{1,0:T(8,128)S(1)}, u32[]{:S(2)}, u32[]{:S(2)}) collective-permute-start(f32[16,440]{1,0:T(8,128)S(1)} %get-tuple-element.87), channel_id=1, source_target_pairs={{0,112},{1,113},{2,114},{3,115},{4,116},{5,117},{6,118},{7,119},{8... | collective-permute-start | bytes 84488 | tf_op jit(solution)/shard_map/ppermute | solution.py:277
  61.2 0.8 shard_map.81
  62.0 0.0 collective-permute-done.10.i0
  62.0 0.0 collective-permute-done.11.i1
  62.0 0.0 collective-permute-done.12.i2
  62.0 0.0 collective-permute-done.13.i3
  62.1 0.2 shard_map.82
  62.3 0.0 collective-permute-start.14
  62.3 1.6 %collective-permute-start.15 = (f32[16,440]{1,0:T(8,128)S(1)}, f32[16,440]{1,0:T(8,128)S(1)}, u32[]{:S(2)}, u32[]{:S(2)}) collective-permute-start(f32[16,440]{1,0:T(8,128)S(1)} %get-tuple-element.92), channel_id=1, source_target_pairs={{0,112},{1,113},{2,114},{3,115},{4,116},{5,117},{6,118},{7,119},{8... | collective-permute-start | bytes 84488 | tf_op jit(solution)/shard_map/ppermute | solution.py:349
  63.8 1.1 %shard_map.83.y = f32[440,256]{1,0:T(8,128)S(1)} custom-call(f32[440,256]{1,0:T(8,128)S(1)} %get-tuple-element.80.y, bf16[320,256]{1,0:T(8,128)(2,1)S(1)} %get-tuple-element.57.adj, f32[8,256]{1,0:T(8,128)S(1)} %get-tuple-element.63.rows, bf16[440,440]{1,0:T(8,128)(2,1)S(1)} %get-tuple-element.81.mix_high, bf16[440,440]{1,0:T(8,128)(2,1)S(1)} %get-tuple-element.82.mix_low, ...), custom_call_target="tpu_custom_call" | custom-call | flops 100000000 | bytes 1000000 | tf_op jit(solution)/shard_map/pallas_call | solution.py:265
  65.0 0.3 shard_map.85
  65.3 0.0 collective-permute-done.14.south
  65.3 0.6 collective-permute-done.15.north
  65.9 0.7 shard_map.84
  66.6 3.4 %collective-permute-start.16 = (f32[440,256]{1,0:T(8,128)S(1)}, f32[440,256]{1,0:T(8,128)S(1)}, u32[]{:S(2)}, u32[]{:S(2)}) collective-permute-start(f32[440,256]{1,0:T(8,128)S(1)} %shard_map.84), channel_id=1, source_target_pairs={{0,320},{1,321},{2,322},{3,323},{4,324},{5,325},{6,326},{7,327},{8... | collective-permute-start | bytes 1351688 | tf_op jit(solution)/shard_map/ppermute | solution.py:353
  70.0 3.0 %collective-permute-start.17 = (f32[16,440]{1,0:T(8,128)S(1)}, f32[16,440]{1,0:T(8,128)S(1)}, u32[]{:S(2)}, u32[]{:S(2)}) collective-permute-start(f32[16,440]{1,0:T(8,128)S(1)} %get-tuple-element.99), channel_id=1, source_target_pairs={{0,321},{1,322},{2,323},{3,324},{4,325},{5,326},{6,327},{7,328},{8... | collective-permute-start | bytes 84488 | tf_op jit(solution)/shard_map/ppermute | solution.py:354
  72.9 6.8 %collective-permute-start.18 = (f32[16,440]{1,0:T(8,128)S(1)}, f32[16,440]{1,0:T(8,128)S(1)}, u32[]{:S(2)}, u32[]{:S(2)}) collective-permute-start(f32[16,440]{1,0:T(8,128)S(1)} %get-tuple-element.100), channel_id=1, source_target_pairs={{0,383},{1,320},{2,321},{3,322},{4,323},{5,324},{6,325},{7,326},{8... | collective-permute-start | bytes 84488 | tf_op jit(solution)/shard_map/ppermute | solution.py:355
  80.4 2.9 %collective-permute-done.17.east = f32[16,440]{1,0:T(8,128)S(1)} collective-permute-done((f32[16,440]{1,0:T(8,128)S(1)}, f32[16,440]{1,0:T(8,128)S(1)}, u32[]{:S(2)}, u32[]{:S(2)}) %collective-permute-start.17) | collective-permute-done | bytes 28192 | tf_op jit(solution)/shard_map/ppermute | solution.py:354
  83.3 0.0 collective-permute-done.18.west
  83.3 0.7 collective-permute-done.16.y
  84.0 1.0 %shard_map.86 = f32[440,256]{1,0:T(8,128)} custom-call(s32[1]{0:T(128)S(6)} %copy.8.count, f32[440,256]{1,0:T(8,128)S(1)} %collective-permute-done.16.y, bf16[32,256]{1,0:T(8,128)(2,1)S(1)} %get-tuple-element.98.ghosts, f32[16,440]{1,0:T(8,128)S(1)} %collective-permute-done.17.east, f32[16,440]{1,0:T(8,128)S(1)} %collective-permute-done.18.west), custom_call_target="tpu_custom_call" | custom-call | flops 100000000 | bytes 1000000 | tf_op jit(solution)/shard_map/pallas_call | solution.py:265
Async XLA Ops:
  2.1 12.8 %collective-permute-start = (f32[72,440]{1,0:T(8,128)}, f32[72,440]{1,0:T(8,128)S(1)}, u32[]{:S(2)}, u32[]{:S(2)}) collective-permute-start(f32[72,440]{1,0:T(8,128)} %get-tuple-element.54), channel_id=1, source_target_pairs={{0,256},{1,257},{2,258},{3,259},{4,260},{5,261},{6,262},{7,263},{8... | collective-permute-start | bytes 380168 | tf_op jit(solution)/shard_map/ppermute | solution.py:307
  9.4 14.6 %all-to-all-start = ((f32[16,16,128]{2,1,0:T(8,128)}), f32[16,16,128]{2,1,0:T(8,128)S(1)}, u32[]{:S(2)}, u32[]{:S(2)}) async-start(f32[16,16,128]{2,1,0:T(8,128)} %get-tuple-element.53), calls=%async_computation | async-start | bytes 262144 | tf_op jit(solution)/shard_map/all_to_all | solution.py:310
  14.8 1.0 %copy-start.2 = (f32[8,55,256]{2,0,1:T(8,128)S(1)}, f32[8,55,256]{2,0,1:T(8,128)}, u32[]{:S(2)}) copy-start(f32[8,55,256]{2,0,1:T(8,128)} %param.7) | copy-start | bytes 1351684
  14.8 6.7 %copy-start = (s32[6,256]{1,0:T(8,128)S(1)}, s32[6,256]{1,0:T(8,128)}, u32[]{:S(2)}) copy-start(s32[6,256]{1,0:T(8,128)} %named.1) | copy-start | bytes 18436
  14.8 6.7 %copy-start.1 = (f32[55,55]{1,0:T(8,128)S(1)}, f32[55,55]{1,0:T(8,128)}, u32[]{:S(2)}) copy-start(f32[55,55]{1,0:T(8,128)} %vloc) | copy-start | bytes 36304
  15.8 22.4 %collective-permute-start.1 = (f32[440,256]{1,0:T(8,128)S(1)}, f32[440,256]{1,0:T(8,128)S(1)}, u32[]{:S(2)}, u32[]{:S(2)}) collective-permute-start(f32[440,256]{1,0:T(8,128)S(1)} %bitcast.12), channel_id=1, source_target_pairs={{0,256},{1,257},{2,258},{3,259},{4,260},{5,261},{6,262},{7,263},{8... | collective-permute-start | bytes 1351688 | tf_op jit(solution)/shard_map/ppermute | solution.py:309
  24.5 14.5 %collective-permute-start.2 = (f32[16,440]{1,0:T(8,128)S(1)}, f32[16,440]{1,0:T(8,128)S(1)}, u32[]{:S(2)}, u32[]{:S(2)}) collective-permute-start(f32[16,440]{1,0:T(8,128)S(1)} %get-tuple-element.68), channel_id=1, source_target_pairs={{0,64},{1,65},{2,66},{3,67},{4,68},{5,69},{6,70},{7,71},{8,72},{9,... | collective-permute-start | bytes 84488 | tf_op jit(solution)/shard_map/ppermute | solution.py:277
  24.5 14.5 %collective-permute-start.3 = (f32[16,440]{1,0:T(8,128)S(1)}, f32[16,440]{1,0:T(8,128)S(1)}, u32[]{:S(2)}, u32[]{:S(2)}) collective-permute-start(f32[16,440]{1,0:T(8,128)S(1)} %get-tuple-element.69), channel_id=1, source_target_pairs={{0,1},{1,2},{2,3},{3,4},{4,5},{5,6},{6,7},{7,64},{8,9},{9,10},{10,... | collective-permute-start | bytes 84488 | tf_op jit(solution)/shard_map/ppermute | solution.py:277
  27.8 11.2 %collective-permute-start.4 = (f32[16,440]{1,0:T(8,128)S(1)}, f32[16,440]{1,0:T(8,128)S(1)}, u32[]{:S(2)}, u32[]{:S(2)}) collective-permute-start(f32[16,440]{1,0:T(8,128)S(1)} %get-tuple-element.70), channel_id=1, source_target_pairs={{0,119},{1,0},{2,1},{3,2},{4,3},{5,4},{6,5},{7,6},{8,127},{9,8},{1... | collective-permute-start | bytes 84488 | tf_op jit(solution)/shard_map/ppermute | solution.py:277
  36.0 3.4 %collective-permute-start.5 = (f32[16,440]{1,0:T(8,128)S(1)}, f32[16,440]{1,0:T(8,128)S(1)}, u32[]{:S(2)}, u32[]{:S(2)}) collective-permute-start(f32[16,440]{1,0:T(8,128)S(1)} %get-tuple-element.71), channel_id=1, source_target_pairs={{0,112},{1,113},{2,114},{3,115},{4,116},{5,117},{6,118},{7,119},{8... | collective-permute-start | bytes 84488 | tf_op jit(solution)/shard_map/ppermute | solution.py:277
  39.6 10.8 %collective-permute-start.6 = (f32[16,440]{1,0:T(8,128)S(1)}, f32[16,440]{1,0:T(8,128)S(1)}, u32[]{:S(2)}, u32[]{:S(2)}) collective-permute-start(f32[16,440]{1,0:T(8,128)S(1)} %get-tuple-element.75), channel_id=1, source_target_pairs={{0,64},{1,65},{2,66},{3,67},{4,68},{5,69},{6,70},{7,71},{8,72},{9,... | collective-permute-start | bytes 84488 | tf_op jit(solution)/shard_map/ppermute | solution.py:277
  39.6 10.8 %collective-permute-start.7 = (f32[16,440]{1,0:T(8,128)S(1)}, f32[16,440]{1,0:T(8,128)S(1)}, u32[]{:S(2)}, u32[]{:S(2)}) collective-permute-start(f32[16,440]{1,0:T(8,128)S(1)} %get-tuple-element.76), channel_id=1, source_target_pairs={{0,1},{1,2},{2,3},{3,4},{4,5},{5,6},{6,7},{7,64},{8,9},{9,10},{10,... | collective-permute-start | bytes 84488 | tf_op jit(solution)/shard_map/ppermute | solution.py:277
  41.6 8.9 %collective-permute-start.8 = (f32[16,440]{1,0:T(8,128)S(1)}, f32[16,440]{1,0:T(8,128)S(1)}, u32[]{:S(2)}, u32[]{:S(2)}) collective-permute-start(f32[16,440]{1,0:T(8,128)S(1)} %get-tuple-element.77), channel_id=1, source_target_pairs={{0,119},{1,0},{2,1},{3,2},{4,3},{5,4},{6,5},{7,6},{8,127},{9,8},{1... | collective-permute-start | bytes 84488 | tf_op jit(solution)/shard_map/ppermute | solution.py:277
  46.4 4.1 %collective-permute-start.9 = (f32[16,440]{1,0:T(8,128)S(1)}, f32[16,440]{1,0:T(8,128)S(1)}, u32[]{:S(2)}, u32[]{:S(2)}) collective-permute-start(f32[16,440]{1,0:T(8,128)S(1)} %get-tuple-element.78), channel_id=1, source_target_pairs={{0,112},{1,113},{2,114},{3,115},{4,116},{5,117},{6,118},{7,119},{8... | collective-permute-start | bytes 84488 | tf_op jit(solution)/shard_map/ppermute | solution.py:277
  50.7 11.3 %collective-permute-start.10 = (f32[16,440]{1,0:T(8,128)S(1)}, f32[16,440]{1,0:T(8,128)S(1)}, u32[]{:S(2)}, u32[]{:S(2)}) collective-permute-start(f32[16,440]{1,0:T(8,128)S(1)} %get-tuple-element.84), channel_id=1, source_target_pairs={{0,64},{1,65},{2,66},{3,67},{4,68},{5,69},{6,70},{7,71},{8,72},{9,... | collective-permute-start | bytes 84488 | tf_op jit(solution)/shard_map/ppermute | solution.py:277
  50.8 11.3 %collective-permute-start.11 = (f32[16,440]{1,0:T(8,128)S(1)}, f32[16,440]{1,0:T(8,128)S(1)}, u32[]{:S(2)}, u32[]{:S(2)}) collective-permute-start(f32[16,440]{1,0:T(8,128)S(1)} %get-tuple-element.85), channel_id=1, source_target_pairs={{0,1},{1,2},{2,3},{3,4},{4,5},{5,6},{6,7},{7,64},{8,9},{9,10},{10,... | collective-permute-start | bytes 84488 | tf_op jit(solution)/shard_map/ppermute | solution.py:277
  52.7 9.4 %collective-permute-start.12 = (f32[16,440]{1,0:T(8,128)S(1)}, f32[16,440]{1,0:T(8,128)S(1)}, u32[]{:S(2)}, u32[]{:S(2)}) collective-permute-start(f32[16,440]{1,0:T(8,128)S(1)} %get-tuple-element.86), channel_id=1, source_target_pairs={{0,119},{1,0},{2,1},{3,2},{4,3},{5,4},{6,5},{7,6},{8,127},{9,8},{1... | collective-permute-start | bytes 84488 | tf_op jit(solution)/shard_map/ppermute | solution.py:277
  57.5 4.5 %collective-permute-start.13 = (f32[16,440]{1,0:T(8,128)S(1)}, f32[16,440]{1,0:T(8,128)S(1)}, u32[]{:S(2)}, u32[]{:S(2)}) collective-permute-start(f32[16,440]{1,0:T(8,128)S(1)} %get-tuple-element.87), channel_id=1, source_target_pairs={{0,112},{1,113},{2,114},{3,115},{4,116},{5,117},{6,118},{7,119},{8... | collective-permute-start | bytes 84488 | tf_op jit(solution)/shard_map/ppermute | solution.py:277
  62.3 3.0 %collective-permute-start.14 = (f32[16,440]{1,0:T(8,128)S(1)}, f32[16,440]{1,0:T(8,128)S(1)}, u32[]{:S(2)}, u32[]{:S(2)}) collective-permute-start(f32[16,440]{1,0:T(8,128)S(1)} %get-tuple-element.91), channel_id=1, source_target_pairs={{0,64},{1,65},{2,66},{3,67},{4,68},{5,69},{6,70},{7,71},{8,72},{9,... | collective-permute-start | bytes 84488 | tf_op jit(solution)/shard_map/ppermute | solution.py:348
  62.3 3.6 %collective-permute-start.15 = (f32[16,440]{1,0:T(8,128)S(1)}, f32[16,440]{1,0:T(8,128)S(1)}, u32[]{:S(2)}, u32[]{:S(2)}) collective-permute-start(f32[16,440]{1,0:T(8,128)S(1)} %get-tuple-element.92), channel_id=1, source_target_pairs={{0,112},{1,113},{2,114},{3,115},{4,116},{5,117},{6,118},{7,119},{8... | collective-permute-start | bytes 84488 | tf_op jit(solution)/shard_map/ppermute | solution.py:349
  66.6 17.5 %collective-permute-start.16 = (f32[440,256]{1,0:T(8,128)S(1)}, f32[440,256]{1,0:T(8,128)S(1)}, u32[]{:S(2)}, u32[]{:S(2)}) collective-permute-start(f32[440,256]{1,0:T(8,128)S(1)} %shard_map.84), channel_id=1, source_target_pairs={{0,320},{1,321},{2,322},{3,323},{4,324},{5,325},{6,326},{7,327},{8... | collective-permute-start | bytes 1351688 | tf_op jit(solution)/shard_map/ppermute | solution.py:353
  70.0 13.4 %collective-permute-start.17 = (f32[16,440]{1,0:T(8,128)S(1)}, f32[16,440]{1,0:T(8,128)S(1)}, u32[]{:S(2)}, u32[]{:S(2)}) collective-permute-start(f32[16,440]{1,0:T(8,128)S(1)} %get-tuple-element.99), channel_id=1, source_target_pairs={{0,321},{1,322},{2,323},{3,324},{4,325},{5,326},{6,327},{7,328},{8... | collective-permute-start | bytes 84488 | tf_op jit(solution)/shard_map/ppermute | solution.py:354
  72.9 10.4 %collective-permute-start.18 = (f32[16,440]{1,0:T(8,128)S(1)}, f32[16,440]{1,0:T(8,128)S(1)}, u32[]{:S(2)}, u32[]{:S(2)}) collective-permute-start(f32[16,440]{1,0:T(8,128)S(1)} %get-tuple-element.100), channel_id=1, source_target_pairs={{0,383},{1,320},{2,321},{3,322},{4,323},{5,324},{6,325},{7,326},{8... | collective-permute-start | bytes 84488 | tf_op jit(solution)/shard_map/ppermute | solution.py:355
